TPU v7x, 32 devices: a whole 2x2x4 slice. The times are simulated.
32 devices in a mesh: section: 2 (over x), seq: 4 (over z), chan: 4 (over y, core).
Axes of the slice: x: 2, y: 2, z: 4, core: 2. Of those that a mesh axis runs over, the one named last changes fastest.
Arguments:
- saved_input: bfloat16 [2, 2, 512, 1024], P('section', None, 'seq', 'chan'), may hold values from -6 to 6
- pre_gate: bfloat16 [2, 2, 512, 1024], P('section', None, 'seq', 'chan'), may hold values from -6 to 6
- post_gate: bfloat16 [2, 2, 512, 1024], P('section', None, 'seq', 'chan'), may hold values from -6 to 6
- grad_held: bfloat16 [2, 512, 1024], P('section', 'seq', 'chan'), may hold values from -6 to 6
- loss_grad: bfloat16 [512, 1024], P('seq', 'chan'), may hold values from -6 to 6
- filters: float32 [2, 512, 256], P('section', 'seq'), may hold values from -1 to 1
- skip_gain: float32 [2, 256], P('section'), may hold values from 0.5 to 1.5
Outputs:
- grad_out: bfloat16 [2, 512, 1024], P('section', 'seq', 'chan')
- filter_grad: float32 [2, 512, 256], P('section', 'seq', 'chan')
All inputs are finite; a program needn't handle non-finite values.
Results may differ from a plain program's by a relative error of at most 0.017.
Values may be sent and summed in bfloat16 or wider, within the bound.
No kernel may reach another device: no remote copies, remote signals or barrier semaphores. Data moves between devices by JAX's collectives and lax.ppermute only.
A program may use at most 64 MiB of HBM per device.

v0:
```python
import math

import jax
import jax.numpy as jnp
from jax import lax
from jax.sharding import PartitionSpec as P


def partner_2(value, axis, distance):
    mask = 2**distance
    pairs = [(source, source ^ mask) for source in range(lax.axis_size(axis))]
    return lax.ppermute(value, axis, pairs)


def shifted(block, axis, distance):
    devices = range(lax.axis_size(axis))
    route = [(i - distance, i) for i in devices if i - distance in devices]
    return lax.ppermute(block, axis, route)


def angle_table(length, signum):
    rows_index = jnp.arange(length, dtype=jnp.int32)
    product = rows_index[:, None] * rows_index[None, :] % length
    angles = 2.0 * math.pi / length * product.astype(jnp.float32)
    table_real = jnp.cos(angles)
    table_imag = signum * jnp.sin(angles)
    return jnp.stack([jnp.stack([table_real, -table_imag]), jnp.stack([table_imag, table_real])])


def complex_scale(values, factor_real, factor_imag):
    real_part = values[0] * factor_real - values[1] * factor_imag
    imag_part = values[0] * factor_imag + values[1] * factor_real
    return jnp.stack([real_part, imag_part])


def apply_table(block_table, values, pattern):
    return jnp.einsum(pattern, block_table, values, precision=lax.Precision.HIGHEST)


def local_transform(values, signum):
    pair_count = values.shape[1]
    length_dev = values.shape[2]
    width_dev = values.shape[3]
    outer_len = 1 << (length_dev.bit_length() - 1) // 2
    inner_len = length_dev // outer_len
    shaped = values.reshape(2, pair_count, outer_len, inner_len, width_dev)
    shaped = apply_table(angle_table(outer_len, signum), shaped, "ozka,zpabh->opkbh")
    outer_index = jnp.arange(outer_len, dtype=jnp.int32)[:, None]
    inner_index = jnp.arange(inner_len, dtype=jnp.int32)[None, :]
    angles = (
        2.0 * math.pi / length_dev * (outer_index * inner_index % length_dev).astype(jnp.float32)
    )
    shaped = complex_scale(
        shaped, jnp.cos(angles)[:, :, None], signum * jnp.sin(angles)[:, :, None]
    )
    shaped = apply_table(angle_table(inner_len, signum), shaped, "ozKb,zpabh->opKah")
    return shaped.reshape(2, pair_count, length_dev, width_dev)


def bit_reverse(seq_index, bit_count):
    result = jnp.zeros((), jnp.int32)
    for offset in range(bit_count):
        result = result + (seq_index >> offset & 1) * (1 << bit_count - 1 - offset)
    return result


def rounds_forward(spectrum, seq_index, bit_count):
    for stride_bit in reversed(range(bit_count)):
        half_span = 1 << stride_bit
        partner = partner_2(spectrum, "seq", stride_bit)
        upper_half = seq_index >> stride_bit & 1 == 1
        within = (seq_index & half_span - 1).astype(jnp.float32)
        angles = jnp.where(upper_half, math.pi / half_span * within, 0.0)
        sign_self = jnp.where(upper_half, -1.0, 1.0)
        spectrum = complex_scale(partner + sign_self * spectrum, jnp.cos(angles), -jnp.sin(angles))
    return spectrum


def rounds_inverse(spectrum, seq_index, bit_count):
    for stride_bit in range(bit_count):
        half_span = 1 << stride_bit
        partner = partner_2(spectrum, "seq", stride_bit)
        upper_half = seq_index >> stride_bit & 1 == 1
        within = (seq_index & half_span - 1).astype(jnp.float32)
        angles = math.pi / half_span * within
        first_term = jnp.where(upper_half, partner, spectrum)
        second_term = jnp.where(upper_half, -spectrum, partner)
        spectrum = first_term + complex_scale(second_term, jnp.cos(angles), jnp.sin(angles))
    return spectrum


def body(saved_input, pre_gate, post_gate, grad_held, loss_grad, filters, skip_gain):
    seq_count = lax.axis_size("seq")
    seq_index = lax.axis_index("seq")
    bit_count = seq_count.bit_length() - 1
    length_dev = saved_input.shape[2]
    tick_count = saved_input.shape[1]
    seq_length = length_dev * seq_count
    local_index = jnp.arange(length_dev, dtype=jnp.int32)
    positions = seq_index * length_dev + local_index
    twist_angle = math.pi / seq_length * positions.astype(jnp.float32)
    twist_cos = jnp.cos(twist_angle)[:, None]
    twist_sin = jnp.sin(twist_angle)[:, None]
    freq_index = bit_reverse(seq_index, bit_count)
    twiddle_angle = (
        2.0 * math.pi / seq_length * (local_index * freq_index % seq_length).astype(jnp.float32)
    )
    twiddle_cos = jnp.cos(twiddle_angle)[:, None]
    twiddle_sin = jnp.sin(twiddle_angle)[:, None]

    def forward(values):
        stacked = jnp.stack(
            [
                jnp.stack([values, values * twist_cos]),
                jnp.stack([jnp.zeros_like(values), -values * twist_sin]),
            ]
        )
        stacked = rounds_forward(stacked, seq_index, bit_count)
        stacked = complex_scale(stacked, twiddle_cos, -twiddle_sin)
        return local_transform(stacked, -1.0)

    def inverse(spectrum):
        spectrum = local_transform(spectrum, 1.0)
        spectrum = complex_scale(spectrum, twiddle_cos, twiddle_sin)
        spectrum = rounds_inverse(spectrum, seq_index, bit_count)
        real_values = spectrum[0, 0] + spectrum[0, 1] * twist_cos - spectrum[1, 1] * twist_sin
        return real_values / (2.0 * seq_length)

    filter_spec = forward(filters[0])
    carried = grad_held[0].astype(jnp.float32)
    spectral_sum = jnp.zeros((2, 2, length_dev, filters.shape[2]), jnp.float32)
    gradient = grad_held[0]
    for tick_step in range(tick_count):
        gate_in = pre_gate[0, tick_step].astype(jnp.float32)
        mixed_input = gate_in * saved_input[0, tick_step].astype(jnp.float32)
        gated_grad = post_gate[0, tick_step].astype(jnp.float32) * carried
        mixed_spec = forward(mixed_input)
        gated_spec = forward(gated_grad)
        filtered = jnp.stack(
            [
                filter_spec[0] * gated_spec[0] + filter_spec[1] * gated_spec[1],
                filter_spec[0] * gated_spec[1] - filter_spec[1] * gated_spec[0],
            ]
        )
        correlated = inverse(filtered)
        gradient = (carried + gate_in * (correlated + skip_gain[0] * gated_grad)).astype(
            jnp.bfloat16
        )
        spectral_sum = spectral_sum + jnp.stack(
            [
                gated_spec[0] * mixed_spec[0] + gated_spec[1] * mixed_spec[1],
                gated_spec[1] * mixed_spec[0] - gated_spec[0] * mixed_spec[1],
            ]
        )
        if tick_step + 1 < tick_count:
            received = shifted(gradient, "section", -1)
            is_last = lax.axis_index("section") == lax.axis_size("section") - 1
            carried = jnp.where(
                is_last, loss_grad.astype(jnp.float32), received.astype(jnp.float32)
            )
    grad_scale = 1.0 / math.sqrt(seq_length * lax.axis_size("chan") * tick_count)
    reduced = lax.psum_scatter(
        spectral_sum.astype(jnp.bfloat16), "chan", scatter_dimension=3, tiled=True
    ).astype(jnp.float32)
    lag_grad = inverse(reduced)
    return (gradient[None], (lag_grad * grad_scale)[None])


def solution(mesh):
    placed = (
        P("section", None, "seq", "chan"),
        P("section", None, "seq", "chan"),
        P("section", None, "seq", "chan"),
        P("section", "seq", "chan"),
        P("seq", "chan"),
        P("section", "seq", None),
        P("section", None),
    )
    return jax.shard_map(
        body,
        mesh=mesh,
        in_specs=placed,
        out_specs=(P("section", "seq", "chan"), P("section", "seq", "chan")),
        check_vma=False,
    )
```

profile of v0, /device:TPU:0, one launch (start us, length us, event | category | flops | bytes accessed | tf_op | source)
XLA Modules:
  0.0 347.5 jit_solution(18201572479407669542)
XLA Ops:
  10.4 4.0 %collective-permute-start.13 = (f32[2,2,128,256]{3,2,1,0:T(8,128)}, f32[2,2,128,256]{3,2,1,0:T(8,128)}, u32[]{:S(2)}, u32[]{:S(2)}) collective-permute-start(f32[2,2,128,256]{3,2,1,0:T(8,128)} %pad_maximum_fusion.10), channel_id=1, source_target_pairs={{0,8},{4,12},{8,0},{12,4},{1,9},{5,13},{9,1},{13,5},{2,10},{6,14},... | collective-permute-start | bytes 1572872 | tf_op jit(solution)/shard_map/ppermute | solution.py:12
  16.2 2.9 collective-permute-start.11
  21.5 50.9 %collective-permute-done.13 = f32[2,2,128,256]{3,2,1,0:T(8,128)} collective-permute-done((f32[2,2,128,256]{3,2,1,0:T(8,128)}, f32[2,2,128,256]{3,2,1,0:T(8,128)}, u32[]{:S(2)}, u32[]{:S(2)}) %collective-permute-start.13) | collective-permute-done | bytes 524320 | tf_op jit(solution)/shard_map/ppermute | solution.py:12
  73.7 10.0 %collective-permute-done.2 = f32[2,2,128,256]{3,2,1,0:T(8,128)} collective-permute-done((f32[2,2,128,256]{3,2,1,0:T(8,128)}, f32[2,2,128,256]{3,2,1,0:T(8,128)}, u32[]{:S(2)}, u32[]{:S(2)}) %collective-permute-start.2) | collective-permute-done | bytes 524320 | tf_op jit(solution)/shard_map/ppermute | solution.py:12
  85.0 9.9 %collective-permute-done.11 = f32[2,2,128,256]{3,2,1,0:T(8,128)} collective-permute-done((f32[2,2,128,256]{3,2,1,0:T(8,128)}, f32[2,2,128,256]{3,2,1,0:T(8,128)}, u32[]{:S(2)}, u32[]{:S(2)}) %collective-permute-start.11) | collective-permute-done | bytes 524320 | tf_op jit(solution)/shard_map/ppermute | solution.py:12
  96.3 9.0 %collective-permute-done = f32[2,2,128,256]{3,2,1,0:T(8,128)S(1)} collective-permute-done((f32[2,2,128,256]{3,2,1,0:T(8,128)}, f32[2,2,128,256]{3,2,1,0:T(8,128)S(1)}, u32[]{:S(2)}, u32[]{:S(2)}) %collective-permute-start) | collective-permute-done | bytes 524320 | tf_op jit(solution)/shard_map/ppermute | solution.py:12
  106.3 10.2 %collective-permute-done.14 = f32[2,2,128,256]{3,2,1,0:T(8,128)S(1)} collective-permute-done((f32[2,2,128,256]{3,2,1,0:T(8,128)S(1)}, f32[2,2,128,256]{3,2,1,0:T(8,128)S(1)}, u32[]{:S(2)}, u32[]{:S(2)}) %collective-permute-start.14) | collective-permute-done | bytes 524320 | tf_op jit(solution)/shard_map/ppermute | solution.py:12
  116.6 11.2 %collective-permute-done.3 = f32[2,2,128,256]{3,2,1,0:T(8,128)S(1)} collective-permute-done((f32[2,2,128,256]{3,2,1,0:T(8,128)S(1)}, f32[2,2,128,256]{3,2,1,0:T(8,128)S(1)}, u32[]{:S(2)}, u32[]{:S(2)}) %collective-permute-start.3) | collective-permute-done | bytes 524320 | tf_op jit(solution)/shard_map/ppermute | solution.py:12
  127.8 11.2 %collective-permute-done.12 = f32[2,2,128,256]{3,2,1,0:T(8,128)S(1)} collective-permute-done((f32[2,2,128,256]{3,2,1,0:T(8,128)S(1)}, f32[2,2,128,256]{3,2,1,0:T(8,128)S(1)}, u32[]{:S(2)}, u32[]{:S(2)}) %collective-permute-start.12) | collective-permute-done | bytes 524320 | tf_op jit(solution)/shard_map/ppermute | solution.py:12
  139.1 11.1 %collective-permute-done.1 = f32[2,2,128,256]{3,2,1,0:T(8,128)S(1)} collective-permute-done((f32[2,2,128,256]{3,2,1,0:T(8,128)S(1)}, f32[2,2,128,256]{3,2,1,0:T(8,128)S(1)}, u32[]{:S(2)}, u32[]{:S(2)}) %collective-permute-start.1) | collective-permute-done | bytes 524320 | tf_op jit(solution)/shard_map/ppermute | solution.py:12
  162.4 13.8 %collective-permute-done.4 = f32[2,2,128,256]{3,2,1,0:T(8,128)S(1)} collective-permute-done((f32[2,2,128,256]{3,2,1,0:T(8,128)S(1)}, f32[2,2,128,256]{3,2,1,0:T(8,128)S(1)}, u32[]{:S(2)}, u32[]{:S(2)}) %collective-permute-start.4) | collective-permute-done | bytes 524320 | tf_op jit(solution)/shard_map/ppermute | solution.py:12
  177.2 2.4 collective-permute-start.5
  179.7 22.9 %collective-permute-done.5 = f32[2,2,128,256]{3,2,1,0:T(8,128)S(1)} collective-permute-done((f32[2,2,128,256]{3,2,1,0:T(8,128)}, f32[2,2,128,256]{3,2,1,0:T(8,128)S(1)}, u32[]{:S(2)}, u32[]{:S(2)}) %collective-permute-start.5) | collective-permute-done | bytes 524320 | tf_op jit(solution)/shard_map/ppermute | solution.py:12
  203.9 1.3 collective-permute-start.6
  205.2 4.9 %collective-permute-done.6 = bf16[128,256]{1,0:T(8,128)(2,1)S(1)} collective-permute-done((bf16[128,256]{1,0:T(8,128)(2,1)S(1)}, bf16[128,256]{1,0:T(8,128)(2,1)S(1)}, u32[]{:S(2)}, u32[]{:S(2)}) %collective-permute-start.6) | collective-permute-done | bytes 65568 | tf_op jit(solution)/shard_map/ppermute | solution.py:18
  210.8 23.9 %collective-permute-done.7 = f32[2,2,128,256]{3,2,1,0:T(8,128)S(1)} collective-permute-done((f32[2,2,128,256]{3,2,1,0:T(8,128)S(1)}, f32[2,2,128,256]{3,2,1,0:T(8,128)S(1)}, u32[]{:S(2)}, u32[]{:S(2)}) %collective-permute-start.7) | collective-permute-done | bytes 524320 | tf_op jit(solution)/shard_map/ppermute | solution.py:12
  240.4 7.6 %collective-permute-done.8 = f32[2,2,128,256]{3,2,1,0:T(8,128)S(1)} collective-permute-done((f32[2,2,128,256]{3,2,1,0:T(8,128)}, f32[2,2,128,256]{3,2,1,0:T(8,128)S(1)}, u32[]{:S(2)}, u32[]{:S(2)}) %collective-permute-start.8) | collective-permute-done | bytes 524320 | tf_op jit(solution)/shard_map/ppermute | solution.py:12
  256.1 31.8 %all-reduce.8.cloned.1.call-done = bf16[2,2,128,256]{2,1,0,3:T(2,128)(2,1)} async-done(((bf16[2,2,128,256]{2,1,0,3:T(2,128)(2,1)}), bf16[2,2,128,256]{2,1,0,3:T(2,128)(2,1)}) %all-reduce.8.cloned.1.call-update) | async-done | bytes 262160
  290.7 1.5 collective-permute-start.15
  293.2 9.6 %collective-permute-done.15 = f32[2,2,128,64]{3,2,1,0:T(8,128)S(1)} collective-permute-done((f32[2,2,128,64]{3,2,1,0:T(8,128)S(1)}, f32[2,2,128,64]{3,2,1,0:T(8,128)S(1)}, u32[]{:S(2)}, u32[]{:S(2)}) %collective-permute-start.15) | collective-permute-done | bytes 131104 | tf_op jit(solution)/shard_map/ppermute | solution.py:12
  302.9 1.3 collective-permute-start.16
  304.2 9.3 %collective-permute-done.16 = f32[2,2,128,64]{3,2,1,0:T(8,128)S(1)} collective-permute-done((f32[2,2,128,64]{3,2,1,0:T(8,128)S(1)}, f32[2,2,128,64]{3,2,1,0:T(8,128)S(1)}, u32[]{:S(2)}, u32[]{:S(2)}) %collective-permute-start.16) | collective-permute-done | bytes 131104 | tf_op jit(solution)/shard_map/ppermute | solution.py:12
  314.5 2.9 collective-permute-start.10
  318.9 19.9 %collective-permute-done.10 = f32[2,2,128,256]{3,2,1,0:T(8,128)S(1)} collective-permute-done((f32[2,2,128,256]{3,2,1,0:T(8,128)S(1)}, f32[2,2,128,256]{3,2,1,0:T(8,128)S(1)}, u32[]{:S(2)}, u32[]{:S(2)}) %collective-permute-start.10) | collective-permute-done | bytes 524320 | tf_op jit(solution)/shard_map/ppermute | solution.py:12
  (255 shorter events, 47.6 us)
Async XLA Ops:
  7.2 280.8 %all-reduce.8.cloned.1.call-start = ((), (), s32[]{:S(2)}) async-start(), calls=%async_computation | async-start | bytes 524288
  10.4 62.0 %collective-permute-start.13 = (f32[2,2,128,256]{3,2,1,0:T(8,128)}, f32[2,2,128,256]{3,2,1,0:T(8,128)}, u32[]{:S(2)}, u32[]{:S(2)}) collective-permute-start(f32[2,2,128,256]{3,2,1,0:T(8,128)} %pad_maximum_fusion.10), channel_id=1, source_target_pairs={{0,8},{4,12},{8,0},{12,4},{1,9},{5,13},{9,1},{13,5},{2,10},{6,14},... | collective-permute-start | bytes 1572872 | tf_op jit(solution)/shard_map/ppermute | solution.py:12
  15.3 68.4 %collective-permute-start.2 = (f32[2,2,128,256]{3,2,1,0:T(8,128)}, f32[2,2,128,256]{3,2,1,0:T(8,128)}, u32[]{:S(2)}, u32[]{:S(2)}) collective-permute-start(f32[2,2,128,256]{3,2,1,0:T(8,128)} %pad_maximum_fusion.2), channel_id=1, source_target_pairs={{0,8},{4,12},{8,0},{12,4},{1,9},{5,13},{9,1},{13,5},{2,10},{6,14},... | collective-permute-start | bytes 1572872 | tf_op jit(solution)/shard_map/ppermute | solution.py:12
  16.2 78.8 %collective-permute-start.11 = (f32[2,2,128,256]{3,2,1,0:T(8,128)}, f32[2,2,128,256]{3,2,1,0:T(8,128)}, u32[]{:S(2)}, u32[]{:S(2)}) collective-permute-start(f32[2,2,128,256]{3,2,1,0:T(8,128)} %pad_maximum_fusion.8), channel_id=1, source_target_pairs={{0,8},{4,12},{8,0},{12,4},{1,9},{5,13},{9,1},{13,5},{2,10},{6,14},... | collective-permute-start | bytes 1572872 | tf_op jit(solution)/shard_map/ppermute | solution.py:12
  20.0 85.3 %collective-permute-start = (f32[2,2,128,256]{3,2,1,0:T(8,128)}, f32[2,2,128,256]{3,2,1,0:T(8,128)S(1)}, u32[]{:S(2)}, u32[]{:S(2)}) collective-permute-start(f32[2,2,128,256]{3,2,1,0:T(8,128)} %pad_maximum_fusion), channel_id=1, source_target_pairs={{0,8},{4,12},{8,0},{12,4},{1,9},{5,13},{9,1},{13,5},{2,10},{6,14},... | collective-permute-start | bytes 1572872 | tf_op jit(solution)/shard_map/ppermute | solution.py:12
  21.3 140.1 %copy-start.43 = (f32[128]{0:T(128)}, f32[128]{0:T(128)S(1)}, u32[]{:S(2)}) copy-start(f32[128]{0:T(128)S(1)} %fusion.100) | copy-start | bytes 1540
  21.4 137.8 %copy-start.28 = (f32[1,2,8,8]{3,2,1,0:T(8,128)}, f32[1,2,8,8]{3,2,1,0:T(8,128)S(1)}, u32[]{:S(2)}) copy-start(f32[1,2,8,8]{3,2,1,0:T(8,128)S(1)} %get-tuple-element.104) | copy-start | bytes 1540
  21.4 137.8 %copy-start.30 = (f32[1,2,8,8]{3,2,1,0:T(8,128)}, f32[1,2,8,8]{3,2,1,0:T(8,128)S(1)}, u32[]{:S(2)}) copy-start(f32[1,2,8,8]{3,2,1,0:T(8,128)S(1)} %get-tuple-element.105) | copy-start | bytes 1540
  21.5 136.0 %copy-start.2 = (f32[1,2,16,16]{3,2,1,0:T(8,128)}, f32[1,2,16,16]{3,2,1,0:T(8,128)S(1)}, u32[]{:S(2)}) copy-start(f32[1,2,16,16]{3,2,1,0:T(8,128)S(1)} %get-tuple-element.103) | copy-start | bytes 6148
  21.5 138.6 %copy-start.17 = (f32[1,2,16,16]{3,2,1,0:T(8,128)}, f32[1,2,16,16]{3,2,1,0:T(8,128)S(1)}, u32[]{:S(2)}) copy-start(f32[1,2,16,16]{3,2,1,0:T(8,128)S(1)} %get-tuple-element.100) | copy-start | bytes 6148
  21.5 138.6 %copy-start.19 = (f32[1,2,16,16]{3,2,1,0:T(8,128)}, f32[1,2,16,16]{3,2,1,0:T(8,128)S(1)}, u32[]{:S(2)}) copy-start(f32[1,2,16,16]{3,2,1,0:T(8,128)S(1)} %get-tuple-element.101) | copy-start | bytes 6148
  73.6 42.9 %collective-permute-start.14 = (f32[2,2,128,256]{3,2,1,0:T(8,128)S(1)}, f32[2,2,128,256]{3,2,1,0:T(8,128)S(1)}, u32[]{:S(2)}, u32[]{:S(2)}) collective-permute-start(f32[2,2,128,256]{3,2,1,0:T(8,128)S(1)} %pad_maximum_fusion.11), channel_id=1, source_target_pairs={{0,4},{4,0},{8,12},{12,8},{1,5},{5,1},{9,13},{13,9},{2,6},{6,2},{1... | collective-permute-start | bytes 1572872 | tf_op jit(solution)/shard_map/ppermute | solution.py:12
  85.0 42.8 %collective-permute-start.3 = (f32[2,2,128,256]{3,2,1,0:T(8,128)S(1)}, f32[2,2,128,256]{3,2,1,0:T(8,128)S(1)}, u32[]{:S(2)}, u32[]{:S(2)}) collective-permute-start(f32[2,2,128,256]{3,2,1,0:T(8,128)S(1)} %pad_maximum_fusion.3), channel_id=1, source_target_pairs={{0,4},{4,0},{8,12},{12,8},{1,5},{5,1},{9,13},{13,9},{2,6},{6,2},{1... | collective-permute-start | bytes 1572872 | tf_op jit(solution)/shard_map/ppermute | solution.py:12
  96.2 42.8 %collective-permute-start.12 = (f32[2,2,128,256]{3,2,1,0:T(8,128)S(1)}, f32[2,2,128,256]{3,2,1,0:T(8,128)S(1)}, u32[]{:S(2)}, u32[]{:S(2)}) collective-permute-start(f32[2,2,128,256]{3,2,1,0:T(8,128)S(1)} %pad_maximum_fusion.9), channel_id=1, source_target_pairs={{0,4},{4,0},{8,12},{12,8},{1,5},{5,1},{9,13},{13,9},{2,6},{6,2},{1... | collective-permute-start | bytes 1572872 | tf_op jit(solution)/shard_map/ppermute | solution.py:12
  105.5 44.7 %collective-permute-start.1 = (f32[2,2,128,256]{3,2,1,0:T(8,128)S(1)}, f32[2,2,128,256]{3,2,1,0:T(8,128)S(1)}, u32[]{:S(2)}, u32[]{:S(2)}) collective-permute-start(f32[2,2,128,256]{3,2,1,0:T(8,128)S(1)} %pad_maximum_fusion.1), channel_id=1, source_target_pairs={{0,4},{4,0},{8,12},{12,8},{1,5},{5,1},{9,13},{13,9},{2,6},{6,2},{1... | collective-permute-start | bytes 1572872 | tf_op jit(solution)/shard_map/ppermute | solution.py:12
  162.3 13.9 %collective-permute-start.4 = (f32[2,2,128,256]{3,2,1,0:T(8,128)S(1)}, f32[2,2,128,256]{3,2,1,0:T(8,128)S(1)}, u32[]{:S(2)}, u32[]{:S(2)}) collective-permute-start(f32[2,2,128,256]{3,2,1,0:T(8,128)S(1)} %pad_maximum_fusion.4), channel_id=1, source_target_pairs={{0,4},{4,0},{8,12},{12,8},{1,5},{5,1},{9,13},{13,9},{2,6},{6,2},{1... | collective-permute-start | bytes 1572872 | tf_op jit(solution)/shard_map/ppermute | solution.py:12
  177.2 25.4 %collective-permute-start.5 = (f32[2,2,128,256]{3,2,1,0:T(8,128)}, f32[2,2,128,256]{3,2,1,0:T(8,128)S(1)}, u32[]{:S(2)}, u32[]{:S(2)}) collective-permute-start(f32[2,2,128,256]{3,2,1,0:T(8,128)} %maximum_add_fusion), channel_id=1, source_target_pairs={{0,8},{4,12},{8,0},{12,4},{1,9},{5,13},{9,1},{13,5},{2,10},{6,14},... | collective-permute-start | bytes 1572872 | tf_op jit(solution)/shard_map/ppermute | solution.py:12
  203.9 6.2 %collective-permute-start.6 = (bf16[128,256]{1,0:T(8,128)(2,1)S(1)}, bf16[128,256]{1,0:T(8,128)(2,1)S(1)}, u32[]{:S(2)}, u32[]{:S(2)}) collective-permute-start(bf16[128,256]{1,0:T(8,128)(2,1)S(1)} %fusion.32), channel_id=1, source_target_pairs={{16,0},{17,1},{18,2},{19,3},{20,4},{21,5},{22,6},{23,7},{24,8},{25... | collective-permute-start | bytes 196616 | tf_op jit(solution)/shard_map/ppermute | solution.py:18
  210.8 24.0 %collective-permute-start.7 = (f32[2,2,128,256]{3,2,1,0:T(8,128)S(1)}, f32[2,2,128,256]{3,2,1,0:T(8,128)S(1)}, u32[]{:S(2)}, u32[]{:S(2)}) collective-permute-start(f32[2,2,128,256]{3,2,1,0:T(8,128)S(1)} %pad_maximum_fusion.5), channel_id=1, source_target_pairs={{0,8},{4,12},{8,0},{12,4},{1,9},{5,13},{9,1},{13,5},{2,10},{6,14},... | collective-permute-start | bytes 1572872 | tf_op jit(solution)/shard_map/ppermute | solution.py:12
  235.7 12.2 %collective-permute-start.8 = (f32[2,2,128,256]{3,2,1,0:T(8,128)}, f32[2,2,128,256]{3,2,1,0:T(8,128)S(1)}, u32[]{:S(2)}, u32[]{:S(2)}) collective-permute-start(f32[2,2,128,256]{3,2,1,0:T(8,128)} %pad_maximum_fusion.6), channel_id=1, source_target_pairs={{0,4},{4,0},{8,12},{12,8},{1,5},{5,1},{9,13},{13,9},{2,6},{6,2},{1... | collective-permute-start | bytes 1572872 | tf_op jit(solution)/shard_map/ppermute | solution.py:12
  290.7 12.1 %collective-permute-start.15 = (f32[2,2,128,64]{3,2,1,0:T(8,128)S(1)}, f32[2,2,128,64]{3,2,1,0:T(8,128)S(1)}, u32[]{:S(2)}, u32[]{:S(2)}) collective-permute-start(f32[2,2,128,64]{3,2,1,0:T(8,128)S(1)} %pad_maximum_fusion.12), channel_id=1, source_target_pairs={{0,4},{4,0},{8,12},{12,8},{1,5},{5,1},{9,13},{13,9},{2,6},{6,2},{1... | collective-permute-start | bytes 393224 | tf_op jit(solution)/shard_map/ppermute | solution.py:12
  292.6 21.7 %collective-permute-start.9 = (f32[2,2,128,256]{3,2,1,0:T(8,128)S(1)}, f32[2,2,128,256]{3,2,1,0:T(8,128)S(1)}, u32[]{:S(2)}, u32[]{:S(2)}) collective-permute-start(f32[2,2,128,256]{3,2,1,0:T(8,128)S(1)} %pad_maximum_fusion.7), channel_id=1, source_target_pairs={{0,4},{4,0},{8,12},{12,8},{1,5},{5,1},{9,13},{13,9},{2,6},{6,2},{1... | collective-permute-start | bytes 1572872 | tf_op jit(solution)/shard_map/ppermute | solution.py:12
  302.9 10.6 %collective-permute-start.16 = (f32[2,2,128,64]{3,2,1,0:T(8,128)S(1)}, f32[2,2,128,64]{3,2,1,0:T(8,128)S(1)}, u32[]{:S(2)}, u32[]{:S(2)}) collective-permute-start(f32[2,2,128,64]{3,2,1,0:T(8,128)S(1)} %maximum_add_fusion.5), channel_id=1, source_target_pairs={{0,8},{4,12},{8,0},{12,4},{1,9},{5,13},{9,1},{13,5},{2,10},{6,14},... | collective-permute-start | bytes 393224 | tf_op jit(solution)/shard_map/ppermute | solution.py:12
  314.5 24.3 %collective-permute-start.10 = (f32[2,2,128,256]{3,2,1,0:T(8,128)S(1)}, f32[2,2,128,256]{3,2,1,0:T(8,128)S(1)}, u32[]{:S(2)}, u32[]{:S(2)}) collective-permute-start(f32[2,2,128,256]{3,2,1,0:T(8,128)S(1)} %maximum_add_fusion.2), channel_id=1, source_target_pairs={{0,8},{4,12},{8,0},{12,4},{1,9},{5,13},{9,1},{13,5},{2,10},{6,14},... | collective-permute-start | bytes 1572872 | tf_op jit(solution)/shard_map/ppermute | solution.py:12
  (44 other events, 846.6 us)
Sparse Core Ops, SparseCore 0:
  256.2 31.7 all-reduce.7
where the time goes:
time: 349 us; the launch traced here: 348 us
  waiting for transfers between devices  268 us (77%)
  other arithmetic  18.6 us (5%)
  starting transfers between devices  18.2 us (5%)
  between operations  16.4 us (5%)
  local copies, waits for them, and re-layouts  14.9 us (4%)
  matrix products  11.7 us (3%)
    ppermute x16, waiting for transfers between devices, partner_2(): return lax.ppermute(value, axis, pairs)  231 us
    unnamed x2, waiting for transfers between devices  31.9 us
    ppermute x16, starting transfers between devices, partner_2(): return lax.ppermute(value, axis, pairs)  16.9 us
    dot_general x16, matrix products, apply_table(): jnp.einsum(pattern, block_table, values, precision=lax.Precision.HIGHEST)  11.7 us
    unnamed x103, local copies, waits for them, and re-layouts  10.2 us
  transfers between devices with their start and end apart: 18, of which 18 were waited for; matrix products, arithmetic and copies ran while one was open for 3% of the time, Pallas kernels for 0%

commit v1 on v0

v1 whole, which is shorter than its diff:
```python
import functools
import math

import jax
import jax.numpy as jnp
import ml_dtypes
import numpy as np
from jax import lax
from jax.experimental import pallas as pl
from jax.experimental.pallas import tpu as pltpu
from jax.sharding import PartitionSpec as P

BF16 = jnp.bfloat16
F32 = jnp.float32
VMEM_LIMIT = 56 * 1024 * 1024


def transform_tables(length):
    odd = 2 * np.arange(length, dtype=np.int64) + 1
    angles = math.pi / (4 * length) * (odd[:, None] * odd[None, :] % (8 * length))
    table = np.concatenate([np.cos(angles), np.sin(angles)], axis=0)
    half_angle = math.pi / (4 * length) * odd
    turns = np.stack([np.cos(half_angle), np.sin(half_angle)])
    return table.astype(ml_dtypes.bfloat16), turns.astype(np.float32)


def call(kernel, out_shape, scratch=()):
    def run(index, *arrays):
        return pl.pallas_call(
            kernel,
            out_shape=out_shape,
            in_specs=[pl.BlockSpec(memory_space=pltpu.SMEM)]
            + [pl.BlockSpec(memory_space=pltpu.VMEM)] * len(arrays),
            scratch_shapes=scratch,
            compiler_params=pltpu.CompilerParams(vmem_limit_bytes=VMEM_LIMIT),
        )(index, *arrays)

    return run


def dot(left, right):
    return jnp.dot(left, right, preferred_element_type=F32)


def pack(arrays, stage, outs, seq_index):
    count = len(outs)
    unit = arrays[0].shape[1] // count
    for block in range(count):
        lanes = slice(block * unit, (block + 1) * unit)
        stage[block] = jnp.concatenate([array[:, lanes] for array in arrays], axis=1)
    for step, out in enumerate(outs):
        out[...] = stage[seq_index ^ step]


def pack_first(index, post, held, loss, pre, filters, *rest):
    outs, stage = rest[:-1], rest[-1]
    held_value = held[0]
    gated = (post[0, 0].astype(F32) * held_value.astype(F32)).astype(BF16)
    kept = jnp.where(index[1] == 0, loss[...], held_value)
    pack([gated, filters[0].astype(BF16), kept, pre[0, 0]], stage, outs, index[0])


def pack_second(index, saved, pre, post, *rest):
    outs, stage = rest[:-1], rest[-1]
    mixed = (saved[0].astype(F32) * pre[0].astype(F32)).astype(BF16)
    pack([mixed[0], mixed[1], post[0, 1], pre[0, 1]], stage, outs, index[0])


def gather_positions(chunks, held, seq_index):
    rows = chunks[0].shape[0]
    for step, chunk in enumerate(chunks):
        at = pl.multiple_of((seq_index ^ step) * rows, rows)
        held[pl.ds(at, rows), :] = chunk[...]


def turned(spectrum, turns):
    length = spectrum.shape[0] // 2
    real, imag = spectrum[:length], spectrum[length:]
    return real * turns[0] + imag * turns[1], imag * turns[0] - real * turns[1]


def times_conj(spectrum, other_real, other_imag):
    length = spectrum.shape[0] // 2
    real, imag = spectrum[:length], spectrum[length:]
    return real * other_real + imag * other_imag, imag * other_real - real * other_imag


def inverse(table, real, imag):
    length = table.shape[1]
    return dot(table[:length], real.astype(BF16)) + dot(table[length:], imag.astype(BF16))


def first_tick(index, gain, table, turns, *rest):
    chunks, (out, gated_spec, filter_spec, held) = rest[:-4], rest[-4:]
    length = held.shape[0]
    unit = held.shape[1] // 4
    gather_positions(chunks, held, index[0])
    spec = dot(table[...], held[:, : 2 * unit])
    spec, filters = spec[:, :unit], turned(spec[:, unit:], turns)
    gated_spec[...] = spec
    filter_spec[0], filter_spec[1] = filters
    correlated = inverse(table, *times_conj(spec, *filters)) * (1.0 / length)
    gated = held[:, :unit].astype(F32)
    kept = held[:, 2 * unit : 3 * unit]
    gate_in = held[:, 3 * unit :].astype(F32)
    gradient = (kept.astype(F32) + gate_in * (correlated + gain[...] * gated)).astype(BF16)
    gradient = jnp.where(index[1] == 0, kept, gradient)
    out[...] = jnp.concatenate([gradient[: length // 2], gradient[length // 2 :]], axis=1)


def mixed_spectra(index, table, turns, gated_spec, *rest):
    chunks, (gates, lag_spec, mixed_spec, held) = rest[:-4], rest[-4:]
    unit = held.shape[1] // 4
    gather_positions(chunks, held, index[0])
    gates[...] = held[:, 2 * unit :]
    spec = dot(table[...], held[:, : 2 * unit])
    first = turned(spec[:, :unit], turns)
    lag_spec[0], lag_spec[1] = times_conj(gated_spec[...], *first)
    mixed_spec[0], mixed_spec[1] = turned(spec[:, unit:], turns)


def second_tick(
    scale, index, gain, table, received, filter_spec, lag_spec, mixed_spec, gates, *rest
):
    outs, stage = rest[:-1], rest[-1]
    length = table.shape[1]
    unit = gain.shape[1]
    carried = jnp.concatenate([received[:, :unit], received[:, unit:]], axis=0).astype(F32)
    gated = (gates[:, :unit].astype(F32) * carried).astype(BF16)
    spec = dot(table[...], gated)
    filtered = times_conj(spec, filter_spec[0], filter_spec[1])
    lagged = times_conj(spec, mixed_spec[0], mixed_spec[1])
    real = jnp.concatenate([filtered[0], lag_spec[0] + lagged[0]], axis=1)
    imag = jnp.concatenate([filtered[1], lag_spec[1] + lagged[1]], axis=1)
    both = inverse(table, real, imag)
    correlated = both[:, :unit] * (1.0 / length)
    lag_grad = both[:, unit:] * (scale / length)
    gate_in = gates[:, unit:].astype(F32)
    gradient = carried + gate_in * (correlated + gain[...] * gated.astype(F32))
    result = jnp.concatenate([gradient, lag_grad], axis=1).astype(BF16)
    stage[...] = result.reshape(stage.shape)
    for step, out in enumerate(outs):
        out[...] = stage[index[0] ^ step]


def unpack(index, *rest):
    *refs, stage, lag_stage = rest
    count = stage.shape[0]
    chan_count = lag_stage.shape[0]
    chunks, grad, lags = refs[:count], refs[count], refs[count + 1 :]
    unit = stage.shape[2] // 2
    for step, chunk in enumerate(chunks):
        stage[index[0] ^ step] = chunk[...]
    grad[0] = jnp.concatenate([stage[block][:, :unit] for block in range(count)], axis=1)
    lag_grad = jnp.concatenate([stage[block][:, unit:] for block in range(count)], axis=1)
    lag_grad = lag_grad.astype(F32)
    width = lag_grad.shape[1] // chan_count
    for block in range(chan_count):
        lag_stage[block] = lag_grad[:, block * width : (block + 1) * width]
    for step, lag in enumerate(lags):
        lag[...] = lag_stage[index[2] ^ step]


def exchange(chunks, axis):
    size = lax.axis_size(axis)
    return [chunks[0]] + [
        lax.ppermute(chunks[step], axis, [(i, i ^ step) for i in range(size)])
        for step in range(1, size)
    ]


def body(table, turns, *args):
    saved_input, pre_gate, post_gate, grad_held, loss_grad, filters, skip_gain = args
    seq_count = lax.axis_size("seq")
    chan_count = lax.axis_size("chan")
    section_count = lax.axis_size("section")
    _, tick_count, rows, width = saved_input.shape
    length = rows * seq_count
    unit = width // seq_count
    seq_index = lax.axis_index("seq")
    index = jnp.stack([seq_index, lax.axis_index("section"), lax.axis_index("chan")])
    index = index.astype(jnp.int32)
    table = jnp.asarray(table)
    turns = jnp.asarray(np.broadcast_to(turns[:, :, None], (2, length, unit)))
    gain = lax.dynamic_slice(skip_gain, (0, seq_index * unit), (1, unit))
    struct = jax.ShapeDtypeStruct
    chunk = struct((rows, 4 * unit), BF16)
    stage = pltpu.VMEM((seq_count, rows, 4 * unit), BF16)
    held_rows = pltpu.VMEM((length, 4 * unit), BF16)
    spectrum = struct((2, length, unit), F32)

    first = call(pack_first, [chunk] * seq_count, [stage])(
        index, post_gate, grad_held, loss_grad, pre_gate, filters
    )
    first = exchange(first, "seq")
    second = call(pack_second, [chunk] * seq_count, [stage])(
        index, saved_input, pre_gate, post_gate
    )
    second = exchange(second, "seq")

    gradient, gated_spec, filter_spec = call(
        first_tick,
        [
            struct((length // 2, 2 * unit), BF16),
            struct((2 * length, unit), F32),
            spectrum,
        ],
        [held_rows],
    )(index, gain, table, turns, *first)
    ring = [(i, (i - 1) % section_count) for i in range(section_count)]
    received = lax.ppermute(gradient, "section", ring)

    gates, lag_spec, mixed_spec = call(
        mixed_spectra, [struct((length, 2 * unit), BF16), spectrum, spectrum], [held_rows]
    )(index, table, turns, gated_spec, *second)

    scale = 1.0 / math.sqrt(length * chan_count * tick_count)
    result = call(
        functools.partial(second_tick, scale),
        [struct((rows, 2 * unit), BF16)] * seq_count,
        [pltpu.VMEM((seq_count, rows, 2 * unit), BF16)],
    )(index, gain, table, received, filter_spec, lag_spec, mixed_spec, gates)
    result = exchange(result, "seq")

    lag_width = width // chan_count
    grad_out, *lags = call(
        unpack,
        [struct((1, rows, width), BF16)] + [struct((rows, lag_width), F32)] * chan_count,
        [
            pltpu.VMEM((seq_count, rows, 2 * unit), BF16),
            pltpu.VMEM((chan_count, rows, lag_width), F32),
        ],
    )(index, *result)
    lags = exchange(lags, "chan")
    return grad_out, functools.reduce(jnp.add, lags)[None]


def solution(mesh):
    placed = (
        P("section", None, "seq", "chan"),
        P("section", None, "seq", "chan"),
        P("section", None, "seq", "chan"),
        P("section", "seq", "chan"),
        P("seq", "chan"),
        P("section", "seq", None),
        P("section", None),
    )

    def program(*args):
        return jax.shard_map(
            functools.partial(body, *transform_tables(args[0].shape[2])),
            mesh=mesh,
            in_specs=placed,
            out_specs=(P("section", "seq", "chan"), P("section", "seq", "chan")),
            check_vma=False,
        )(*args)

    return program
```

time: 349 us -> 52.6 us (0.15)
  waiting for transfers between devices: 268 us -> 11.6 us
  other arithmetic: 18.6 us -> 1.44 us
  Pallas kernels: 0 us -> 16.1 us
  between operations: 16.4 us -> 0.71 us
  matrix products: 11.7 us -> 0 us
  local copies, waits for them, and re-layouts: 14.9 us -> 4.15 us
    ppermute x17 -> x13, waiting for transfers between devices: 236 us -> 11.6 us  [the longest x12 11.6 us: exchange(): lax.ppermute(chunks[step], axis, [(i, i ^ step) for i in range(size)])]
    unnamed x2 -> x0, waiting for transfers between devices: 31.9 us -> none
    pallas_call x0 -> x6, Pallas kernels: none -> 16.1 us  [run(): pl.pallas_call(kernel, out_shape=out_shape, in_specs=[pl.BlockSpec(memory...]
    dot_general x16 -> x0, matrix products: 11.7 us -> none  [apply_table(): jnp.einsum(pattern, block_table, values, precision=lax.Precision.HIGHEST)]
    unnamed x103 -> x27, local copies, waits for them, and re-layouts: 10.2 us -> 2.58 us
    add x18 -> x0, other arithmetic: 5.67 us -> none  [the longest x10 3.83 us: rounds_forward(): partner + sign_self * spectrum]
    another operation x29 -> x1, other arithmetic: 4.93 us -> 0.58 us  [body(): jnp.stack([seq_index, lax.axis_index('section'), lax.axis_index('chan')])]
    ppermute x17 -> x13, starting transfers between devices: 18.2 us -> 18.2 us  [the longest x12 16.7 us: exchange(): lax.ppermute(chunks[step], axis, [(i, i ^ step) for i in range(size)])]
  transfers between devices with their start and end apart: 18 -> 13, of which waited for: 18 -> 5; matrix products, arithmetic and copies ran while one was open for 3% -> 3% of each run, Pallas kernels for 0% -> 17%
where the time goes in v1:
time: 52.6 us; the launch traced here: 52.2 us
  starting transfers between devices  18.2 us (35%)
  Pallas kernels  16.1 us (31%)
  waiting for transfers between devices  11.6 us (22%)
  local copies, waits for them, and re-layouts  4.15 us (8%)
  other arithmetic  1.44 us (3%)
  between operations  0.71 us (1%)
    ppermute x12, starting transfers between devices, exchange(): lax.ppermute(chunks[step], axis, [(i, i ^ step) for i in range(size)])  16.7 us
    pallas_call x6, Pallas kernels, run(): pl.pallas_call(kernel, out_shape=out_shape, in_specs=[pl.BlockSpec(memory...  16.1 us
    ppermute x12, waiting for transfers between devices, exchange(): lax.ppermute(chunks[step], axis, [(i, i ^ step) for i in range(size)])  11.6 us
    unnamed x27, local copies, waits for them, and re-layouts  2.58 us
    ppermute x1, starting transfers between devices, body(): received = lax.ppermute(gradient, 'section', ring)  1.49 us
  transfers between devices with their start and end apart: 13, of which 5 were waited for; matrix products, arithmetic and copies ran while one was open for 3% of the time, Pallas kernels for 17%

profile of v1, /device:TPU:0, one launch (start us, length us, event | category | flops | bytes accessed | tf_op | source)
XLA Modules:
  0.0 52.2 jit_solution(2463888639163165096)
XLA Ops:
  1.2 1.9 %shard_map.106 = (bf16[128,256]{1,0:T(8,128)(2,1)}, bf16[128,256]{1,0:T(8,128)(2,1)}, bf16[128,256]{1,0:T(8,128)(2,1)}, bf16[128,256]{1,0:T(8,128)(2,1)}) custom-call(s32[3]{0:T(128)} %pad_add_fusion.index, bf16[1,2,128,256]{3,2,1,0:T(8,128)(2,1)} %saved.1, bf16[1,2,128,256]{3,2,1,0:T(8,128)(2,1)} %pre.3, bf16[1,2,128,256]{3,2,1,0:T(8,128)(2,1)} %post.3), custom_call_target="tpu_custom_call" | custom-call | tf_op jit(solution)/shard_map/pallas_call | solution.py:29
  3.1 3.0 %collective-permute-start.4 = (bf16[128,256]{1,0:T(8,128)(2,1)}, bf16[128,256]{1,0:T(8,128)(2,1)S(1)}, u32[]{:S(2)}, u32[]{:S(2)}) collective-permute-start(bf16[128,256]{1,0:T(8,128)(2,1)} %get-tuple-element.33), channel_id=1, source_target_pairs={{0,4},{4,0},{8,12},{12,8},{1,5},{5,1},{9,13},{13,9},{2,6},{6,2},{1... | collective-permute-start | bytes 196616 | tf_op jit(solution)/shard_map/ppermute | solution.py:167
  6.1 2.6 %collective-permute-start.5 = (bf16[128,256]{1,0:T(8,128)(2,1)}, bf16[128,256]{1,0:T(8,128)(2,1)S(1)}, u32[]{:S(2)}, u32[]{:S(2)}) collective-permute-start(bf16[128,256]{1,0:T(8,128)(2,1)} %get-tuple-element.34), channel_id=1, source_target_pairs={{0,8},{4,12},{8,0},{12,4},{1,9},{5,13},{9,1},{13,5},{2,10},{6,14},... | collective-permute-start | bytes 196616 | tf_op jit(solution)/shard_map/ppermute | solution.py:167
  8.7 1.9 %shard_map.104 = (bf16[128,256]{1,0:T(8,128)(2,1)}, bf16[128,256]{1,0:T(8,128)(2,1)}, bf16[128,256]{1,0:T(8,128)(2,1)}, bf16[128,256]{1,0:T(8,128)(2,1)}) custom-call(s32[3]{0:T(128)} %pad_add_fusion.index, bf16[1,2,128,256]{3,2,1,0:T(8,128)(2,1)} %post.3, bf16[1,128,256]{2,1,0:T(8,128)(2,1)} %held.1, bf16[128,256]{1,0:T(8,128)(2,1)} %loss.1, ...), custom_call_target="tpu_custom_call" | custom-call | tf_op jit(solution)/shard_map/pallas_call | solution.py:29
  11.2 3.9 %collective-permute-start.2 = (bf16[128,256]{1,0:T(8,128)(2,1)}, bf16[128,256]{1,0:T(8,128)(2,1)S(1)}, u32[]{:S(2)}, u32[]{:S(2)}) collective-permute-start(bf16[128,256]{1,0:T(8,128)(2,1)} %get-tuple-element.28), channel_id=1, source_target_pairs={{0,12},{4,8},{8,4},{12,0},{1,13},{5,9},{9,5},{13,1},{2,14},{6,10},... | collective-permute-start | bytes 196616 | tf_op jit(solution)/shard_map/ppermute | solution.py:167
  16.0 3.9 %collective-permute-done.1.rest_2_ = bf16[128,256]{1,0:T(8,128)(2,1)S(1)} collective-permute-done((bf16[128,256]{1,0:T(8,128)(2,1)}, bf16[128,256]{1,0:T(8,128)(2,1)S(1)}, u32[]{:S(2)}, u32[]{:S(2)}) %collective-permute-start.1) | collective-permute-done | bytes 65568 | tf_op jit(solution)/shard_map/ppermute | solution.py:167
  20.0 1.0 %jit_solution_.3.turns = f32[2,512,64]{2,1,0:T(8,128)} broadcast(f32[2,512]{1,0:T(2,128)S(1)} %copy-done.11), dimensions={0,1} | broadcast | bytes 266240 | tf_op jit(solution)
  21.0 3.6 %shard_map.105 = (bf16[256,128]{1,0:T(8,128)(2,1)}, f32[1024,64]{1,0:T(8,128)}, f32[2,512,64]{2,1,0:T(8,128)}) custom-call(s32[3]{0:T(128)} %pad_add_fusion.index, f32[1,64]{1,0:T(1,128)} %constant_dynamic-slice_fusion.gain, bf16[1024,512]{1,0:T(8,128)(2,1)} %constant.23.clone.table, f32[2,512,64]{2,1,0:T(8,128)} %jit_solution_.3.turns, ...), custom_call_target="tpu_custom_call" | custom-call | tf_op jit(solution)/shard_map/pallas_call | solution.py:29
  24.6 1.5 %collective-permute-start.3 = (bf16[256,128]{1,0:T(8,128)(2,1)}, bf16[256,128]{1,0:T(8,128)(2,1)S(1)}, u32[]{:S(2)}, u32[]{:S(2)}) collective-permute-start(bf16[256,128]{1,0:T(8,128)(2,1)} %get-tuple-element.29), channel_id=1, source_target_pairs={{0,16},{16,0},{1,17},{17,1},{2,18},{18,2},{3,19},{19,3},{4,20},{20... | collective-permute-start | bytes 196616 | tf_op jit(solution)/shard_map/ppermute | solution.py:211
  26.8 3.1 %shard_map.107 = (bf16[512,128]{1,0:T(8,128)(2,1)}, f32[2,512,64]{2,1,0:T(8,128)}, f32[2,512,64]{2,1,0:T(8,128)}) custom-call(s32[3]{0:T(128)} %pad_add_fusion.index, bf16[1024,512]{1,0:T(8,128)(2,1)} %constant.23.clone.table, f32[2,512,64]{2,1,0:T(8,128)} %jit_solution_.3.turns, f32[1024,64]{1,0:T(8,128)} %get-tuple-element.31.gated_spec, ...), custom_call_target="tpu_custom_call" | custom-call | tf_op jit(solution)/shard_map/pallas_call | solution.py:29
  29.9 0.6 %copy-done.7 = bf16[256,128]{1,0:T(8,128)(2,1)} copy-done((bf16[256,128]{1,0:T(8,128)(2,1)}, bf16[256,128]{1,0:T(8,128)(2,1)S(1)}, u32[]{:S(2)}) %copy-start.7) | copy-done | bytes 65560
  30.5 3.9 %shard_map.108 = (bf16[128,128]{1,0:T(8,128)(2,1)}, bf16[128,128]{1,0:T(8,128)(2,1)}, bf16[128,128]{1,0:T(8,128)(2,1)}, bf16[128,128]{1,0:T(8,128)(2,1)}) custom-call(s32[3]{0:T(128)} %pad_add_fusion.index, f32[1,64]{1,0:T(1,128)} %constant_dynamic-slice_fusion.gain, bf16[1024,512]{1,0:T(8,128)(2,1)} %constant.23.clone.table, bf16[256,128]{1,0:T(8,128)(2,1)} %copy-done.7, ...), custom_call_target="tpu_custom_call" | custom-call | tf_op jit(solution)/shard_map/pallas_call | solution.py:29
  34.4 1.4 %collective-permute-start.7 = (bf16[128,128]{1,0:T(8,128)(2,1)}, bf16[128,128]{1,0:T(8,128)(2,1)S(1)}, u32[]{:S(2)}, u32[]{:S(2)}) collective-permute-start(bf16[128,128]{1,0:T(8,128)(2,1)} %get-tuple-element.40), channel_id=1, source_target_pairs={{0,4},{4,0},{8,12},{12,8},{1,5},{5,1},{9,13},{13,9},{2,6},{6,2},{1... | collective-permute-start | bytes 98312 | tf_op jit(solution)/shard_map/ppermute | solution.py:167
  35.9 0.7 %collective-permute-start.8 = (bf16[128,128]{1,0:T(8,128)(2,1)}, bf16[128,128]{1,0:T(8,128)(2,1)S(1)}, u32[]{:S(2)}, u32[]{:S(2)}) collective-permute-start(bf16[128,128]{1,0:T(8,128)(2,1)} %get-tuple-element.41), channel_id=1, source_target_pairs={{0,8},{4,12},{8,0},{12,4},{1,9},{5,13},{9,1},{13,5},{2,10},{6,14},... | collective-permute-start | bytes 98312 | tf_op jit(solution)/shard_map/ppermute | solution.py:167
  36.5 2.3 %collective-permute-start.9 = (bf16[128,128]{1,0:T(8,128)(2,1)}, bf16[128,128]{1,0:T(8,128)(2,1)S(1)}, u32[]{:S(2)}, u32[]{:S(2)}) collective-permute-start(bf16[128,128]{1,0:T(8,128)(2,1)} %get-tuple-element.42), channel_id=1, source_target_pairs={{0,12},{4,8},{8,4},{12,0},{1,13},{5,9},{9,5},{13,1},{2,14},{6,10},... | collective-permute-start | bytes 98312 | tf_op jit(solution)/shard_map/ppermute | solution.py:167
  38.8 2.4 %collective-permute-done.8.rest_2_ = bf16[128,128]{1,0:T(8,128)(2,1)S(1)} collective-permute-done((bf16[128,128]{1,0:T(8,128)(2,1)}, bf16[128,128]{1,0:T(8,128)(2,1)S(1)}, u32[]{:S(2)}, u32[]{:S(2)}) %collective-permute-start.8) | collective-permute-done | bytes 32800 | tf_op jit(solution)/shard_map/ppermute | solution.py:167
  41.2 1.2 %collective-permute-done.9.rest_3_ = bf16[128,128]{1,0:T(8,128)(2,1)S(1)} collective-permute-done((bf16[128,128]{1,0:T(8,128)(2,1)}, bf16[128,128]{1,0:T(8,128)(2,1)S(1)}, u32[]{:S(2)}, u32[]{:S(2)}) %collective-permute-start.9) | collective-permute-done | bytes 32800 | tf_op jit(solution)/shard_map/ppermute | solution.py:167
  42.5 0.6 %copy-done.10 = bf16[128,128]{1,0:T(8,128)(2,1)} copy-done((bf16[128,128]{1,0:T(8,128)(2,1)}, bf16[128,128]{1,0:T(8,128)(2,1)S(1)}, u32[]{:S(2)}) %copy-start.10) | copy-done | bytes 32792
  43.0 1.7 %shard_map.109 = (bf16[1,128,256]{2,1,0:T(8,128)(2,1)}, f32[128,64]{1,0:T(8,128)}, f32[128,64]{1,0:T(8,128)}, f32[128,64]{1,0:T(8,128)}, f32[128,64]{1,0:T(8,128)}) custom-call(s32[3]{0:T(128)} %pad_add_fusion.index, bf16[128,128]{1,0:T(8,128)(2,1)} %get-tuple-element.39.rest_0_, bf16[128,128]{1,0:T(8,128)(2,1)} %copy-done.8, bf16[128,128]{1,0:T(8,128)(2,1)} %copy-done.9, ...), custom_call_target="tpu_custom_call" | custom-call | tf_op jit(solution)/shard_map/pallas_call | solution.py:29
  44.7 1.6 %collective-permute-start.11 = (f32[128,64]{1,0:T(8,128)}, f32[128,64]{1,0:T(8,128)S(1)}, u32[]{:S(2)}, u32[]{:S(2)}) collective-permute-start(f32[128,64]{1,0:T(8,128)} %get-tuple-element.46), channel_id=1, source_target_pairs={{0,2},{1,3},{2,0},{3,1},{4,6},{5,7},{6,4},{7,5},{8,10},{9,11},{10,... | collective-permute-start | bytes 98312 | tf_op jit(solution)/shard_map/ppermute | solution.py:167
  46.6 2.9 %collective-permute-done.11 = f32[128,64]{1,0:T(8,128)S(1)} collective-permute-done((f32[128,64]{1,0:T(8,128)}, f32[128,64]{1,0:T(8,128)S(1)}, u32[]{:S(2)}, u32[]{:S(2)}) %collective-permute-start.11) | collective-permute-done | bytes 32800 | tf_op jit(solution)/shard_map/ppermute | solution.py:167
  49.5 1.2 %collective-permute-done.12 = f32[128,64]{1,0:T(8,128)S(1)} collective-permute-done((f32[128,64]{1,0:T(8,128)}, f32[128,64]{1,0:T(8,128)S(1)}, u32[]{:S(2)}, u32[]{:S(2)}) %collective-permute-start.12) | collective-permute-done | bytes 32800 | tf_op jit(solution)/shard_map/ppermute | solution.py:167
  50.6 0.9 %add_bitcast_fusion = f32[1,128,64]{2,1,0:T(8,128)S(1)} fusion(f32[128,64]{1,0:T(8,128)S(1)} %collective-permute-done.12, f32[128,64]{1,0:T(8,128)S(1)} %collective-permute-done.11, f32[128,64]{1,0:T(8,128)} %get-tuple-element.44, f32[128,64]{1,0:T(8,128)S(1)} %collective-permute-done.10), kind=kLoop, calls=%fused_computation | loop fusion | flops 24576 | bytes 163840 | tf_op jit(solution)/shard_map/broadcast_in_dim | solution.py:235
  51.5 0.7 %copy.11 = f32[1,128,64]{1,2,0:T(8,128)} copy(f32[1,128,64]{2,1,0:T(8,128)S(1)} %add_bitcast_fusion) | data formatting | bytes 65536
  (39 shorter events, 3.0 us)
Async XLA Ops:
  0.6 14.4 %copy-start = (f32[1,256]{1,0:T(1,128)S(1)}, f32[1,256]{1,0:T(1,128)}, u32[]{:S(2)}) copy-start(f32[1,256]{1,0:T(1,128)} %param.15) | copy-start | bytes 3076
  3.1 23.0 %collective-permute-start.4 = (bf16[128,256]{1,0:T(8,128)(2,1)}, bf16[128,256]{1,0:T(8,128)(2,1)S(1)}, u32[]{:S(2)}, u32[]{:S(2)}) collective-permute-start(bf16[128,256]{1,0:T(8,128)(2,1)} %get-tuple-element.33), channel_id=1, source_target_pairs={{0,4},{4,0},{8,12},{12,8},{1,5},{5,1},{9,13},{13,9},{2,6},{6,2},{1... | collective-permute-start | bytes 196616 | tf_op jit(solution)/shard_map/ppermute | solution.py:167
  6.1 9.5 %copy-start.12 = (bf16[128,256]{1,0:T(8,128)(2,1)S(1)}, bf16[128,256]{1,0:T(8,128)(2,1)}, u32[]{:S(2)}) copy-start(bf16[128,256]{1,0:T(8,128)(2,1)} %get-tuple-element.35) | copy-start | bytes 196612
  6.1 20.0 %collective-permute-start.5 = (bf16[128,256]{1,0:T(8,128)(2,1)}, bf16[128,256]{1,0:T(8,128)(2,1)S(1)}, u32[]{:S(2)}, u32[]{:S(2)}) collective-permute-start(bf16[128,256]{1,0:T(8,128)(2,1)} %get-tuple-element.34), channel_id=1, source_target_pairs={{0,8},{4,12},{8,0},{12,4},{1,9},{5,13},{9,1},{13,5},{2,10},{6,14},... | collective-permute-start | bytes 196616 | tf_op jit(solution)/shard_map/ppermute | solution.py:167
  10.7 5.0 %collective-permute-start = (bf16[128,256]{1,0:T(8,128)(2,1)}, bf16[128,256]{1,0:T(8,128)(2,1)S(1)}, u32[]{:S(2)}, u32[]{:S(2)}) collective-permute-start(bf16[128,256]{1,0:T(8,128)(2,1)} %get-tuple-element.26), channel_id=1, source_target_pairs={{0,4},{4,0},{8,12},{12,8},{1,5},{5,1},{9,13},{13,9},{2,6},{6,2},{1... | collective-permute-start | bytes 196616 | tf_op jit(solution)/shard_map/ppermute | solution.py:167
  11.1 8.8 %collective-permute-start.1 = (bf16[128,256]{1,0:T(8,128)(2,1)}, bf16[128,256]{1,0:T(8,128)(2,1)S(1)}, u32[]{:S(2)}, u32[]{:S(2)}) collective-permute-start(bf16[128,256]{1,0:T(8,128)(2,1)} %get-tuple-element.27), channel_id=1, source_target_pairs={{0,8},{4,12},{8,0},{12,4},{1,9},{5,13},{9,1},{13,5},{2,10},{6,14},... | collective-permute-start | bytes 196616 | tf_op jit(solution)/shard_map/ppermute | solution.py:167
  11.2 8.8 %collective-permute-start.2 = (bf16[128,256]{1,0:T(8,128)(2,1)}, bf16[128,256]{1,0:T(8,128)(2,1)S(1)}, u32[]{:S(2)}, u32[]{:S(2)}) collective-permute-start(bf16[128,256]{1,0:T(8,128)(2,1)} %get-tuple-element.28), channel_id=1, source_target_pairs={{0,12},{4,8},{8,4},{12,0},{1,13},{5,9},{9,5},{13,1},{2,14},{6,10},... | collective-permute-start | bytes 196616 | tf_op jit(solution)/shard_map/ppermute | solution.py:167
  15.1 4.9 %copy-start.11 = (f32[2,512]{1,0:T(2,128)S(1)}, f32[2,512]{1,0:T(2,128)}, u32[]{:S(2)}) copy-start(f32[2,512]{1,0:T(2,128)} %constant.24.clone) | copy-start | bytes 12292
  15.6 5.4 %copy-start.3 = (bf16[128,256]{1,0:T(8,128)(2,1)}, bf16[128,256]{1,0:T(8,128)(2,1)S(1)}, u32[]{:S(2)}) copy-start(bf16[128,256]{1,0:T(8,128)(2,1)S(1)} %collective-permute-done.rest_1_) | copy-start | bytes 196612
  15.6 10.5 %collective-permute-start.6 = (bf16[128,256]{1,0:T(8,128)(2,1)S(1)}, bf16[128,256]{1,0:T(8,128)(2,1)S(1)}, u32[]{:S(2)}, u32[]{:S(2)}) collective-permute-start(bf16[128,256]{1,0:T(8,128)(2,1)S(1)} %copy-done.12), channel_id=1, source_target_pairs={{0,12},{4,8},{8,4},{12,0},{1,13},{5,9},{9,5},{13,1},{2,14},{6,10},... | collective-permute-start | bytes 196616 | tf_op jit(solution)/shard_map/ppermute | solution.py:167
  19.9 1.0 %copy-start.5 = (bf16[128,256]{1,0:T(8,128)(2,1)}, bf16[128,256]{1,0:T(8,128)(2,1)S(1)}, u32[]{:S(2)}) copy-start(bf16[128,256]{1,0:T(8,128)(2,1)S(1)} %collective-permute-done.1.rest_2_) | copy-start | bytes 196612
  20.0 1.0 %copy-start.6 = (bf16[128,256]{1,0:T(8,128)(2,1)}, bf16[128,256]{1,0:T(8,128)(2,1)S(1)}, u32[]{:S(2)}) copy-start(bf16[128,256]{1,0:T(8,128)(2,1)S(1)} %collective-permute-done.2.rest_3_) | copy-start | bytes 196612
  24.6 5.3 %collective-permute-start.3 = (bf16[256,128]{1,0:T(8,128)(2,1)}, bf16[256,128]{1,0:T(8,128)(2,1)S(1)}, u32[]{:S(2)}, u32[]{:S(2)}) collective-permute-start(bf16[256,128]{1,0:T(8,128)(2,1)} %get-tuple-element.29), channel_id=1, source_target_pairs={{0,16},{16,0},{1,17},{17,1},{2,18},{18,2},{3,19},{19,3},{4,20},{20... | collective-permute-start | bytes 196616 | tf_op jit(solution)/shard_map/ppermute | solution.py:211
  26.1 0.6 %copy-start.1 = (bf16[128,256]{1,0:T(8,128)(2,1)}, bf16[128,256]{1,0:T(8,128)(2,1)S(1)}, u32[]{:S(2)}) copy-start(bf16[128,256]{1,0:T(8,128)(2,1)S(1)} %collective-permute-done.4.rest_1_) | copy-start | bytes 196612
  26.1 0.6 %copy-start.2 = (bf16[128,256]{1,0:T(8,128)(2,1)}, bf16[128,256]{1,0:T(8,128)(2,1)S(1)}, u32[]{:S(2)}) copy-start(bf16[128,256]{1,0:T(8,128)(2,1)S(1)} %collective-permute-done.5.rest_2_) | copy-start | bytes 196612
  26.1 0.6 %copy-start.4 = (bf16[128,256]{1,0:T(8,128)(2,1)}, bf16[128,256]{1,0:T(8,128)(2,1)S(1)}, u32[]{:S(2)}) copy-start(bf16[128,256]{1,0:T(8,128)(2,1)S(1)} %collective-permute-done.6.rest_3_) | copy-start | bytes 196612
  34.4 4.4 %collective-permute-start.7 = (bf16[128,128]{1,0:T(8,128)(2,1)}, bf16[128,128]{1,0:T(8,128)(2,1)S(1)}, u32[]{:S(2)}, u32[]{:S(2)}) collective-permute-start(bf16[128,128]{1,0:T(8,128)(2,1)} %get-tuple-element.40), channel_id=1, source_target_pairs={{0,4},{4,0},{8,12},{12,8},{1,5},{5,1},{9,13},{13,9},{2,6},{6,2},{1... | collective-permute-start | bytes 98312 | tf_op jit(solution)/shard_map/ppermute | solution.py:167
  35.9 5.4 %collective-permute-start.8 = (bf16[128,128]{1,0:T(8,128)(2,1)}, bf16[128,128]{1,0:T(8,128)(2,1)S(1)}, u32[]{:S(2)}, u32[]{:S(2)}) collective-permute-start(bf16[128,128]{1,0:T(8,128)(2,1)} %get-tuple-element.41), channel_id=1, source_target_pairs={{0,8},{4,12},{8,0},{12,4},{1,9},{5,13},{9,1},{13,5},{2,10},{6,14},... | collective-permute-start | bytes 98312 | tf_op jit(solution)/shard_map/ppermute | solution.py:167
  36.5 5.9 %collective-permute-start.9 = (bf16[128,128]{1,0:T(8,128)(2,1)}, bf16[128,128]{1,0:T(8,128)(2,1)S(1)}, u32[]{:S(2)}, u32[]{:S(2)}) collective-permute-start(bf16[128,128]{1,0:T(8,128)(2,1)} %get-tuple-element.42), channel_id=1, source_target_pairs={{0,12},{4,8},{8,4},{12,0},{1,13},{5,9},{9,5},{13,1},{2,14},{6,10},... | collective-permute-start | bytes 98312 | tf_op jit(solution)/shard_map/ppermute | solution.py:167
  38.8 3.7 %copy-start.8 = (bf16[128,128]{1,0:T(8,128)(2,1)}, bf16[128,128]{1,0:T(8,128)(2,1)S(1)}, u32[]{:S(2)}) copy-start(bf16[128,128]{1,0:T(8,128)(2,1)S(1)} %collective-permute-done.7.rest_1_) | copy-start | bytes 98308
  41.2 1.2 %copy-start.9 = (bf16[128,128]{1,0:T(8,128)(2,1)}, bf16[128,128]{1,0:T(8,128)(2,1)S(1)}, u32[]{:S(2)}) copy-start(bf16[128,128]{1,0:T(8,128)(2,1)S(1)} %collective-permute-done.8.rest_2_) | copy-start | bytes 98308
  44.7 1.9 %collective-permute-start.10 = (f32[128,64]{1,0:T(8,128)}, f32[128,64]{1,0:T(8,128)S(1)}, u32[]{:S(2)}, u32[]{:S(2)}) collective-permute-start(f32[128,64]{1,0:T(8,128)} %get-tuple-element.45), channel_id=1, source_target_pairs={{0,1},{1,0},{2,3},{3,2},{4,5},{5,4},{6,7},{7,6},{8,9},{9,8},{10,11... | collective-permute-start | bytes 98312 | tf_op jit(solution)/shard_map/ppermute | solution.py:167
  44.7 4.7 %collective-permute-start.11 = (f32[128,64]{1,0:T(8,128)}, f32[128,64]{1,0:T(8,128)S(1)}, u32[]{:S(2)}, u32[]{:S(2)}) collective-permute-start(f32[128,64]{1,0:T(8,128)} %get-tuple-element.46), channel_id=1, source_target_pairs={{0,2},{1,3},{2,0},{3,1},{4,6},{5,7},{6,4},{7,5},{8,10},{9,11},{10,... | collective-permute-start | bytes 98312 | tf_op jit(solution)/shard_map/ppermute | solution.py:167
  46.3 4.3 %collective-permute-start.12 = (f32[128,64]{1,0:T(8,128)}, f32[128,64]{1,0:T(8,128)S(1)}, u32[]{:S(2)}, u32[]{:S(2)}) collective-permute-start(f32[128,64]{1,0:T(8,128)} %get-tuple-element.47), channel_id=1, source_target_pairs={{0,3},{1,2},{2,1},{3,0},{4,7},{5,6},{6,5},{7,4},{8,11},{9,10},{10,... | collective-permute-start | bytes 98312 | tf_op jit(solution)/shard_map/ppermute | solution.py:167
  (2 other events, 1.2 us)

commit v2 on v1

--- a/solution.py
+++ b/solution.py
@@ -12,7 +12,6 @@
 
 BF16 = jnp.bfloat16
 F32 = jnp.float32
-VMEM_LIMIT = 56 * 1024 * 1024
 
 
 def transform_tables(length):
@@ -24,16 +23,24 @@
     return table.astype(ml_dtypes.bfloat16), turns.astype(np.float32)
 
 
+def size_of(shapes):
+    total = 0
+    for shape in shapes:
+        lanes = -(-shape.shape[-1] // 128) * 128
+        total += math.prod(shape.shape[:-1]) * lanes * jnp.dtype(shape.dtype).itemsize
+    return total
+
+
 def call(kernel, out_shape, scratch=()):
-    def run(index, *arrays):
+    def run(*arrays):
+        held = size_of([*arrays, *out_shape, *scratch])
         return pl.pallas_call(
             kernel,
             out_shape=out_shape,
-            in_specs=[pl.BlockSpec(memory_space=pltpu.SMEM)]
-            + [pl.BlockSpec(memory_space=pltpu.VMEM)] * len(arrays),
-            scratch_shapes=scratch,
-            compiler_params=pltpu.CompilerParams(vmem_limit_bytes=VMEM_LIMIT),
-        )(index, *arrays)
+            in_specs=[pl.BlockSpec(memory_space=pltpu.VMEM)] * len(arrays),
+            scratch_shapes=[pltpu.VMEM(shape.shape, shape.dtype) for shape in scratch],
+            compiler_params=pltpu.CompilerParams(vmem_limit_bytes=2 * held + (4 << 20)),
+        )(*arrays)
 
     return run
 
@@ -42,7 +49,8 @@
     return jnp.dot(left, right, preferred_element_type=F32)
 
 
-def pack(arrays, stage, outs, seq_index):
+def pack(arrays, stage, outs):
+    seq_index = lax.axis_index("seq")
     count = len(outs)
     unit = arrays[0].shape[1] // count
     for block in range(count):
@@ -52,21 +60,23 @@
         out[...] = stage[seq_index ^ step]
 
 
-def pack_first(index, post, held, loss, pre, filters, *rest):
+def pack_first(post, held, loss, pre, filters, *rest):
     outs, stage = rest[:-1], rest[-1]
     held_value = held[0]
     gated = (post[0, 0].astype(F32) * held_value.astype(F32)).astype(BF16)
-    kept = jnp.where(index[1] == 0, loss[...], held_value)
-    pack([gated, filters[0].astype(BF16), kept, pre[0, 0]], stage, outs, index[0])
-
-
-def pack_second(index, saved, pre, post, *rest):
+    kept = jnp.where(lax.axis_index("section") == 0, loss[...], held_value)
+    pack([gated, filters[0].astype(BF16), kept, pre[0, 0]], stage, outs)
+
+
+def pack_second(after, saved, pre, post, *rest):
+    del after
     outs, stage = rest[:-1], rest[-1]
     mixed = (saved[0].astype(F32) * pre[0].astype(F32)).astype(BF16)
-    pack([mixed[0], mixed[1], post[0, 1], pre[0, 1]], stage, outs, index[0])
-
-
-def gather_positions(chunks, held, seq_index):
+    pack([mixed[0], mixed[1], post[0, 1], pre[0, 1]], stage, outs)
+
+
+def gather_positions(chunks, held):
+    seq_index = lax.axis_index("seq")
     rows = chunks[0].shape[0]
     for step, chunk in enumerate(chunks):
         at = pl.multiple_of((seq_index ^ step) * rows, rows)
@@ -90,11 +100,11 @@
     return dot(table[:length], real.astype(BF16)) + dot(table[length:], imag.astype(BF16))
 
 
-def first_tick(index, gain, table, turns, *rest):
+def first_tick(gain, table, turns, *rest):
     chunks, (out, gated_spec, filter_spec, held) = rest[:-4], rest[-4:]
     length = held.shape[0]
     unit = held.shape[1] // 4
-    gather_positions(chunks, held, index[0])
+    gather_positions(chunks, held)
     spec = dot(table[...], held[:, : 2 * unit])
     spec, filters = spec[:, :unit], turned(spec[:, unit:], turns)
     gated_spec[...] = spec
@@ -104,14 +114,14 @@
     kept = held[:, 2 * unit : 3 * unit]
     gate_in = held[:, 3 * unit :].astype(F32)
     gradient = (kept.astype(F32) + gate_in * (correlated + gain[...] * gated)).astype(BF16)
-    gradient = jnp.where(index[1] == 0, kept, gradient)
+    gradient = jnp.where(lax.axis_index("section") == 0, kept, gradient)
     out[...] = jnp.concatenate([gradient[: length // 2], gradient[length // 2 :]], axis=1)
 
 
-def mixed_spectra(index, table, turns, gated_spec, *rest):
+def mixed_spectra(table, turns, gated_spec, *rest):
     chunks, (gates, lag_spec, mixed_spec, held) = rest[:-4], rest[-4:]
     unit = held.shape[1] // 4
-    gather_positions(chunks, held, index[0])
+    gather_positions(chunks, held)
     gates[...] = held[:, 2 * unit :]
     spec = dot(table[...], held[:, : 2 * unit])
     first = turned(spec[:, :unit], turns)
@@ -120,7 +130,7 @@
 
 
 def second_tick(
-    scale, index, gain, table, received, filter_spec, lag_spec, mixed_spec, gates, *rest
+    scale, gain, table, received, filter_spec, lag_spec, mixed_spec, gates, *rest
 ):
     outs, stage = rest[:-1], rest[-1]
     length = table.shape[1]
@@ -140,25 +150,28 @@
     result = jnp.concatenate([gradient, lag_grad], axis=1).astype(BF16)
     stage[...] = result.reshape(stage.shape)
     for step, out in enumerate(outs):
-        out[...] = stage[index[0] ^ step]
-
-
-def unpack(index, *rest):
+        out[...] = stage[lax.axis_index("seq") ^ step]
+
+
+def unpack(*rest):
     *refs, stage, lag_stage = rest
     count = stage.shape[0]
-    chan_count = lag_stage.shape[0]
     chunks, grad, lags = refs[:count], refs[count], refs[count + 1 :]
     unit = stage.shape[2] // 2
+    seq_index, chan_index = lax.axis_index("seq"), lax.axis_index("chan")
     for step, chunk in enumerate(chunks):
-        stage[index[0] ^ step] = chunk[...]
+        stage[seq_index ^ step] = chunk[...]
     grad[0] = jnp.concatenate([stage[block][:, :unit] for block in range(count)], axis=1)
     lag_grad = jnp.concatenate([stage[block][:, unit:] for block in range(count)], axis=1)
-    lag_grad = lag_grad.astype(F32)
-    width = lag_grad.shape[1] // chan_count
-    for block in range(chan_count):
-        lag_stage[block] = lag_grad[:, block * width : (block + 1) * width]
+    lag_stage[...] = lag_grad.astype(F32).T
     for step, lag in enumerate(lags):
-        lag[...] = lag_stage[index[2] ^ step]
+        width = lag.shape[0]
+        lag[...] = lag_stage[pl.ds(pl.multiple_of((chan_index ^ step) * width, width), width), :]
+
+
+def add_up(*refs):
+    *lags, out = refs
+    out[...] = functools.reduce(jnp.add, [lag[...] for lag in lags])
 
 
 def exchange(chunks, axis):
@@ -178,24 +191,22 @@
     length = rows * seq_count
     unit = width // seq_count
     seq_index = lax.axis_index("seq")
-    index = jnp.stack([seq_index, lax.axis_index("section"), lax.axis_index("chan")])
-    index = index.astype(jnp.int32)
     table = jnp.asarray(table)
-    turns = jnp.asarray(np.broadcast_to(turns[:, :, None], (2, length, unit)))
+    turns = jnp.asarray(np.array(np.broadcast_to(turns[:, :, None], (2, length, unit))))
     gain = lax.dynamic_slice(skip_gain, (0, seq_index * unit), (1, unit))
     struct = jax.ShapeDtypeStruct
     chunk = struct((rows, 4 * unit), BF16)
-    stage = pltpu.VMEM((seq_count, rows, 4 * unit), BF16)
-    held_rows = pltpu.VMEM((length, 4 * unit), BF16)
+    stage = struct((seq_count, rows, 4 * unit), BF16)
+    held_rows = struct((length, 4 * unit), BF16)
     spectrum = struct((2, length, unit), F32)
 
     first = call(pack_first, [chunk] * seq_count, [stage])(
-        index, post_gate, grad_held, loss_grad, pre_gate, filters
+        post_gate, grad_held, loss_grad, pre_gate, filters
+    )
+    second = call(pack_second, [chunk] * seq_count, [stage])(
+        first[0], saved_input, pre_gate, post_gate
     )
     first = exchange(first, "seq")
-    second = call(pack_second, [chunk] * seq_count, [stage])(
-        index, saved_input, pre_gate, post_gate
-    )
     second = exchange(second, "seq")
 
     gradient, gated_spec, filter_spec = call(
@@ -206,33 +217,34 @@
             spectrum,
         ],
         [held_rows],
-    )(index, gain, table, turns, *first)
+    )(gain, table, turns, *first)
     ring = [(i, (i - 1) % section_count) for i in range(section_count)]
     received = lax.ppermute(gradient, "section", ring)
 
     gates, lag_spec, mixed_spec = call(
         mixed_spectra, [struct((length, 2 * unit), BF16), spectrum, spectrum], [held_rows]
-    )(index, table, turns, gated_spec, *second)
+    )(table, turns, gated_spec, *second)
 
     scale = 1.0 / math.sqrt(length * chan_count * tick_count)
     result = call(
         functools.partial(second_tick, scale),
         [struct((rows, 2 * unit), BF16)] * seq_count,
-        [pltpu.VMEM((seq_count, rows, 2 * unit), BF16)],
-    )(index, gain, table, received, filter_spec, lag_spec, mixed_spec, gates)
+        [struct((seq_count, rows, 2 * unit), BF16)],
+    )(gain, table, received, filter_spec, lag_spec, mixed_spec, gates)
     result = exchange(result, "seq")
 
     lag_width = width // chan_count
     grad_out, *lags = call(
         unpack,
-        [struct((1, rows, width), BF16)] + [struct((rows, lag_width), F32)] * chan_count,
+        [struct((1, rows, width), BF16)] + [struct((lag_width, rows), F32)] * chan_count,
         [
-            pltpu.VMEM((seq_count, rows, 2 * unit), BF16),
-            pltpu.VMEM((chan_count, rows, lag_width), F32),
+            struct((seq_count, rows, 2 * unit), BF16),
+            struct((width, rows), F32),
         ],
-    )(index, *result)
+    )(*result)
     lags = exchange(lags, "chan")
-    return grad_out, functools.reduce(jnp.add, lags)[None]
+    (lag_grad,) = call(add_up, [struct((lag_width, rows), F32)])(*lags)
+    return grad_out, lag_grad.T[None]
 
 
 def solution(mesh):

time: 52.6 us -> 43.8 us (0.83)
  Pallas kernels: 16.1 us -> 5.47 us
  local copies, waits for them, and re-layouts: 4.15 us -> 8.47 us
  other arithmetic: 1.44 us -> 0 us
  waiting for transfers between devices: 11.6 us -> 10.6 us
    pallas_call x6 -> x7, Pallas kernels: 16.1 us -> 5.47 us  [run(): pl.pallas_call(kernel, out_shape=out_shape, in_specs=[pl.BlockSpec(memory...]
    unnamed x27 -> x24, local copies, waits for them, and re-layouts: 2.58 us -> 8.39 us
    ppermute x12, waiting for transfers between devices: 11.6 us -> 10.2 us  [exchange(): lax.ppermute(chunks[step], axis, [(i, i ^ step) for i in range(size)])]
    another operation x1 -> x0, local copies, waits for them, and re-layouts: 1.02 us -> none
    broadcast_in_dim x1 -> x0, other arithmetic: 0.86 us -> none  [body(): return (grad_out, functools.reduce(jnp.add, lags)[None])]
    another operation x1 -> x0, other arithmetic: 0.58 us -> none  [body(): jnp.stack([seq_index, lax.axis_index('section'), lax.axis_index('chan')])]
  transfers between devices with their start and end apart: 13 -> 13, of which waited for: 5 -> 6; matrix products, arithmetic and copies ran while one was open for 3% -> 0% of each run, Pallas kernels for 17% -> 6%
where the time goes in v2:
time: 43.8 us; the launch traced here: 43.5 us
  starting transfers between devices  18.2 us (42%)
  waiting for transfers between devices  10.6 us (24%)
  local copies, waits for them, and re-layouts  8.47 us (19%)
  Pallas kernels  5.47 us (12%)
  between operations  0.75 us (2%)
    ppermute x12, starting transfers between devices, exchange(): lax.ppermute(chunks[step], axis, [(i, i ^ step) for i in range(size)])  16.5 us
    ppermute x12, waiting for transfers between devices, exchange(): lax.ppermute(chunks[step], axis, [(i, i ^ step) for i in range(size)])  10.2 us
    unnamed x24, local copies, waits for them, and re-layouts  8.39 us
    pallas_call x7, Pallas kernels, run(): pl.pallas_call(kernel, out_shape=out_shape, in_specs=[pl.BlockSpec(memory...  5.47 us
    ppermute x1, starting transfers between devices, body(): received = lax.ppermute(gradient, 'section', ring)  1.73 us
  transfers between devices with their start and end apart: 13, of which 6 were waited for; matrix products, arithmetic and copies ran while one was open for 0% of the time, Pallas kernels for 6%

profile of v2, /device:TPU:0, one launch (start us, length us, event | category | flops | bytes accessed | tf_op | source)
XLA Modules:
  0.0 43.5 jit_solution(1112559718971507153)
XLA Ops:
  0.7 1.0 %copy-done.4 = bf16[1,2,128,256]{3,2,1,0:T(8,128)(2,1)S(1)} copy-done((bf16[1,2,128,256]{3,2,1,0:T(8,128)(2,1)S(1)}, bf16[1,2,128,256]{3,2,1,0:T(8,128)(2,1)}, u32[]{:S(2)}) %copy-start.4) | copy-done | bytes 131096
  1.6 0.9 %copy-done.6 = bf16[1,2,128,256]{3,2,1,0:T(8,128)(2,1)S(1)} copy-done((bf16[1,2,128,256]{3,2,1,0:T(8,128)(2,1)S(1)}, bf16[1,2,128,256]{3,2,1,0:T(8,128)(2,1)}, u32[]{:S(2)}) %copy-start.6) | copy-done | bytes 131096
  2.5 0.9 %copy-done.9 = f32[1,128,256]{2,1,0:T(8,128)S(1)} copy-done((f32[1,128,256]{2,1,0:T(8,128)S(1)}, f32[1,128,256]{2,1,0:T(8,128)}, u32[]{:S(2)}) %copy-start.9) | copy-done | bytes 131096
  3.4 0.8 %copy-done.10 = bf16[1,128,256]{2,1,0:T(8,128)(2,1)S(1)} copy-done((bf16[1,128,256]{2,1,0:T(8,128)(2,1)S(1)}, bf16[1,128,256]{2,1,0:T(8,128)(2,1)}, u32[]{:S(2)}) %copy-start.10) | copy-done | bytes 65560
  4.3 0.8 %copy-done.11 = bf16[128,256]{1,0:T(8,128)(2,1)S(1)} copy-done((bf16[128,256]{1,0:T(8,128)(2,1)S(1)}, bf16[128,256]{1,0:T(8,128)(2,1)}, u32[]{:S(2)}) %copy-start.11) | copy-done | bytes 65560
  5.3 3.1 %collective-permute-start = (bf16[128,256]{1,0:T(8,128)(2,1)S(1)}, bf16[128,256]{1,0:T(8,128)(2,1)S(1)}, u32[]{:S(2)}, u32[]{:S(2)}) collective-permute-start(bf16[128,256]{1,0:T(8,128)(2,1)S(1)} %get-tuple-element.26), channel_id=1, source_target_pairs={{0,4},{4,0},{8,12},{12,8},{1,5},{5,1},{9,13},{13,9},{2,6},{6,2},{1... | collective-permute-start | bytes 196616 | tf_op jit(solution)/shard_map/ppermute | solution.py:180
  8.4 2.6 %collective-permute-start.1 = (bf16[128,256]{1,0:T(8,128)(2,1)S(1)}, bf16[128,256]{1,0:T(8,128)(2,1)S(1)}, u32[]{:S(2)}, u32[]{:S(2)}) collective-permute-start(bf16[128,256]{1,0:T(8,128)(2,1)S(1)} %get-tuple-element.27), channel_id=1, source_target_pairs={{0,8},{4,12},{8,0},{12,4},{1,9},{5,13},{9,1},{13,5},{2,10},{6,14},... | collective-permute-start | bytes 196616 | tf_op jit(solution)/shard_map/ppermute | solution.py:180
  11.0 0.9 %copy-done.5 = bf16[1,2,128,256]{3,2,1,0:T(8,128)(2,1)S(1)} copy-done((bf16[1,2,128,256]{3,2,1,0:T(8,128)(2,1)S(1)}, bf16[1,2,128,256]{3,2,1,0:T(8,128)(2,1)}, u32[]{:S(2)}) %copy-start.5) | copy-done | bytes 131096
  11.9 0.9 %copy-done.7 = bf16[1,2,128,256]{3,2,1,0:T(8,128)(2,1)S(1)} copy-done((bf16[1,2,128,256]{3,2,1,0:T(8,128)(2,1)S(1)}, bf16[1,2,128,256]{3,2,1,0:T(8,128)(2,1)}, u32[]{:S(2)}) %copy-start.7) | copy-done | bytes 131096
  12.8 0.9 %copy-done.8 = bf16[1,2,128,256]{3,2,1,0:T(8,128)(2,1)S(1)} copy-done((bf16[1,2,128,256]{3,2,1,0:T(8,128)(2,1)S(1)}, bf16[1,2,128,256]{3,2,1,0:T(8,128)(2,1)}, u32[]{:S(2)}) %copy-start.8) | copy-done | bytes 131096
  13.8 1.0 %collective-permute-start.4 = (bf16[128,256]{1,0:T(8,128)(2,1)S(1)}, bf16[128,256]{1,0:T(8,128)(2,1)S(1)}, u32[]{:S(2)}, u32[]{:S(2)}) collective-permute-start(bf16[128,256]{1,0:T(8,128)(2,1)S(1)} %get-tuple-element.33), channel_id=1, source_target_pairs={{0,4},{4,0},{8,12},{12,8},{1,5},{5,1},{9,13},{13,9},{2,6},{6,2},{1... | collective-permute-start | bytes 196616 | tf_op jit(solution)/shard_map/ppermute | solution.py:180
  14.8 3.5 %collective-permute-start.5 = (bf16[128,256]{1,0:T(8,128)(2,1)S(1)}, bf16[128,256]{1,0:T(8,128)(2,1)S(1)}, u32[]{:S(2)}, u32[]{:S(2)}) collective-permute-start(bf16[128,256]{1,0:T(8,128)(2,1)S(1)} %get-tuple-element.34), channel_id=1, source_target_pairs={{0,8},{4,12},{8,0},{12,4},{1,9},{5,13},{9,1},{13,5},{2,10},{6,14},... | collective-permute-start | bytes 196616 | tf_op jit(solution)/shard_map/ppermute | solution.py:180
  18.4 1.2 %copy-done.1 = bf16[1024,512]{1,0:T(8,128)(2,1)S(1)} copy-done((bf16[1024,512]{1,0:T(8,128)(2,1)S(1)}, bf16[1024,512]{1,0:T(8,128)(2,1)}, u32[]{:S(2)}) %copy-start.1) | copy-done | bytes 1048600
  19.7 1.6 %shard_map.105 = (bf16[256,128]{1,0:T(8,128)(2,1)S(1)}, f32[1024,64]{1,0:T(8,128)S(1)}, f32[2,512,64]{2,1,0:T(8,128)S(1)}) custom-call(f32[1,64]{1,0:T(1,128)S(1)} %constant_dynamic-slice_fusion.gain, bf16[1024,512]{1,0:T(8,128)(2,1)S(1)} %copy-done.1, f32[2,512,64]{2,1,0:T(8,128)S(1)} %copy-done.3, bf16[128,256]{1,0:T(8,128)(2,1)S(1)} %get-tuple-element.25.rest_0_.after, ...), custom_call_target="tpu_custom_call" | custom-call | tf_op jit(solution)/shard_map/pallas_call | solution.py:37
  21.2 1.7 %collective-permute-start.3 = (bf16[256,128]{1,0:T(8,128)(2,1)S(1)}, bf16[256,128]{1,0:T(8,128)(2,1)S(1)}, u32[]{:S(2)}, u32[]{:S(2)}) collective-permute-start(bf16[256,128]{1,0:T(8,128)(2,1)S(1)} %get-tuple-element.29), channel_id=1, source_target_pairs={{0,16},{16,0},{1,17},{17,1},{2,18},{18,2},{3,19},{19,3},{4,20},{20... | collective-permute-start | bytes 196616 | tf_op jit(solution)/shard_map/ppermute | solution.py:222
  23.0 1.5 %collective-permute-done.6.rest_3_ = bf16[128,256]{1,0:T(8,128)(2,1)S(1)} collective-permute-done((bf16[128,256]{1,0:T(8,128)(2,1)S(1)}, bf16[128,256]{1,0:T(8,128)(2,1)S(1)}, u32[]{:S(2)}, u32[]{:S(2)}) %collective-permute-start.6) | collective-permute-done | bytes 65568 | tf_op jit(solution)/shard_map/ppermute | solution.py:180
  25.6 1.5 %shard_map.108 = (bf16[128,128]{1,0:T(8,128)(2,1)S(1)}, bf16[128,128]{1,0:T(8,128)(2,1)S(1)}, bf16[128,128]{1,0:T(8,128)(2,1)S(1)}, bf16[128,128]{1,0:T(8,128)(2,1)S(1)}) custom-call(f32[1,64]{1,0:T(1,128)S(1)} %constant_dynamic-slice_fusion.gain, bf16[1024,512]{1,0:T(8,128)(2,1)S(1)} %copy-done.2, bf16[256,128]{1,0:T(8,128)(2,1)S(1)} %collective-permute-done.3.received, ...), custom_call_target="tpu_custom_call" | custom-call | tf_op jit(solution)/shard_map/pallas_call | solution.py:37
  27.7 3.8 %collective-permute-start.8 = (bf16[128,128]{1,0:T(8,128)(2,1)S(1)}, bf16[128,128]{1,0:T(8,128)(2,1)S(1)}, u32[]{:S(2)}, u32[]{:S(2)}) collective-permute-start(bf16[128,128]{1,0:T(8,128)(2,1)S(1)} %get-tuple-element.41), channel_id=1, source_target_pairs={{0,8},{4,12},{8,0},{12,4},{1,9},{5,13},{9,1},{13,5},{2,10},{6,14},... | collective-permute-start | bytes 98312 | tf_op jit(solution)/shard_map/ppermute | solution.py:180
  31.6 2.2 %collective-permute-done.8.rest_2_ = bf16[128,128]{1,0:T(8,128)(2,1)S(1)} collective-permute-done((bf16[128,128]{1,0:T(8,128)(2,1)S(1)}, bf16[128,128]{1,0:T(8,128)(2,1)S(1)}, u32[]{:S(2)}, u32[]{:S(2)}) %collective-permute-start.8) | collective-permute-done | bytes 32800 | tf_op jit(solution)/shard_map/ppermute | solution.py:180
  33.8 3.5 %collective-permute-done.9.rest_3_ = bf16[128,128]{1,0:T(8,128)(2,1)S(1)} collective-permute-done((bf16[128,128]{1,0:T(8,128)(2,1)S(1)}, bf16[128,128]{1,0:T(8,128)(2,1)S(1)}, u32[]{:S(2)}, u32[]{:S(2)}) %collective-permute-start.9) | collective-permute-done | bytes 32800 | tf_op jit(solution)/shard_map/ppermute | solution.py:180
  37.3 0.7 %shard_map.109 = (bf16[1,128,256]{2,1,0:T(8,128)(2,1)}, f32[64,128]{1,0:T(8,128)S(1)}, f32[64,128]{1,0:T(8,128)S(1)}, f32[64,128]{1,0:T(8,128)S(1)}, f32[64,128]{1,0:T(8,128)S(1)}) custom-call(bf16[128,128]{1,0:T(8,128)(2,1)S(1)} %get-tuple-element.39.rest_0_, bf16[128,128]{1,0:T(8,128)(2,1)S(1)} %collective-permute-done.7.rest_1_, ...), custom_call_target="tpu_custom_call" | custom-call | tf_op jit(solution)/shard_map/pallas_call | solution.py:37
  38.0 1.5 %collective-permute-start.11 = (f32[64,128]{1,0:T(8,128)S(1)}, f32[64,128]{1,0:T(8,128)S(1)}, u32[]{:S(2)}, u32[]{:S(2)}) collective-permute-start(f32[64,128]{1,0:T(8,128)S(1)} %get-tuple-element.46), channel_id=1, source_target_pairs={{0,2},{1,3},{2,0},{3,1},{4,6},{5,7},{6,4},{7,5},{8,10},{9,11},{10,... | collective-permute-start | bytes 98312 | tf_op jit(solution)/shard_map/ppermute | solution.py:180
  39.9 2.1 %collective-permute-done.11.refs_2_ = f32[64,128]{1,0:T(8,128)S(1)} collective-permute-done((f32[64,128]{1,0:T(8,128)S(1)}, f32[64,128]{1,0:T(8,128)S(1)}, u32[]{:S(2)}, u32[]{:S(2)}) %collective-permute-start.11) | collective-permute-done | bytes 32800 | tf_op jit(solution)/shard_map/ppermute | solution.py:180
  41.9 0.9 %collective-permute-done.12.refs_3_ = f32[64,128]{1,0:T(8,128)S(1)} collective-permute-done((f32[64,128]{1,0:T(8,128)S(1)}, f32[64,128]{1,0:T(8,128)S(1)}, u32[]{:S(2)}, u32[]{:S(2)}) %collective-permute-start.12) | collective-permute-done | bytes 32800 | tf_op jit(solution)/shard_map/ppermute | solution.py:180
  (34 shorter events, 3.2 us)
Async XLA Ops:
  0.6 17.7 %copy-start = (f32[1,256]{1,0:T(1,128)S(1)}, f32[1,256]{1,0:T(1,128)}, u32[]{:S(2)}) copy-start(f32[1,256]{1,0:T(1,128)} %param.15) | copy-start | bytes 3076
  0.6 17.8 %copy-start.3 = (f32[2,512,64]{2,1,0:T(8,128)S(1)}, f32[2,512,64]{2,1,0:T(8,128)}, u32[]{:S(2)}) copy-start(f32[2,512,64]{2,1,0:T(8,128)} %constant.16.clone.turns) | copy-start | bytes 786436
  0.7 1.0 %copy-start.4 = (bf16[1,2,128,256]{3,2,1,0:T(8,128)(2,1)S(1)}, bf16[1,2,128,256]{3,2,1,0:T(8,128)(2,1)}, u32[]{:S(2)}) copy-start(bf16[1,2,128,256]{3,2,1,0:T(8,128)(2,1)} %post.3) | copy-start | bytes 393220
  1.6 0.9 %copy-start.6 = (bf16[1,2,128,256]{3,2,1,0:T(8,128)(2,1)S(1)}, bf16[1,2,128,256]{3,2,1,0:T(8,128)(2,1)}, u32[]{:S(2)}) copy-start(bf16[1,2,128,256]{3,2,1,0:T(8,128)(2,1)} %pre.3) | copy-start | bytes 393220
  2.5 0.9 %copy-start.9 = (f32[1,128,256]{2,1,0:T(8,128)S(1)}, f32[1,128,256]{2,1,0:T(8,128)}, u32[]{:S(2)}) copy-start(f32[1,128,256]{2,1,0:T(8,128)} %filters.1) | copy-start | bytes 393220
  3.4 0.8 %copy-start.10 = (bf16[1,128,256]{2,1,0:T(8,128)(2,1)S(1)}, bf16[1,128,256]{2,1,0:T(8,128)(2,1)}, u32[]{:S(2)}) copy-start(bf16[1,128,256]{2,1,0:T(8,128)(2,1)} %held.1) | copy-start | bytes 196612
  5.3 13.1 %collective-permute-start = (bf16[128,256]{1,0:T(8,128)(2,1)S(1)}, bf16[128,256]{1,0:T(8,128)(2,1)S(1)}, u32[]{:S(2)}, u32[]{:S(2)}) collective-permute-start(bf16[128,256]{1,0:T(8,128)(2,1)S(1)} %get-tuple-element.26), channel_id=1, source_target_pairs={{0,4},{4,0},{8,12},{12,8},{1,5},{5,1},{9,13},{13,9},{2,6},{6,2},{1... | collective-permute-start | bytes 196616 | tf_op jit(solution)/shard_map/ppermute | solution.py:180
  8.4 10.0 %collective-permute-start.1 = (bf16[128,256]{1,0:T(8,128)(2,1)S(1)}, bf16[128,256]{1,0:T(8,128)(2,1)S(1)}, u32[]{:S(2)}, u32[]{:S(2)}) collective-permute-start(bf16[128,256]{1,0:T(8,128)(2,1)S(1)} %get-tuple-element.27), channel_id=1, source_target_pairs={{0,8},{4,12},{8,0},{12,4},{1,9},{5,13},{9,1},{13,5},{2,10},{6,14},... | collective-permute-start | bytes 196616 | tf_op jit(solution)/shard_map/ppermute | solution.py:180
  11.0 7.5 %collective-permute-start.2 = (bf16[128,256]{1,0:T(8,128)(2,1)S(1)}, bf16[128,256]{1,0:T(8,128)(2,1)S(1)}, u32[]{:S(2)}, u32[]{:S(2)}) collective-permute-start(bf16[128,256]{1,0:T(8,128)(2,1)S(1)} %get-tuple-element.28), channel_id=1, source_target_pairs={{0,12},{4,8},{8,4},{12,0},{1,13},{5,9},{9,5},{13,1},{2,14},{6,10},... | collective-permute-start | bytes 196616 | tf_op jit(solution)/shard_map/ppermute | solution.py:180
  11.0 0.9 %copy-start.5 = (bf16[1,2,128,256]{3,2,1,0:T(8,128)(2,1)S(1)}, bf16[1,2,128,256]{3,2,1,0:T(8,128)(2,1)}, u32[]{:S(2)}) copy-start(bf16[1,2,128,256]{3,2,1,0:T(8,128)(2,1)} %post.3) | copy-start | bytes 393220
  11.9 0.9 %copy-start.7 = (bf16[1,2,128,256]{3,2,1,0:T(8,128)(2,1)S(1)}, bf16[1,2,128,256]{3,2,1,0:T(8,128)(2,1)}, u32[]{:S(2)}) copy-start(bf16[1,2,128,256]{3,2,1,0:T(8,128)(2,1)} %pre.3) | copy-start | bytes 393220
  12.8 0.9 %copy-start.8 = (bf16[1,2,128,256]{3,2,1,0:T(8,128)(2,1)S(1)}, bf16[1,2,128,256]{3,2,1,0:T(8,128)(2,1)}, u32[]{:S(2)}) copy-start(bf16[1,2,128,256]{3,2,1,0:T(8,128)(2,1)} %saved.1) | copy-start | bytes 393220
  13.8 9.1 %collective-permute-start.4 = (bf16[128,256]{1,0:T(8,128)(2,1)S(1)}, bf16[128,256]{1,0:T(8,128)(2,1)S(1)}, u32[]{:S(2)}, u32[]{:S(2)}) collective-permute-start(bf16[128,256]{1,0:T(8,128)(2,1)S(1)} %get-tuple-element.33), channel_id=1, source_target_pairs={{0,4},{4,0},{8,12},{12,8},{1,5},{5,1},{9,13},{13,9},{2,6},{6,2},{1... | collective-permute-start | bytes 196616 | tf_op jit(solution)/shard_map/ppermute | solution.py:180
  14.8 8.2 %collective-permute-start.5 = (bf16[128,256]{1,0:T(8,128)(2,1)S(1)}, bf16[128,256]{1,0:T(8,128)(2,1)S(1)}, u32[]{:S(2)}, u32[]{:S(2)}) collective-permute-start(bf16[128,256]{1,0:T(8,128)(2,1)S(1)} %get-tuple-element.34), channel_id=1, source_target_pairs={{0,8},{4,12},{8,0},{12,4},{1,9},{5,13},{9,1},{13,5},{2,10},{6,14},... | collective-permute-start | bytes 196616 | tf_op jit(solution)/shard_map/ppermute | solution.py:180
  18.4 6.1 %collective-permute-start.6 = (bf16[128,256]{1,0:T(8,128)(2,1)S(1)}, bf16[128,256]{1,0:T(8,128)(2,1)S(1)}, u32[]{:S(2)}, u32[]{:S(2)}) collective-permute-start(bf16[128,256]{1,0:T(8,128)(2,1)S(1)} %get-tuple-element.35), channel_id=1, source_target_pairs={{0,12},{4,8},{8,4},{12,0},{1,13},{5,9},{9,5},{13,1},{2,14},{6,10},... | collective-permute-start | bytes 196616 | tf_op jit(solution)/shard_map/ppermute | solution.py:180
  18.4 1.2 %copy-start.1 = (bf16[1024,512]{1,0:T(8,128)(2,1)S(1)}, bf16[1024,512]{1,0:T(8,128)(2,1)}, u32[]{:S(2)}) copy-start(bf16[1024,512]{1,0:T(8,128)(2,1)} %constant.15.clone.table) | copy-start | bytes 3145732
  19.7 4.8 %copy-start.2 = (bf16[1024,512]{1,0:T(8,128)(2,1)S(1)}, bf16[1024,512]{1,0:T(8,128)(2,1)}, u32[]{:S(2)}) copy-start(bf16[1024,512]{1,0:T(8,128)(2,1)} %constant.15.clone.table) | copy-start | bytes 3145732
  21.2 4.3 %collective-permute-start.3 = (bf16[256,128]{1,0:T(8,128)(2,1)S(1)}, bf16[256,128]{1,0:T(8,128)(2,1)S(1)}, u32[]{:S(2)}, u32[]{:S(2)}) collective-permute-start(bf16[256,128]{1,0:T(8,128)(2,1)S(1)} %get-tuple-element.29), channel_id=1, source_target_pairs={{0,16},{16,0},{1,17},{17,1},{2,18},{18,2},{3,19},{19,3},{4,20},{20... | collective-permute-start | bytes 196616 | tf_op jit(solution)/shard_map/ppermute | solution.py:222
  27.1 4.5 %collective-permute-start.7 = (bf16[128,128]{1,0:T(8,128)(2,1)S(1)}, bf16[128,128]{1,0:T(8,128)(2,1)S(1)}, u32[]{:S(2)}, u32[]{:S(2)}) collective-permute-start(bf16[128,128]{1,0:T(8,128)(2,1)S(1)} %get-tuple-element.40), channel_id=1, source_target_pairs={{0,4},{4,0},{8,12},{12,8},{1,5},{5,1},{9,13},{13,9},{2,6},{6,2},{1... | collective-permute-start | bytes 98312 | tf_op jit(solution)/shard_map/ppermute | solution.py:180
  27.7 6.1 %collective-permute-start.8 = (bf16[128,128]{1,0:T(8,128)(2,1)S(1)}, bf16[128,128]{1,0:T(8,128)(2,1)S(1)}, u32[]{:S(2)}, u32[]{:S(2)}) collective-permute-start(bf16[128,128]{1,0:T(8,128)(2,1)S(1)} %get-tuple-element.41), channel_id=1, source_target_pairs={{0,8},{4,12},{8,0},{12,4},{1,9},{5,13},{9,1},{13,5},{2,10},{6,14},... | collective-permute-start | bytes 98312 | tf_op jit(solution)/shard_map/ppermute | solution.py:180
  31.5 5.7 %collective-permute-start.9 = (bf16[128,128]{1,0:T(8,128)(2,1)S(1)}, bf16[128,128]{1,0:T(8,128)(2,1)S(1)}, u32[]{:S(2)}, u32[]{:S(2)}) collective-permute-start(bf16[128,128]{1,0:T(8,128)(2,1)S(1)} %get-tuple-element.42), channel_id=1, source_target_pairs={{0,12},{4,8},{8,4},{12,0},{1,13},{5,9},{9,5},{13,1},{2,14},{6,10},... | collective-permute-start | bytes 98312 | tf_op jit(solution)/shard_map/ppermute | solution.py:180
  38.0 1.9 %collective-permute-start.10 = (f32[64,128]{1,0:T(8,128)S(1)}, f32[64,128]{1,0:T(8,128)S(1)}, u32[]{:S(2)}, u32[]{:S(2)}) collective-permute-start(f32[64,128]{1,0:T(8,128)S(1)} %get-tuple-element.45), channel_id=1, source_target_pairs={{0,1},{1,0},{2,3},{3,2},{4,5},{5,4},{6,7},{7,6},{8,9},{9,8},{10,11... | collective-permute-start | bytes 98312 | tf_op jit(solution)/shard_map/ppermute | solution.py:180
  38.0 3.9 %collective-permute-start.11 = (f32[64,128]{1,0:T(8,128)S(1)}, f32[64,128]{1,0:T(8,128)S(1)}, u32[]{:S(2)}, u32[]{:S(2)}) collective-permute-start(f32[64,128]{1,0:T(8,128)S(1)} %get-tuple-element.46), channel_id=1, source_target_pairs={{0,2},{1,3},{2,0},{3,1},{4,6},{5,7},{6,4},{7,5},{8,10},{9,11},{10,... | collective-permute-start | bytes 98312 | tf_op jit(solution)/shard_map/ppermute | solution.py:180
  39.5 3.3 %collective-permute-start.12 = (f32[64,128]{1,0:T(8,128)S(1)}, f32[64,128]{1,0:T(8,128)S(1)}, u32[]{:S(2)}, u32[]{:S(2)}) collective-permute-start(f32[64,128]{1,0:T(8,128)S(1)} %get-tuple-element.47), channel_id=1, source_target_pairs={{0,3},{1,2},{2,1},{3,0},{4,7},{5,6},{6,5},{7,4},{8,11},{9,10},{10,... | collective-permute-start | bytes 98312 | tf_op jit(solution)/shard_map/ppermute | solution.py:180
  (1 other events, 0.8 us)

commit v3 on v2

--- a/solution.py
+++ b/solution.py
@@ -31,18 +31,40 @@
     return total
 
 
-def call(kernel, out_shape, scratch=()):
+def call(kernel, out_shape, scratch=(), spaces=None, copies=0):
     def run(*arrays):
         held = size_of([*arrays, *out_shape, *scratch])
+        if spaces:
+            arrays = [
+                pltpu.with_memory_space_constraint(array, space) if space == pltpu.HBM else array
+                for array, space in zip(arrays, spaces)
+            ]
+        scratch_shapes = [pltpu.VMEM(shape.shape, shape.dtype) for shape in scratch]
+        if copies:
+            scratch_shapes.append(pltpu.SemaphoreType.DMA((copies,)))
         return pl.pallas_call(
             kernel,
             out_shape=out_shape,
-            in_specs=[pl.BlockSpec(memory_space=pltpu.VMEM)] * len(arrays),
-            scratch_shapes=[pltpu.VMEM(shape.shape, shape.dtype) for shape in scratch],
+            in_specs=[
+                pl.BlockSpec(memory_space=space)
+                for space in spaces or [pltpu.VMEM] * len(arrays)
+            ],
+            scratch_shapes=scratch_shapes,
             compiler_params=pltpu.CompilerParams(vmem_limit_bytes=2 * held + (4 << 20)),
         )(*arrays)
 
     return run
+
+
+def fetch(sources, places, semaphores):
+    copies = [
+        pltpu.make_async_copy(source, place, semaphores.at[at])
+        for at, (source, place) in enumerate(zip(sources, places))
+    ]
+    for copy in copies:
+        copy.start()
+    for copy in copies:
+        copy.wait()
 
 
 def dot(left, right):
@@ -61,18 +83,31 @@
 
 
 def pack_first(post, held, loss, pre, filters, *rest):
-    outs, stage = rest[:-1], rest[-1]
-    held_value = held[0]
-    gated = (post[0, 0].astype(F32) * held_value.astype(F32)).astype(BF16)
-    kept = jnp.where(lax.axis_index("section") == 0, loss[...], held_value)
-    pack([gated, filters[0].astype(BF16), kept, pre[0, 0]], stage, outs)
-
-
-def pack_second(after, saved, pre, post, *rest):
+    *outs, stage, gates, lags, semaphores = rest
+    sources = [post.at[0, 0], held.at[0], loss, pre.at[0, 0], filters.at[0]]
+    fetch(sources, [gates.at[at] for at in range(4)] + [lags], semaphores)
+    gated = (gates[0].astype(F32) * gates[1].astype(F32)).astype(BF16)
+    kept = jnp.where(lax.axis_index("section") == 0, gates[2], gates[1])
+    pack([gated, lags[...].astype(BF16), kept, gates[3]], stage, outs)
+
+
+def pack_second(after, saved, pre, post, gains, table, turns, *rest):
     del after
-    outs, stage = rest[:-1], rest[-1]
-    mixed = (saved[0].astype(F32) * pre[0].astype(F32)).astype(BF16)
-    pack([mixed[0], mixed[1], post[0, 1], pre[0, 1]], stage, outs)
+    *outs, gain, table_out, turns_out, stage, gates, all_gains, semaphores = rest
+    sources = [saved.at[0, 0], saved.at[0, 1], pre.at[0, 0], pre.at[0, 1], post.at[0, 1]]
+    fetch(
+        sources + [gains, table, turns],
+        [gates.at[at] for at in range(5)] + [all_gains, table_out, turns_out],
+        semaphores,
+    )
+    mixed = (gates[0:2].astype(F32) * gates[2:4].astype(F32)).astype(BF16)
+    pack([mixed[0], mixed[1], gates[4], gates[3]], stage, outs)
+    unit = gain.shape[1]
+    for block in range(len(outs)):
+
+        @pl.when(lax.axis_index("seq") == block)
+        def _():
+            gain[...] = all_gains[:, block * unit : (block + 1) * unit]
 
 
 def gather_positions(chunks, held):
@@ -190,22 +225,33 @@
     _, tick_count, rows, width = saved_input.shape
     length = rows * seq_count
     unit = width // seq_count
-    seq_index = lax.axis_index("seq")
     table = jnp.asarray(table)
     turns = jnp.asarray(np.array(np.broadcast_to(turns[:, :, None], (2, length, unit))))
-    gain = lax.dynamic_slice(skip_gain, (0, seq_index * unit), (1, unit))
     struct = jax.ShapeDtypeStruct
     chunk = struct((rows, 4 * unit), BF16)
     stage = struct((seq_count, rows, 4 * unit), BF16)
     held_rows = struct((length, 4 * unit), BF16)
     spectrum = struct((2, length, unit), F32)
 
-    first = call(pack_first, [chunk] * seq_count, [stage])(
-        post_gate, grad_held, loss_grad, pre_gate, filters
-    )
-    second = call(pack_second, [chunk] * seq_count, [stage])(
-        first[0], saved_input, pre_gate, post_gate
-    )
+    first = call(
+        pack_first,
+        [chunk] * seq_count,
+        [stage, struct((4, rows, width), BF16), struct((rows, width), F32)],
+        [pltpu.HBM] * 5,
+        5,
+    )(post_gate, grad_held, loss_grad, pre_gate, filters)
+    *second, gain, table, turns = call(
+        pack_second,
+        [chunk] * seq_count
+        + [
+            struct((1, unit), F32),
+            struct(table.shape, BF16),
+            struct(turns.shape, F32),
+        ],
+        [stage, struct((5, rows, width), BF16), struct((1, width), F32)],
+        [pl.ANY] + [pltpu.HBM] * 6,
+        8,
+    )(first[0], saved_input, pre_gate, post_gate, skip_gain, table, turns)
     first = exchange(first, "seq")
     second = exchange(second, "seq")
 

time: 43.8 us -> 37.9 us (0.87)
  local copies, waits for them, and re-layouts: 8.47 us -> 0 us
  Pallas kernels: 5.47 us -> 8.14 us
    unnamed x24 -> x0, local copies, waits for them, and re-layouts: 8.39 us -> none
    pallas_call x7, Pallas kernels: 5.47 us -> 8.14 us  [run(): pl.pallas_call(kernel, out_shape=out_shape, in_specs=[pl.BlockSpec(memory...]
    ppermute x12, waiting for transfers between devices: 10.2 us -> 10.8 us  [exchange(): lax.ppermute(chunks[step], axis, [(i, i ^ step) for i in range(size)])]
  transfers between devices with their start and end apart: 13 -> 13, of which waited for: 6 -> 7; matrix products, arithmetic and copies ran while one was open for 0% -> 0% of each run, Pallas kernels for 6% -> 11%
where the time goes in v3:
time: 37.9 us; the launch traced here: 37.8 us
  starting transfers between devices  18.1 us (48%)
  waiting for transfers between devices  10.8 us (28%)
  Pallas kernels  8.14 us (21%)
  between operations  0.69 us (2%)
    ppermute x12, starting transfers between devices, exchange(): lax.ppermute(chunks[step], axis, [(i, i ^ step) for i in range(size)])  16.5 us
    ppermute x12, waiting for transfers between devices, exchange(): lax.ppermute(chunks[step], axis, [(i, i ^ step) for i in range(size)])  10.8 us
    pallas_call x7, Pallas kernels, run(): pl.pallas_call(kernel, out_shape=out_shape, in_specs=[pl.BlockSpec(memory...  8.14 us
    ppermute x1, starting transfers between devices, body(): received = lax.ppermute(gradient, 'section', ring)  1.6 us
  transfers between devices with their start and end apart: 13, of which 7 were waited for; matrix products, arithmetic and copies ran while one was open for 0% of the time, Pallas kernels for 11%

profile of v3, /device:TPU:0, one launch (start us, length us, event | category | flops | bytes accessed | tf_op | source)
XLA Modules:
  0.0 37.8 jit_solution(10044426021214357328)
XLA Ops:
  0.6 1.2 %shard_map.104 = (bf16[128,256]{1,0:T(8,128)(2,1)S(1)}, bf16[128,256]{1,0:T(8,128)(2,1)S(1)}, bf16[128,256]{1,0:T(8,128)(2,1)S(1)}, bf16[128,256]{1,0:T(8,128)(2,1)S(1)}) custom-call(bf16[1,2,128,256]{3,2,1,0:T(8,128)(2,1)} %post.3, bf16[1,128,256]{2,1,0:T(8,128)(2,1)} %held.1, bf16[128,256]{1,0:T(8,128)(2,1)} %loss.1, bf16[1,2,128,256]{3,2,1,0:T(8,128)(2,1)} %pre.3, ...), custom_call_target="tpu_custom_call" | custom-call | tf_op jit(solution)/shard_map/pallas_call | solution.py:45
  1.9 3.1 %collective-permute-start = (bf16[128,256]{1,0:T(8,128)(2,1)S(1)}, bf16[128,256]{1,0:T(8,128)(2,1)S(1)}, u32[]{:S(2)}, u32[]{:S(2)}) collective-permute-start(bf16[128,256]{1,0:T(8,128)(2,1)S(1)} %get-tuple-element.32), channel_id=1, source_target_pairs={{0,4},{4,0},{8,12},{12,8},{1,5},{5,1},{9,13},{13,9},{2,6},{6,2},{1... | collective-permute-start | bytes 196616 | tf_op jit(solution)/shard_map/ppermute | solution.py:215
  5.0 2.6 %collective-permute-start.1 = (bf16[128,256]{1,0:T(8,128)(2,1)S(1)}, bf16[128,256]{1,0:T(8,128)(2,1)S(1)}, u32[]{:S(2)}, u32[]{:S(2)}) collective-permute-start(bf16[128,256]{1,0:T(8,128)(2,1)S(1)} %get-tuple-element.33), channel_id=1, source_target_pairs={{0,8},{4,12},{8,0},{12,4},{1,9},{5,13},{9,1},{13,5},{2,10},{6,14},... | collective-permute-start | bytes 196616 | tf_op jit(solution)/shard_map/ppermute | solution.py:215
  7.6 1.8 %shard_map.105 = (bf16[128,256]{1,0:T(8,128)(2,1)S(1)}, bf16[128,256]{1,0:T(8,128)(2,1)S(1)}, bf16[128,256]{1,0:T(8,128)(2,1)S(1)}, bf16[128,256]{1,0:T(8,128)(2...) custom-call(bf16[128,256]{1,0:T(8,128)(2,1)S(1)} %get-tuple-element.28.after.rest_0_, ...), custom_call_target="tpu_custom_call" | custom-call | tf_op jit(solution)/shard_map/pallas_call | solution.py:45
  9.4 1.0 %collective-permute-start.4 = (bf16[128,256]{1,0:T(8,128)(2,1)S(1)}, bf16[128,256]{1,0:T(8,128)(2,1)S(1)}, u32[]{:S(2)}, u32[]{:S(2)}) collective-permute-start(bf16[128,256]{1,0:T(8,128)(2,1)S(1)} %get-tuple-element.39), channel_id=1, source_target_pairs={{0,4},{4,0},{8,12},{12,8},{1,5},{5,1},{9,13},{13,9},{2,6},{6,2},{1... | collective-permute-start | bytes 196616 | tf_op jit(solution)/shard_map/ppermute | solution.py:215
  10.4 3.5 %collective-permute-start.5 = (bf16[128,256]{1,0:T(8,128)(2,1)S(1)}, bf16[128,256]{1,0:T(8,128)(2,1)S(1)}, u32[]{:S(2)}, u32[]{:S(2)}) collective-permute-start(bf16[128,256]{1,0:T(8,128)(2,1)S(1)} %get-tuple-element.40), channel_id=1, source_target_pairs={{0,8},{4,12},{8,0},{12,4},{1,9},{5,13},{9,1},{13,5},{2,10},{6,14},... | collective-permute-start | bytes 196616 | tf_op jit(solution)/shard_map/ppermute | solution.py:215
  13.9 0.2 collective-permute-done.2.rest_3_
  14.1 1.6 %shard_map.106 = (bf16[256,128]{1,0:T(8,128)(2,1)S(1)}, f32[1024,64]{1,0:T(8,128)S(1)}, f32[2,512,64]{2,1,0:T(8,128)S(1)}) custom-call(f32[1,64]{1,0:T(1,128)S(1)} %get-tuple-element.29.gain, bf16[1024,512]{1,0:T(8,128)(2,1)S(1)} %get-tuple-element.30.table, f32[2,512,64]{2,1,0:T(8,128)S(1)} %get-tuple-element.31.turns, ...), custom_call_target="tpu_custom_call" | custom-call | tf_op jit(solution)/shard_map/pallas_call | solution.py:45
  15.7 1.6 %collective-permute-start.3 = (bf16[256,128]{1,0:T(8,128)(2,1)S(1)}, bf16[256,128]{1,0:T(8,128)(2,1)S(1)}, u32[]{:S(2)}, u32[]{:S(2)}) collective-permute-start(bf16[256,128]{1,0:T(8,128)(2,1)S(1)} %get-tuple-element.35), channel_id=1, source_target_pairs={{0,16},{16,0},{1,17},{17,1},{2,18},{18,2},{3,19},{19,3},{4,20},{20... | collective-permute-start | bytes 196616 | tf_op jit(solution)/shard_map/ppermute | solution.py:268
  17.3 0.6 %collective-permute-done.5.rest_2_ = bf16[128,256]{1,0:T(8,128)(2,1)S(1)} collective-permute-done((bf16[128,256]{1,0:T(8,128)(2,1)S(1)}, bf16[128,256]{1,0:T(8,128)(2,1)S(1)}, u32[]{:S(2)}, u32[]{:S(2)}) %collective-permute-start.5) | collective-permute-done | bytes 65568 | tf_op jit(solution)/shard_map/ppermute | solution.py:215
  18.0 2.0 %collective-permute-done.6.rest_3_ = bf16[128,256]{1,0:T(8,128)(2,1)S(1)} collective-permute-done((bf16[128,256]{1,0:T(8,128)(2,1)S(1)}, bf16[128,256]{1,0:T(8,128)(2,1)S(1)}, u32[]{:S(2)}, u32[]{:S(2)}) %collective-permute-start.6) | collective-permute-done | bytes 65568 | tf_op jit(solution)/shard_map/ppermute | solution.py:215
  20.0 0.6 %shard_map.107 = (bf16[512,128]{1,0:T(8,128)(2,1)S(1)}, f32[2,512,64]{2,1,0:T(8,128)S(1)}, f32[2,512,64]{2,1,0:T(8,128)S(1)}) custom-call(bf16[1024,512]{1,0:T(8,128)(2,1)S(1)} %get-tuple-element.30.table, f32[2,512,64]{2,1,0:T(8,128)S(1)} %get-tuple-element.31.turns, f32[1024,64]{1,0:T(8,128)S(1)} %get-tuple-element.37.gated_spec, ...), custom_call_target="tpu_custom_call" | custom-call | tf_op jit(solution)/shard_map/pallas_call | solution.py:45
  20.6 1.5 %shard_map.108 = (bf16[128,128]{1,0:T(8,128)(2,1)S(1)}, bf16[128,128]{1,0:T(8,128)(2,1)S(1)}, bf16[128,128]{1,0:T(8,128)(2,1)S(1)}, bf16[128,128]{1,0:T(8,128)(2,1)S(1)}) custom-call(f32[1,64]{1,0:T(1,128)S(1)} %get-tuple-element.29.gain, bf16[1024,512]{1,0:T(8,128)(2,1)S(1)} %get-tuple-element.30.table, ...), custom_call_target="tpu_custom_call" | custom-call | tf_op jit(solution)/shard_map/pallas_call | solution.py:45
  22.1 0.1 collective-permute-start.7
  22.2 3.6 %collective-permute-start.8 = (bf16[128,128]{1,0:T(8,128)(2,1)S(1)}, bf16[128,128]{1,0:T(8,128)(2,1)S(1)}, u32[]{:S(2)}, u32[]{:S(2)}) collective-permute-start(bf16[128,128]{1,0:T(8,128)(2,1)S(1)} %get-tuple-element.47), channel_id=1, source_target_pairs={{0,8},{4,12},{8,0},{12,4},{1,9},{5,13},{9,1},{13,5},{2,10},{6,14},... | collective-permute-start | bytes 98312 | tf_op jit(solution)/shard_map/ppermute | solution.py:215
  25.8 0.8 %collective-permute-start.9 = (bf16[128,128]{1,0:T(8,128)(2,1)S(1)}, bf16[128,128]{1,0:T(8,128)(2,1)S(1)}, u32[]{:S(2)}, u32[]{:S(2)}) collective-permute-start(bf16[128,128]{1,0:T(8,128)(2,1)S(1)} %get-tuple-element.48), channel_id=1, source_target_pairs={{0,12},{4,8},{8,4},{12,0},{1,13},{5,9},{9,5},{13,1},{2,14},{6,10},... | collective-permute-start | bytes 98312 | tf_op jit(solution)/shard_map/ppermute | solution.py:215
  26.6 1.3 %collective-permute-done.8.rest_2_ = bf16[128,128]{1,0:T(8,128)(2,1)S(1)} collective-permute-done((bf16[128,128]{1,0:T(8,128)(2,1)S(1)}, bf16[128,128]{1,0:T(8,128)(2,1)S(1)}, u32[]{:S(2)}, u32[]{:S(2)}) %collective-permute-start.8) | collective-permute-done | bytes 32800 | tf_op jit(solution)/shard_map/ppermute | solution.py:215
  27.8 3.7 %collective-permute-done.9.rest_3_ = bf16[128,128]{1,0:T(8,128)(2,1)S(1)} collective-permute-done((bf16[128,128]{1,0:T(8,128)(2,1)S(1)}, bf16[128,128]{1,0:T(8,128)(2,1)S(1)}, u32[]{:S(2)}, u32[]{:S(2)}) %collective-permute-start.9) | collective-permute-done | bytes 32800 | tf_op jit(solution)/shard_map/ppermute | solution.py:215
  31.5 0.7 %shard_map.109 = (bf16[1,128,256]{2,1,0:T(8,128)(2,1)}, f32[64,128]{1,0:T(8,128)S(1)}, f32[64,128]{1,0:T(8,128)S(1)}, f32[64,128]{1,0:T(8,128)S(1)}, f32[64,128]{1,0:T(8,128)S(1)}) custom-call(bf16[128,128]{1,0:T(8,128)(2,1)S(1)} %get-tuple-element.45.rest_0_, bf16[128,128]{1,0:T(8,128)(2,1)S(1)} %collective-permute-done.7.rest_1_, ...), custom_call_target="tpu_custom_call" | custom-call | tf_op jit(solution)/shard_map/pallas_call | solution.py:45
  32.3 1.5 %collective-permute-start.11 = (f32[64,128]{1,0:T(8,128)S(1)}, f32[64,128]{1,0:T(8,128)S(1)}, u32[]{:S(2)}, u32[]{:S(2)}) collective-permute-start(f32[64,128]{1,0:T(8,128)S(1)} %get-tuple-element.52), channel_id=1, source_target_pairs={{0,2},{1,3},{2,0},{3,1},{4,6},{5,7},{6,4},{7,5},{8,10},{9,11},{10,... | collective-permute-start | bytes 98312 | tf_op jit(solution)/shard_map/ppermute | solution.py:215
  33.8 0.3 collective-permute-start.12
  34.1 2.1 %collective-permute-done.11.refs_2_ = f32[64,128]{1,0:T(8,128)S(1)} collective-permute-done((f32[64,128]{1,0:T(8,128)S(1)}, f32[64,128]{1,0:T(8,128)S(1)}, u32[]{:S(2)}, u32[]{:S(2)}) %collective-permute-start.11) | collective-permute-done | bytes 32800 | tf_op jit(solution)/shard_map/ppermute | solution.py:215
  36.2 0.9 %collective-permute-done.12.refs_3_ = f32[64,128]{1,0:T(8,128)S(1)} collective-permute-done((f32[64,128]{1,0:T(8,128)S(1)}, f32[64,128]{1,0:T(8,128)S(1)}, u32[]{:S(2)}, u32[]{:S(2)}) %collective-permute-start.12) | collective-permute-done | bytes 32800 | tf_op jit(solution)/shard_map/ppermute | solution.py:215
  37.1 0.6 %shard_map.110 = f32[64,128]{1,0:T(8,128)} custom-call(f32[64,128]{1,0:T(8,128)S(1)} %get-tuple-element.50.refs_0_, f32[64,128]{1,0:T(8,128)S(1)} %collective-permute-done.10.refs_1_, f32[64,128]{1,0:T(8,128)S(1)} %collective-permute-done.11.refs_2_, f32[64,128]{1,0:T(8,128)S(1)} %collective-permute-done.12.refs_3_), custom_call_target="tpu_custom_call" | custom-call | tf_op jit(solution)/shard_map/pallas_call | solution.py:45
  (9 shorter events, 0.0 us)
Async XLA Ops:
  1.9 12.0 %collective-permute-start = (bf16[128,256]{1,0:T(8,128)(2,1)S(1)}, bf16[128,256]{1,0:T(8,128)(2,1)S(1)}, u32[]{:S(2)}, u32[]{:S(2)}) collective-permute-start(bf16[128,256]{1,0:T(8,128)(2,1)S(1)} %get-tuple-element.32), channel_id=1, source_target_pairs={{0,4},{4,0},{8,12},{12,8},{1,5},{5,1},{9,13},{13,9},{2,6},{6,2},{1... | collective-permute-start | bytes 196616 | tf_op jit(solution)/shard_map/ppermute | solution.py:215
  5.0 8.9 %collective-permute-start.1 = (bf16[128,256]{1,0:T(8,128)(2,1)S(1)}, bf16[128,256]{1,0:T(8,128)(2,1)S(1)}, u32[]{:S(2)}, u32[]{:S(2)}) collective-permute-start(bf16[128,256]{1,0:T(8,128)(2,1)S(1)} %get-tuple-element.33), channel_id=1, source_target_pairs={{0,8},{4,12},{8,0},{12,4},{1,9},{5,13},{9,1},{13,5},{2,10},{6,14},... | collective-permute-start | bytes 196616 | tf_op jit(solution)/shard_map/ppermute | solution.py:215
  7.6 6.6 %collective-permute-start.2 = (bf16[128,256]{1,0:T(8,128)(2,1)S(1)}, bf16[128,256]{1,0:T(8,128)(2,1)S(1)}, u32[]{:S(2)}, u32[]{:S(2)}) collective-permute-start(bf16[128,256]{1,0:T(8,128)(2,1)S(1)} %get-tuple-element.34), channel_id=1, source_target_pairs={{0,12},{4,8},{8,4},{12,0},{1,13},{5,9},{9,5},{13,1},{2,14},{6,10},... | collective-permute-start | bytes 196616 | tf_op jit(solution)/shard_map/ppermute | solution.py:215
  9.4 8.0 %collective-permute-start.4 = (bf16[128,256]{1,0:T(8,128)(2,1)S(1)}, bf16[128,256]{1,0:T(8,128)(2,1)S(1)}, u32[]{:S(2)}, u32[]{:S(2)}) collective-permute-start(bf16[128,256]{1,0:T(8,128)(2,1)S(1)} %get-tuple-element.39), channel_id=1, source_target_pairs={{0,4},{4,0},{8,12},{12,8},{1,5},{5,1},{9,13},{13,9},{2,6},{6,2},{1... | collective-permute-start | bytes 196616 | tf_op jit(solution)/shard_map/ppermute | solution.py:215
  10.4 7.6 %collective-permute-start.5 = (bf16[128,256]{1,0:T(8,128)(2,1)S(1)}, bf16[128,256]{1,0:T(8,128)(2,1)S(1)}, u32[]{:S(2)}, u32[]{:S(2)}) collective-permute-start(bf16[128,256]{1,0:T(8,128)(2,1)S(1)} %get-tuple-element.40), channel_id=1, source_target_pairs={{0,8},{4,12},{8,0},{12,4},{1,9},{5,13},{9,1},{13,5},{2,10},{6,14},... | collective-permute-start | bytes 196616 | tf_op jit(solution)/shard_map/ppermute | solution.py:215
  13.9 6.1 %collective-permute-start.6 = (bf16[128,256]{1,0:T(8,128)(2,1)S(1)}, bf16[128,256]{1,0:T(8,128)(2,1)S(1)}, u32[]{:S(2)}, u32[]{:S(2)}) collective-permute-start(bf16[128,256]{1,0:T(8,128)(2,1)S(1)} %get-tuple-element.41), channel_id=1, source_target_pairs={{0,12},{4,8},{8,4},{12,0},{1,13},{5,9},{9,5},{13,1},{2,14},{6,10},... | collective-permute-start | bytes 196616 | tf_op jit(solution)/shard_map/ppermute | solution.py:215
  15.7 4.9 %collective-permute-start.3 = (bf16[256,128]{1,0:T(8,128)(2,1)S(1)}, bf16[256,128]{1,0:T(8,128)(2,1)S(1)}, u32[]{:S(2)}, u32[]{:S(2)}) collective-permute-start(bf16[256,128]{1,0:T(8,128)(2,1)S(1)} %get-tuple-element.35), channel_id=1, source_target_pairs={{0,16},{16,0},{1,17},{17,1},{2,18},{18,2},{3,19},{19,3},{4,20},{20... | collective-permute-start | bytes 196616 | tf_op jit(solution)/shard_map/ppermute | solution.py:268
  22.1 4.5 %collective-permute-start.7 = (bf16[128,128]{1,0:T(8,128)(2,1)S(1)}, bf16[128,128]{1,0:T(8,128)(2,1)S(1)}, u32[]{:S(2)}, u32[]{:S(2)}) collective-permute-start(bf16[128,128]{1,0:T(8,128)(2,1)S(1)} %get-tuple-element.46), channel_id=1, source_target_pairs={{0,4},{4,0},{8,12},{12,8},{1,5},{5,1},{9,13},{13,9},{2,6},{6,2},{1... | collective-permute-start | bytes 98312 | tf_op jit(solution)/shard_map/ppermute | solution.py:215
  22.2 5.6 %collective-permute-start.8 = (bf16[128,128]{1,0:T(8,128)(2,1)S(1)}, bf16[128,128]{1,0:T(8,128)(2,1)S(1)}, u32[]{:S(2)}, u32[]{:S(2)}) collective-permute-start(bf16[128,128]{1,0:T(8,128)(2,1)S(1)} %get-tuple-element.47), channel_id=1, source_target_pairs={{0,8},{4,12},{8,0},{12,4},{1,9},{5,13},{9,1},{13,5},{2,10},{6,14},... | collective-permute-start | bytes 98312 | tf_op jit(solution)/shard_map/ppermute | solution.py:215
  25.8 5.7 %collective-permute-start.9 = (bf16[128,128]{1,0:T(8,128)(2,1)S(1)}, bf16[128,128]{1,0:T(8,128)(2,1)S(1)}, u32[]{:S(2)}, u32[]{:S(2)}) collective-permute-start(bf16[128,128]{1,0:T(8,128)(2,1)S(1)} %get-tuple-element.48), channel_id=1, source_target_pairs={{0,12},{4,8},{8,4},{12,0},{1,13},{5,9},{9,5},{13,1},{2,14},{6,10},... | collective-permute-start | bytes 98312 | tf_op jit(solution)/shard_map/ppermute | solution.py:215
  32.3 1.9 %collective-permute-start.10 = (f32[64,128]{1,0:T(8,128)S(1)}, f32[64,128]{1,0:T(8,128)S(1)}, u32[]{:S(2)}, u32[]{:S(2)}) collective-permute-start(f32[64,128]{1,0:T(8,128)S(1)} %get-tuple-element.51), channel_id=1, source_target_pairs={{0,1},{1,0},{2,3},{3,2},{4,5},{5,4},{6,7},{7,6},{8,9},{9,8},{10,11... | collective-permute-start | bytes 98312 | tf_op jit(solution)/shard_map/ppermute | solution.py:215
  32.3 3.9 %collective-permute-start.11 = (f32[64,128]{1,0:T(8,128)S(1)}, f32[64,128]{1,0:T(8,128)S(1)}, u32[]{:S(2)}, u32[]{:S(2)}) collective-permute-start(f32[64,128]{1,0:T(8,128)S(1)} %get-tuple-element.52), channel_id=1, source_target_pairs={{0,2},{1,3},{2,0},{3,1},{4,6},{5,7},{6,4},{7,5},{8,10},{9,11},{10,... | collective-permute-start | bytes 98312 | tf_op jit(solution)/shard_map/ppermute | solution.py:215
  33.8 3.3 %collective-permute-start.12 = (f32[64,128]{1,0:T(8,128)S(1)}, f32[64,128]{1,0:T(8,128)S(1)}, u32[]{:S(2)}, u32[]{:S(2)}) collective-permute-start(f32[64,128]{1,0:T(8,128)S(1)} %get-tuple-element.53), channel_id=1, source_target_pairs={{0,3},{1,2},{2,1},{3,0},{4,7},{5,6},{6,5},{7,4},{8,11},{9,10},{10,... | collective-permute-start | bytes 98312 | tf_op jit(solution)/shard_map/ppermute | solution.py:215

commit v4 on v3

--- a/solution.py
+++ b/solution.py
@@ -110,10 +110,10 @@
             gain[...] = all_gains[:, block * unit : (block + 1) * unit]
 
 
-def gather_positions(chunks, held):
+def gather_positions(chunks, steps, held):
     seq_index = lax.axis_index("seq")
     rows = chunks[0].shape[0]
-    for step, chunk in enumerate(chunks):
+    for step, chunk in zip([0, *steps], chunks):
         at = pl.multiple_of((seq_index ^ step) * rows, rows)
         held[pl.ds(at, rows), :] = chunk[...]
 
@@ -139,7 +139,7 @@
     chunks, (out, gated_spec, filter_spec, held) = rest[:-4], rest[-4:]
     length = held.shape[0]
     unit = held.shape[1] // 4
-    gather_positions(chunks, held)
+    gather_positions(chunks, middle_first(len(chunks)), held)
     spec = dot(table[...], held[:, : 2 * unit])
     spec, filters = spec[:, :unit], turned(spec[:, unit:], turns)
     gated_spec[...] = spec
@@ -156,7 +156,7 @@
 def mixed_spectra(table, turns, gated_spec, *rest):
     chunks, (gates, lag_spec, mixed_spec, held) = rest[:-4], rest[-4:]
     unit = held.shape[1] // 4
-    gather_positions(chunks, held)
+    gather_positions(chunks, near_first(len(chunks)), held)
     gates[...] = held[:, 2 * unit :]
     spec = dot(table[...], held[:, : 2 * unit])
     first = turned(spec[:, :unit], turns)
@@ -194,7 +194,7 @@
     chunks, grad, lags = refs[:count], refs[count], refs[count + 1 :]
     unit = stage.shape[2] // 2
     seq_index, chan_index = lax.axis_index("seq"), lax.axis_index("chan")
-    for step, chunk in enumerate(chunks):
+    for step, chunk in zip([0, *middle_first(count)], chunks):
         stage[seq_index ^ step] = chunk[...]
     grad[0] = jnp.concatenate([stage[block][:, :unit] for block in range(count)], axis=1)
     lag_grad = jnp.concatenate([stage[block][:, unit:] for block in range(count)], axis=1)
@@ -209,12 +209,23 @@
     out[...] = functools.reduce(jnp.add, [lag[...] for lag in lags])
 
 
-def exchange(chunks, axis):
+def exchange(chunks, axis, steps):
     size = lax.axis_size(axis)
     return [chunks[0]] + [
-        lax.ppermute(chunks[step], axis, [(i, i ^ step) for i in range(size)])
-        for step in range(1, size)
+        lax.ppermute(chunks[step], axis, [(i, i ^ step) for i in range(size)]) for step in steps
     ]
+
+
+def middle_first(size):
+    return [*range(2, size), 1]
+
+
+def near_first(size):
+    return list(range(1, size))
+
+
+def far_first(size):
+    return list(reversed(range(1, size)))
 
 
 def body(table, turns, *args):
@@ -252,8 +263,8 @@
         [pl.ANY] + [pltpu.HBM] * 6,
         8,
     )(first[0], saved_input, pre_gate, post_gate, skip_gain, table, turns)
-    first = exchange(first, "seq")
-    second = exchange(second, "seq")
+    first = exchange(first, "seq", middle_first(seq_count))
+    second = exchange(second, "seq", near_first(seq_count))
 
     gradient, gated_spec, filter_spec = call(
         first_tick,
@@ -277,7 +288,7 @@
         [struct((rows, 2 * unit), BF16)] * seq_count,
         [struct((seq_count, rows, 2 * unit), BF16)],
     )(gain, table, received, filter_spec, lag_spec, mixed_spec, gates)
-    result = exchange(result, "seq")
+    result = exchange(result, "seq", middle_first(seq_count))
 
     lag_width = width // chan_count
     grad_out, *lags = call(
@@ -288,7 +299,7 @@
             struct((width, rows), F32),
         ],
     )(*result)
-    lags = exchange(lags, "chan")
+    lags = exchange(lags, "chan", far_first(chan_count))
     (lag_grad,) = call(add_up, [struct((lag_width, rows), F32)])(*lags)
     return grad_out, lag_grad.T[None]
 

time: 37.9 us -> 34.5 us (0.910)
  waiting for transfers between devices: 10.8 us -> 7.4 us
    ppermute x12, waiting for transfers between devices: 10.8 us -> 6.39 us  [exchange(): lax.ppermute(chunks[step], axis, [(i, i ^ step) for i in range(size)])]
    ppermute x1, waiting for transfers between devices: 0.01 us -> 1.01 us  [body(): received = lax.ppermute(gradient, 'section', ring)]
  transfers between devices with their start and end apart: 13 -> 13, of which waited for: 7 -> 6; matrix products, arithmetic and copies ran while one was open for 0% -> 0% of each run, Pallas kernels for 11% -> 12%
where the time goes in v4:
time: 34.5 us; the launch traced here: 34.4 us
  starting transfers between devices  18.2 us (53%)
  Pallas kernels  8.15 us (24%)
  waiting for transfers between devices  7.4 us (21%)
  between operations  0.68 us (2%)
    ppermute x12, starting transfers between devices, exchange(): lax.ppermute(chunks[step], axis, [(i, i ^ step) for i in range(size)])  16.6 us
    pallas_call x7, Pallas kernels, run(): pl.pallas_call(kernel, out_shape=out_shape, in_specs=[pl.BlockSpec(memory...  8.15 us
    ppermute x12, waiting for transfers between devices, exchange(): lax.ppermute(chunks[step], axis, [(i, i ^ step) for i in range(size)])  6.39 us
    ppermute x1, starting transfers between devices, body(): received = lax.ppermute(gradient, 'section', ring)  1.55 us
    ppermute x1, waiting for transfers between devices, body(): received = lax.ppermute(gradient, 'section', ring)  1.01 us
  transfers between devices with their start and end apart: 13, of which 6 were waited for; matrix products, arithmetic and copies ran while one was open for 0% of the time, Pallas kernels for 12%

profile of v4, /device:TPU:0, one launch (start us, length us, event | category | flops | bytes accessed | tf_op | source)
XLA Modules:
  0.0 34.4 jit_solution(7226585009766536304)
XLA Ops:
  0.6 1.2 %shard_map.104 = (bf16[128,256]{1,0:T(8,128)(2,1)S(1)}, bf16[128,256]{1,0:T(8,128)(2,1)S(1)}, bf16[128,256]{1,0:T(8,128)(2,1)S(1)}, bf16[128,256]{1,0:T(8,128)(2,1)S(1)}) custom-call(bf16[1,2,128,256]{3,2,1,0:T(8,128)(2,1)} %post.3, bf16[1,128,256]{2,1,0:T(8,128)(2,1)} %held.1, bf16[128,256]{1,0:T(8,128)(2,1)} %loss.1, bf16[1,2,128,256]{3,2,1,0:T(8,128)(2,1)} %pre.3, ...), custom_call_target="tpu_custom_call" | custom-call | tf_op jit(solution)/shard_map/pallas_call | solution.py:45
  1.9 4.1 %collective-permute-start = (bf16[128,256]{1,0:T(8,128)(2,1)S(1)}, bf16[128,256]{1,0:T(8,128)(2,1)S(1)}, u32[]{:S(2)}, u32[]{:S(2)}) collective-permute-start(bf16[128,256]{1,0:T(8,128)(2,1)S(1)} %get-tuple-element.32), channel_id=1, source_target_pairs={{0,8},{4,12},{8,0},{12,4},{1,9},{5,13},{9,1},{13,5},{2,10},{6,14},... | collective-permute-start | bytes 196616 | tf_op jit(solution)/shard_map/ppermute | solution.py:215
  6.0 1.3 %collective-permute-start.1 = (bf16[128,256]{1,0:T(8,128)(2,1)S(1)}, bf16[128,256]{1,0:T(8,128)(2,1)S(1)}, u32[]{:S(2)}, u32[]{:S(2)}) collective-permute-start(bf16[128,256]{1,0:T(8,128)(2,1)S(1)} %get-tuple-element.33), channel_id=1, source_target_pairs={{0,12},{4,8},{8,4},{12,0},{1,13},{5,9},{9,5},{13,1},{2,14},{6,10},... | collective-permute-start | bytes 196616 | tf_op jit(solution)/shard_map/ppermute | solution.py:215
  7.6 1.8 %shard_map.105 = (bf16[128,256]{1,0:T(8,128)(2,1)S(1)}, bf16[128,256]{1,0:T(8,128)(2,1)S(1)}, bf16[128,256]{1,0:T(8,128)(2,1)S(1)}, bf16[128,256]{1,0:T(8,128)(2...) custom-call(bf16[128,256]{1,0:T(8,128)(2,1)S(1)} %get-tuple-element.28.after.rest_0_, ...), custom_call_target="tpu_custom_call" | custom-call | tf_op jit(solution)/shard_map/pallas_call | solution.py:45
  9.4 1.9 %collective-permute-start.4 = (bf16[128,256]{1,0:T(8,128)(2,1)S(1)}, bf16[128,256]{1,0:T(8,128)(2,1)S(1)}, u32[]{:S(2)}, u32[]{:S(2)}) collective-permute-start(bf16[128,256]{1,0:T(8,128)(2,1)S(1)} %get-tuple-element.39), channel_id=1, source_target_pairs={{0,4},{4,0},{8,12},{12,8},{1,5},{5,1},{9,13},{13,9},{2,6},{6,2},{1... | collective-permute-start | bytes 196616 | tf_op jit(solution)/shard_map/ppermute | solution.py:215
  11.3 1.7 %collective-permute-start.5 = (bf16[128,256]{1,0:T(8,128)(2,1)S(1)}, bf16[128,256]{1,0:T(8,128)(2,1)S(1)}, u32[]{:S(2)}, u32[]{:S(2)}) collective-permute-start(bf16[128,256]{1,0:T(8,128)(2,1)S(1)} %get-tuple-element.40), channel_id=1, source_target_pairs={{0,8},{4,12},{8,0},{12,4},{1,9},{5,13},{9,1},{13,5},{2,10},{6,14},... | collective-permute-start | bytes 196616 | tf_op jit(solution)/shard_map/ppermute | solution.py:215
  13.0 1.9 %collective-permute-start.6 = (bf16[128,256]{1,0:T(8,128)(2,1)S(1)}, bf16[128,256]{1,0:T(8,128)(2,1)S(1)}, u32[]{:S(2)}, u32[]{:S(2)}) collective-permute-start(bf16[128,256]{1,0:T(8,128)(2,1)S(1)} %get-tuple-element.41), channel_id=1, source_target_pairs={{0,12},{4,8},{8,4},{12,0},{1,13},{5,9},{9,5},{13,1},{2,14},{6,10},... | collective-permute-start | bytes 196616 | tf_op jit(solution)/shard_map/ppermute | solution.py:215
  14.9 1.6 %shard_map.106 = (bf16[256,128]{1,0:T(8,128)(2,1)S(1)}, f32[1024,64]{1,0:T(8,128)S(1)}, f32[2,512,64]{2,1,0:T(8,128)S(1)}) custom-call(f32[1,64]{1,0:T(1,128)S(1)} %get-tuple-element.29.gain, bf16[1024,512]{1,0:T(8,128)(2,1)S(1)} %get-tuple-element.30.table, f32[2,512,64]{2,1,0:T(8,128)S(1)} %get-tuple-element.31.turns, ...), custom_call_target="tpu_custom_call" | custom-call | tf_op jit(solution)/shard_map/pallas_call | solution.py:45
  16.5 1.6 %collective-permute-start.3 = (bf16[256,128]{1,0:T(8,128)(2,1)S(1)}, bf16[256,128]{1,0:T(8,128)(2,1)S(1)}, u32[]{:S(2)}, u32[]{:S(2)}) collective-permute-start(bf16[256,128]{1,0:T(8,128)(2,1)S(1)} %get-tuple-element.35), channel_id=1, source_target_pairs={{0,16},{16,0},{1,17},{17,1},{2,18},{18,2},{3,19},{19,3},{4,20},{20... | collective-permute-start | bytes 196616 | tf_op jit(solution)/shard_map/ppermute | solution.py:279
  18.0 1.1 %collective-permute-done.6.rest_3_ = bf16[128,256]{1,0:T(8,128)(2,1)S(1)} collective-permute-done((bf16[128,256]{1,0:T(8,128)(2,1)S(1)}, bf16[128,256]{1,0:T(8,128)(2,1)S(1)}, u32[]{:S(2)}, u32[]{:S(2)}) %collective-permute-start.6) | collective-permute-done | bytes 65568 | tf_op jit(solution)/shard_map/ppermute | solution.py:215
  19.2 0.6 %shard_map.107 = (bf16[512,128]{1,0:T(8,128)(2,1)S(1)}, f32[2,512,64]{2,1,0:T(8,128)S(1)}, f32[2,512,64]{2,1,0:T(8,128)S(1)}) custom-call(bf16[1024,512]{1,0:T(8,128)(2,1)S(1)} %get-tuple-element.30.table, f32[2,512,64]{2,1,0:T(8,128)S(1)} %get-tuple-element.31.turns, f32[1024,64]{1,0:T(8,128)S(1)} %get-tuple-element.37.gated_spec, ...), custom_call_target="tpu_custom_call" | custom-call | tf_op jit(solution)/shard_map/pallas_call | solution.py:45
  19.8 1.0 %collective-permute-done.3.received = bf16[256,128]{1,0:T(8,128)(2,1)S(1)} collective-permute-done((bf16[256,128]{1,0:T(8,128)(2,1)S(1)}, bf16[256,128]{1,0:T(8,128)(2,1)S(1)}, u32[]{:S(2)}, u32[]{:S(2)}) %collective-permute-start.3) | collective-permute-done | bytes 65568 | tf_op jit(solution)/shard_map/ppermute | solution.py:279
  20.8 1.5 %shard_map.108 = (bf16[128,128]{1,0:T(8,128)(2,1)S(1)}, bf16[128,128]{1,0:T(8,128)(2,1)S(1)}, bf16[128,128]{1,0:T(8,128)(2,1)S(1)}, bf16[128,128]{1,0:T(8,128)(2,1)S(1)}) custom-call(f32[1,64]{1,0:T(1,128)S(1)} %get-tuple-element.29.gain, bf16[1024,512]{1,0:T(8,128)(2,1)S(1)} %get-tuple-element.30.table, ...), custom_call_target="tpu_custom_call" | custom-call | tf_op jit(solution)/shard_map/pallas_call | solution.py:45
  22.3 0.9 %collective-permute-start.7 = (bf16[128,128]{1,0:T(8,128)(2,1)S(1)}, bf16[128,128]{1,0:T(8,128)(2,1)S(1)}, u32[]{:S(2)}, u32[]{:S(2)}) collective-permute-start(bf16[128,128]{1,0:T(8,128)(2,1)S(1)} %get-tuple-element.46), channel_id=1, source_target_pairs={{0,8},{4,12},{8,0},{12,4},{1,9},{5,13},{9,1},{13,5},{2,10},{6,14},... | collective-permute-start | bytes 98312 | tf_op jit(solution)/shard_map/ppermute | solution.py:215
  23.2 1.4 %collective-permute-start.8 = (bf16[128,128]{1,0:T(8,128)(2,1)S(1)}, bf16[128,128]{1,0:T(8,128)(2,1)S(1)}, u32[]{:S(2)}, u32[]{:S(2)}) collective-permute-start(bf16[128,128]{1,0:T(8,128)(2,1)S(1)} %get-tuple-element.47), channel_id=1, source_target_pairs={{0,12},{4,8},{8,4},{12,0},{1,13},{5,9},{9,5},{13,1},{2,14},{6,10},... | collective-permute-start | bytes 98312 | tf_op jit(solution)/shard_map/ppermute | solution.py:215
  24.7 1.2 %collective-permute-start.9 = (bf16[128,128]{1,0:T(8,128)(2,1)S(1)}, bf16[128,128]{1,0:T(8,128)(2,1)S(1)}, u32[]{:S(2)}, u32[]{:S(2)}) collective-permute-start(bf16[128,128]{1,0:T(8,128)(2,1)S(1)} %get-tuple-element.48), channel_id=1, source_target_pairs={{0,4},{4,0},{8,12},{12,8},{1,5},{5,1},{9,13},{13,9},{2,6},{6,2},{1... | collective-permute-start | bytes 98312 | tf_op jit(solution)/shard_map/ppermute | solution.py:215
  25.9 1.3 %collective-permute-done.7.rest_1_ = bf16[128,128]{1,0:T(8,128)(2,1)S(1)} collective-permute-done((bf16[128,128]{1,0:T(8,128)(2,1)S(1)}, bf16[128,128]{1,0:T(8,128)(2,1)S(1)}, u32[]{:S(2)}, u32[]{:S(2)}) %collective-permute-start.7) | collective-permute-done | bytes 32800 | tf_op jit(solution)/shard_map/ppermute | solution.py:215
  27.2 1.7 %collective-permute-done.8.rest_2_ = bf16[128,128]{1,0:T(8,128)(2,1)S(1)} collective-permute-done((bf16[128,128]{1,0:T(8,128)(2,1)S(1)}, bf16[128,128]{1,0:T(8,128)(2,1)S(1)}, u32[]{:S(2)}, u32[]{:S(2)}) %collective-permute-start.8) | collective-permute-done | bytes 32800 | tf_op jit(solution)/shard_map/ppermute | solution.py:215
  29.0 0.7 %shard_map.109 = (bf16[1,128,256]{2,1,0:T(8,128)(2,1)}, f32[64,128]{1,0:T(8,128)S(1)}, f32[64,128]{1,0:T(8,128)S(1)}, f32[64,128]{1,0:T(8,128)S(1)}, f32[64,128]{1,0:T(8,128)S(1)}) custom-call(bf16[128,128]{1,0:T(8,128)(2,1)S(1)} %get-tuple-element.45.rest_0_, bf16[128,128]{1,0:T(8,128)(2,1)S(1)} %collective-permute-done.7.rest_1_, ...), custom_call_target="tpu_custom_call" | custom-call | tf_op jit(solution)/shard_map/pallas_call | solution.py:45
  29.7 1.6 %collective-permute-start.11 = (f32[64,128]{1,0:T(8,128)S(1)}, f32[64,128]{1,0:T(8,128)S(1)}, u32[]{:S(2)}, u32[]{:S(2)}) collective-permute-start(f32[64,128]{1,0:T(8,128)S(1)} %get-tuple-element.52), channel_id=1, source_target_pairs={{0,2},{1,3},{2,0},{3,1},{4,6},{5,7},{6,4},{7,5},{8,10},{9,11},{10,... | collective-permute-start | bytes 98312 | tf_op jit(solution)/shard_map/ppermute | solution.py:215
  31.3 0.3 collective-permute-start.12
  31.6 1.8 %collective-permute-done.10.refs_1_ = f32[64,128]{1,0:T(8,128)S(1)} collective-permute-done((f32[64,128]{1,0:T(8,128)S(1)}, f32[64,128]{1,0:T(8,128)S(1)}, u32[]{:S(2)}, u32[]{:S(2)}) %collective-permute-start.10) | collective-permute-done | bytes 32800 | tf_op jit(solution)/shard_map/ppermute | solution.py:215
  33.3 0.4 %collective-permute-done.11.refs_2_ = f32[64,128]{1,0:T(8,128)S(1)} collective-permute-done((f32[64,128]{1,0:T(8,128)S(1)}, f32[64,128]{1,0:T(8,128)S(1)}, u32[]{:S(2)}, u32[]{:S(2)}) %collective-permute-start.11) | collective-permute-done | bytes 32800 | tf_op jit(solution)/shard_map/ppermute | solution.py:215
  33.8 0.6 %shard_map.110 = f32[64,128]{1,0:T(8,128)} custom-call(f32[64,128]{1,0:T(8,128)S(1)} %get-tuple-element.50.refs_0_, f32[64,128]{1,0:T(8,128)S(1)} %collective-permute-done.10.refs_1_, f32[64,128]{1,0:T(8,128)S(1)} %collective-permute-done.11.refs_2_, f32[64,128]{1,0:T(8,128)S(1)} %collective-permute-done.12.refs_3_), custom_call_target="tpu_custom_call" | custom-call | tf_op jit(solution)/shard_map/pallas_call | solution.py:45
  (9 shorter events, 0.3 us)
Async XLA Ops:
  1.9 11.1 %collective-permute-start = (bf16[128,256]{1,0:T(8,128)(2,1)S(1)}, bf16[128,256]{1,0:T(8,128)(2,1)S(1)}, u32[]{:S(2)}, u32[]{:S(2)}) collective-permute-start(bf16[128,256]{1,0:T(8,128)(2,1)S(1)} %get-tuple-element.32), channel_id=1, source_target_pairs={{0,8},{4,12},{8,0},{12,4},{1,9},{5,13},{9,1},{13,5},{2,10},{6,14},... | collective-permute-start | bytes 196616 | tf_op jit(solution)/shard_map/ppermute | solution.py:215
  6.0 8.9 %collective-permute-start.1 = (bf16[128,256]{1,0:T(8,128)(2,1)S(1)}, bf16[128,256]{1,0:T(8,128)(2,1)S(1)}, u32[]{:S(2)}, u32[]{:S(2)}) collective-permute-start(bf16[128,256]{1,0:T(8,128)(2,1)S(1)} %get-tuple-element.33), channel_id=1, source_target_pairs={{0,12},{4,8},{8,4},{12,0},{1,13},{5,9},{9,5},{13,1},{2,14},{6,10},... | collective-permute-start | bytes 196616 | tf_op jit(solution)/shard_map/ppermute | solution.py:215
  7.3 7.5 %collective-permute-start.2 = (bf16[128,256]{1,0:T(8,128)(2,1)S(1)}, bf16[128,256]{1,0:T(8,128)(2,1)S(1)}, u32[]{:S(2)}, u32[]{:S(2)}) collective-permute-start(bf16[128,256]{1,0:T(8,128)(2,1)S(1)} %get-tuple-element.34), channel_id=1, source_target_pairs={{0,4},{4,0},{8,12},{12,8},{1,5},{5,1},{9,13},{13,9},{2,6},{6,2},{1... | collective-permute-start | bytes 196616 | tf_op jit(solution)/shard_map/ppermute | solution.py:215
  9.4 8.7 %collective-permute-start.4 = (bf16[128,256]{1,0:T(8,128)(2,1)S(1)}, bf16[128,256]{1,0:T(8,128)(2,1)S(1)}, u32[]{:S(2)}, u32[]{:S(2)}) collective-permute-start(bf16[128,256]{1,0:T(8,128)(2,1)S(1)} %get-tuple-element.39), channel_id=1, source_target_pairs={{0,4},{4,0},{8,12},{12,8},{1,5},{5,1},{9,13},{13,9},{2,6},{6,2},{1... | collective-permute-start | bytes 196616 | tf_op jit(solution)/shard_map/ppermute | solution.py:215
  11.3 6.8 %collective-permute-start.5 = (bf16[128,256]{1,0:T(8,128)(2,1)S(1)}, bf16[128,256]{1,0:T(8,128)(2,1)S(1)}, u32[]{:S(2)}, u32[]{:S(2)}) collective-permute-start(bf16[128,256]{1,0:T(8,128)(2,1)S(1)} %get-tuple-element.40), channel_id=1, source_target_pairs={{0,8},{4,12},{8,0},{12,4},{1,9},{5,13},{9,1},{13,5},{2,10},{6,14},... | collective-permute-start | bytes 196616 | tf_op jit(solution)/shard_map/ppermute | solution.py:215
  13.0 6.2 %collective-permute-start.6 = (bf16[128,256]{1,0:T(8,128)(2,1)S(1)}, bf16[128,256]{1,0:T(8,128)(2,1)S(1)}, u32[]{:S(2)}, u32[]{:S(2)}) collective-permute-start(bf16[128,256]{1,0:T(8,128)(2,1)S(1)} %get-tuple-element.41), channel_id=1, source_target_pairs={{0,12},{4,8},{8,4},{12,0},{1,13},{5,9},{9,5},{13,1},{2,14},{6,10},... | collective-permute-start | bytes 196616 | tf_op jit(solution)/shard_map/ppermute | solution.py:215
  16.5 4.3 %collective-permute-start.3 = (bf16[256,128]{1,0:T(8,128)(2,1)S(1)}, bf16[256,128]{1,0:T(8,128)(2,1)S(1)}, u32[]{:S(2)}, u32[]{:S(2)}) collective-permute-start(bf16[256,128]{1,0:T(8,128)(2,1)S(1)} %get-tuple-element.35), channel_id=1, source_target_pairs={{0,16},{16,0},{1,17},{17,1},{2,18},{18,2},{3,19},{19,3},{4,20},{20... | collective-permute-start | bytes 196616 | tf_op jit(solution)/shard_map/ppermute | solution.py:279
  22.3 4.9 %collective-permute-start.7 = (bf16[128,128]{1,0:T(8,128)(2,1)S(1)}, bf16[128,128]{1,0:T(8,128)(2,1)S(1)}, u32[]{:S(2)}, u32[]{:S(2)}) collective-permute-start(bf16[128,128]{1,0:T(8,128)(2,1)S(1)} %get-tuple-element.46), channel_id=1, source_target_pairs={{0,8},{4,12},{8,0},{12,4},{1,9},{5,13},{9,1},{13,5},{2,10},{6,14},... | collective-permute-start | bytes 98312 | tf_op jit(solution)/shard_map/ppermute | solution.py:215
  23.2 5.7 %collective-permute-start.8 = (bf16[128,128]{1,0:T(8,128)(2,1)S(1)}, bf16[128,128]{1,0:T(8,128)(2,1)S(1)}, u32[]{:S(2)}, u32[]{:S(2)}) collective-permute-start(bf16[128,128]{1,0:T(8,128)(2,1)S(1)} %get-tuple-element.47), channel_id=1, source_target_pairs={{0,12},{4,8},{8,4},{12,0},{1,13},{5,9},{9,5},{13,1},{2,14},{6,10},... | collective-permute-start | bytes 98312 | tf_op jit(solution)/shard_map/ppermute | solution.py:215
  24.7 4.3 %collective-permute-start.9 = (bf16[128,128]{1,0:T(8,128)(2,1)S(1)}, bf16[128,128]{1,0:T(8,128)(2,1)S(1)}, u32[]{:S(2)}, u32[]{:S(2)}) collective-permute-start(bf16[128,128]{1,0:T(8,128)(2,1)S(1)} %get-tuple-element.48), channel_id=1, source_target_pairs={{0,4},{4,0},{8,12},{12,8},{1,5},{5,1},{9,13},{13,9},{2,6},{6,2},{1... | collective-permute-start | bytes 98312 | tf_op jit(solution)/shard_map/ppermute | solution.py:215
  29.7 3.6 %collective-permute-start.10 = (f32[64,128]{1,0:T(8,128)S(1)}, f32[64,128]{1,0:T(8,128)S(1)}, u32[]{:S(2)}, u32[]{:S(2)}) collective-permute-start(f32[64,128]{1,0:T(8,128)S(1)} %get-tuple-element.51), channel_id=1, source_target_pairs={{0,3},{1,2},{2,1},{3,0},{4,7},{5,6},{6,5},{7,4},{8,11},{9,10},{10,... | collective-permute-start | bytes 98312 | tf_op jit(solution)/shard_map/ppermute | solution.py:215
  29.7 4.0 %collective-permute-start.11 = (f32[64,128]{1,0:T(8,128)S(1)}, f32[64,128]{1,0:T(8,128)S(1)}, u32[]{:S(2)}, u32[]{:S(2)}) collective-permute-start(f32[64,128]{1,0:T(8,128)S(1)} %get-tuple-element.52), channel_id=1, source_target_pairs={{0,2},{1,3},{2,0},{3,1},{4,6},{5,7},{6,4},{7,5},{8,10},{9,11},{10,... | collective-permute-start | bytes 98312 | tf_op jit(solution)/shard_map/ppermute | solution.py:215
  31.3 2.5 %collective-permute-start.12 = (f32[64,128]{1,0:T(8,128)S(1)}, f32[64,128]{1,0:T(8,128)S(1)}, u32[]{:S(2)}, u32[]{:S(2)}) collective-permute-start(f32[64,128]{1,0:T(8,128)S(1)} %get-tuple-element.53), channel_id=1, source_target_pairs={{0,1},{1,0},{2,3},{3,2},{4,5},{5,4},{6,7},{7,6},{8,9},{9,8},{10,11... | collective-permute-start | bytes 98312 | tf_op jit(solution)/shard_map/ppermute | solution.py:215

commit v5 on v4

v5 whole, which is shorter than its diff:
```python
import functools
import math

import jax
import jax.numpy as jnp
import ml_dtypes
import numpy as np
from jax import lax
from jax.experimental import pallas as pl
from jax.experimental.pallas import tpu as pltpu
from jax.sharding import PartitionSpec as P

BF16 = jnp.bfloat16
F32 = jnp.float32
HALF_TURN = math.sqrt(0.5)


def transform_tables(length):
    freq = np.concatenate([np.arange(rest, length, 4, dtype=np.int64) for rest in range(4)])
    position = np.arange(length // 2, dtype=np.int64)
    angles = math.pi / (2 * length) * ((2 * freq[:, None] + 1) * position[None, :] % (4 * length))
    table = np.concatenate([np.cos(angles), np.sin(angles)], axis=0).astype(ml_dtypes.bfloat16)
    return table, np.ascontiguousarray(table.T)


def size_of(shapes):
    total = 0
    for shape in shapes:
        lanes = -(-shape.shape[-1] // 128) * 128
        total += math.prod(shape.shape[:-1]) * lanes * jnp.dtype(shape.dtype).itemsize
    return total


def call(kernel, out_shape, scratch=(), spaces=None, copies=0):
    def run(*arrays):
        held = size_of([*arrays, *out_shape, *scratch])
        if spaces:
            arrays = [
                pltpu.with_memory_space_constraint(array, space) if space == pltpu.HBM else array
                for array, space in zip(arrays, spaces)
            ]
        scratch_shapes = [pltpu.VMEM(shape.shape, shape.dtype) for shape in scratch]
        if copies:
            scratch_shapes.append(pltpu.SemaphoreType.DMA((copies,)))
        return pl.pallas_call(
            kernel,
            out_shape=out_shape,
            in_specs=[
                pl.BlockSpec(memory_space=space)
                for space in spaces or [pltpu.VMEM] * len(arrays)
            ],
            scratch_shapes=scratch_shapes,
            compiler_params=pltpu.CompilerParams(vmem_limit_bytes=2 * held + (4 << 20)),
        )(*arrays)

    return run


def fetch(sources, places, semaphores):
    copies = [
        pltpu.make_async_copy(source, place, semaphores.at[at])
        for at, (source, place) in enumerate(zip(sources, places))
    ]
    for copy in copies:
        copy.start()
    return copies


def wait(copies):
    for copy in copies:
        copy.wait()


def dot(left, right):
    return jnp.dot(left, right, preferred_element_type=F32)


def pack(arrays, stage, outs):
    seq_index = lax.axis_index("seq")
    count = len(outs)
    unit = arrays[0].shape[1] // count
    for block in range(count):
        lanes = slice(block * unit, (block + 1) * unit)
        stage[block] = jnp.concatenate([array[:, lanes] for array in arrays], axis=1)
    for step, out in enumerate(outs):
        out[...] = stage[seq_index ^ step]


def pack_first(post, held, loss, pre, filters, *rest):
    *outs, stage, gates, lags, semaphores = rest
    sources = [post.at[0, 0], held.at[0], loss, pre.at[0, 0], filters.at[0]]
    wait(fetch(sources, [gates.at[at] for at in range(4)] + [lags], semaphores))
    gated = (gates[0].astype(F32) * gates[1].astype(F32)).astype(BF16)
    kept = jnp.where(lax.axis_index("section") == 0, gates[2], gates[1])
    pack([lags[...].astype(BF16), gated, gates[3], kept], stage, outs)


def pack_second(after, saved, pre, post, gains, forward, backward, *rest):
    del after
    *outs, gain, forward_out, backward_out, stage, gates, all_gains, semaphores = rest
    sources = [saved.at[0, 0], saved.at[0, 1], pre.at[0, 0], pre.at[0, 1], post.at[0, 1]]
    places = [gates.at[at] for at in range(5)]
    copies = fetch(
        [*sources, gains, forward, backward],
        [*places, all_gains, forward_out, backward_out],
        semaphores,
    )
    wait(copies[:6])
    mixed = (gates[0:2].astype(F32) * gates[2:4].astype(F32)).astype(BF16)
    pack([mixed[0], mixed[1], gates[4], gates[3]], stage, outs)
    unit = gain.shape[1] // 2
    for block in range(len(outs)):

        @pl.when(lax.axis_index("seq") == block)
        def _():
            own = all_gains[:, block * unit : (block + 1) * unit]
            gain[...] = jnp.concatenate([own, own], axis=1)

    wait(copies[6:])


def gather_positions(chunks, steps, held):
    seq_index = lax.axis_index("seq")
    rows = chunks[0].shape[0]
    for step, chunk in zip([0, *steps], chunks):
        at = pl.multiple_of((seq_index ^ step) * rows, rows)
        held[pl.ds(at, rows), :] = chunk[...]


def swap(array):
    unit = array.shape[1] // 2
    return jnp.concatenate([array[:, unit:], array[:, :unit]], axis=1)


def first_unit(array):
    return lax.broadcasted_iota(jnp.int32, array.shape, 1) < array.shape[1] // 2


def quarters(*arrays):
    size = arrays[0].shape[0] // 4
    return jnp.concatenate(
        [array[at * size : (at + 1) * size] for at, array in enumerate(arrays)], axis=0
    )


def spectrum(forward, top, bottom):
    both = dot(forward[...], jnp.concatenate([top, bottom], axis=1))
    length, lanes = both.shape[0] // 2, top.shape[1]
    real, imag = both[:length, lanes:], both[length:, lanes:]
    plus, minus = (real + imag) * HALF_TURN, (real - imag) * HALF_TURN
    return (
        both[:length, :lanes] + quarters(minus, -plus, -minus, plus),
        both[length:, :lanes] + quarters(plus, minus, -plus, -minus),
    )


def inverse(backward, real, imag):
    plus, minus = (real + imag) * HALF_TURN, (real - imag) * HALF_TURN
    real = jnp.concatenate([real, quarters(plus, -minus, -plus, minus)], axis=1)
    imag = jnp.concatenate([imag, quarters(-minus, -plus, minus, plus)], axis=1)
    return dot(backward[...], jnp.concatenate([real, imag], axis=0).astype(BF16))


def times_conj(real, imag, other_real, other_imag):
    return real * other_real + imag * other_imag, imag * other_real - real * other_imag


def halves(array):
    size, lanes = array.shape[0] // 2, array.shape[1] // 2
    return [
        (array[part * size : (part + 1) * size, :lanes], array[part * size : (part + 1) * size, lanes:])
        for part in range(2)
    ]


def first_tick(gain, forward, backward, *rest):
    *chunks, out, spectra, held = rest
    gather_positions(chunks, middle_first(len(chunks)), held)
    length, lanes = held.shape[0], gain.shape[1]
    parts = halves(held)
    real, imag = spectrum(forward, parts[0][0], parts[1][0])
    spectra[0], spectra[1] = real, imag
    both = inverse(backward, *times_conj(real, imag, swap(real), swap(imag))) * (1.0 / length)
    gradients = []
    for part, (first, second) in enumerate(parts):
        correlated = both[:, part * lanes : (part + 1) * lanes]
        kept = second.astype(F32)
        gradient = kept + swap(kept) * (correlated + gain[...] * first.astype(F32))
        gradients.append(jnp.where(lax.axis_index("section") == 0, kept, gradient))
    top, bottom = gradients
    out[...] = jnp.where(first_unit(top), swap(top), bottom).astype(BF16)


def mixed_spectra(scale, forward, spectra, *rest):
    *chunks, post, weight, other, lag_spec, held = rest
    gather_positions(chunks, near_first(len(chunks)), held)
    parts = halves(held)
    real, imag = spectrum(forward, parts[0][0], parts[1][0])
    low = first_unit(real)
    other[0] = jnp.where(low, spectra[0], real)
    other[1] = jnp.where(low, spectra[1], imag)
    lag_real, lag_imag = times_conj(spectra[0], spectra[1], swap(real), swap(imag))
    lag_spec[0] = jnp.where(low, 0.0, lag_real)
    lag_spec[1] = jnp.where(low, 0.0, lag_imag)
    for part, (_, gates) in enumerate(parts):
        gates = gates.astype(F32)
        low = first_unit(gates)
        post[part] = jnp.where(low, gates, swap(gates))
        weight[part] = jnp.where(low, swap(gates), scale)


def second_tick(gain, forward, backward, received, post, weight, other, lag_spec, *rest):
    *outs, stage = rest
    count, rows, lanes = stage.shape
    length = count * rows
    carried = received[...].astype(F32)
    low = first_unit(carried)
    carried = [jnp.where(low, carried, swap(carried)), jnp.where(low, swap(carried), carried)]
    gated = [(post[part] * carried[part]).astype(BF16) for part in range(2)]
    real, imag = times_conj(*spectrum(forward, *gated), other[0], other[1])
    both = inverse(backward, real + lag_spec[0], imag + lag_spec[1]) * (1.0 / length)
    for part in range(2):
        skipped = jnp.where(low, gain[...] * gated[part].astype(F32), 0.0)
        result = weight[part] * (both[:, part * lanes : (part + 1) * lanes] + skipped)
        result = jnp.where(low, carried[part] + result, result).astype(BF16)
        for block in range(count // 2):
            stage[part * (count // 2) + block] = result[block * rows : (block + 1) * rows]
    for step, out in enumerate(outs):
        out[...] = stage[lax.axis_index("seq") ^ step]


def unpack_gradient(*rest):
    *chunks, grad, stage = rest
    count = stage.shape[0]
    unit = stage.shape[2] // 2
    seq_index = lax.axis_index("seq")
    for step, chunk in zip([0, *middle_first(count)], chunks):
        stage[seq_index ^ step] = chunk[...]
    grad[0] = jnp.concatenate([stage[block][:, :unit] for block in range(count)], axis=1)


def unpack_lags(*rest):
    *refs, stage, lag_stage = rest
    count = stage.shape[0]
    chunks, lags = refs[:count], refs[count:]
    unit = stage.shape[2] // 2
    seq_index, chan_index = lax.axis_index("seq"), lax.axis_index("chan")
    for step, chunk in zip([0, *middle_first(count)], chunks):
        stage[seq_index ^ step] = chunk[...]
    lag_grad = jnp.concatenate([stage[block][:, unit:] for block in range(count)], axis=1)
    lag_stage[...] = lag_grad.astype(F32).T
    for step, lag in enumerate(lags):
        width = lag.shape[0]
        lag[...] = lag_stage[pl.ds(pl.multiple_of((chan_index ^ step) * width, width), width), :]


def add_up(*refs):
    *lags, out = refs
    out[...] = functools.reduce(jnp.add, [lag[...] for lag in lags])


def exchange(chunks, axis, steps):
    size = lax.axis_size(axis)
    return [chunks[0]] + [
        lax.ppermute(chunks[step], axis, [(i, i ^ step) for i in range(size)]) for step in steps
    ]


def middle_first(size):
    return [*range(2, size), 1]


def near_first(size):
    return list(range(1, size))


def far_first(size):
    return list(reversed(range(1, size)))


def body(forward, backward, *args):
    saved_input, pre_gate, post_gate, grad_held, loss_grad, filters, skip_gain = args
    seq_count = lax.axis_size("seq")
    chan_count = lax.axis_size("chan")
    section_count = lax.axis_size("section")
    _, tick_count, rows, width = saved_input.shape
    length = rows * seq_count
    unit = width // seq_count
    forward, backward = jnp.asarray(forward), jnp.asarray(backward)
    scale = 1.0 / math.sqrt(length * chan_count * tick_count)
    struct = jax.ShapeDtypeStruct
    chunk = struct((rows, 4 * unit), BF16)
    stage = struct((seq_count, rows, 4 * unit), BF16)
    held_rows = struct((length, 4 * unit), BF16)
    two_spectra = struct((2, length, 2 * unit), F32)
    two_parts = struct((2, length // 2, 2 * unit), F32)

    first = call(
        pack_first,
        [chunk] * seq_count,
        [stage, struct((4, rows, width), BF16), struct((rows, width), F32)],
        [pltpu.HBM] * 5,
        5,
    )(post_gate, grad_held, loss_grad, pre_gate, filters)
    *second, gain, forward, backward = call(
        pack_second,
        [chunk] * seq_count
        + [
            struct((1, 2 * unit), F32),
            struct(forward.shape, BF16),
            struct(backward.shape, BF16),
        ],
        [stage, struct((5, rows, width), BF16), struct((1, width), F32)],
        [pl.ANY] + [pltpu.HBM] * 6,
        8,
    )(first[0], saved_input, pre_gate, post_gate, skip_gain, forward, backward)
    first = exchange(first, "seq", middle_first(seq_count))
    second = exchange(second, "seq", near_first(seq_count))

    gradient, spectra = call(
        first_tick,
        [struct((length // 2, 2 * unit), BF16), two_spectra],
        [held_rows],
    )(gain, forward, backward, *first)
    ring = [(i, (i - 1) % section_count) for i in range(section_count)]
    received = lax.ppermute(gradient, "section", ring)

    prepared = call(
        functools.partial(mixed_spectra, scale),
        [two_parts, two_parts, two_spectra, two_spectra],
        [held_rows],
    )(forward, spectra, *second)

    sorted_chunks = struct((seq_count, rows, 2 * unit), BF16)
    result = call(
        second_tick,
        [struct((rows, 2 * unit), BF16)] * seq_count,
        [sorted_chunks],
    )(gain, forward, backward, received, *prepared)
    result = exchange(result, "seq", middle_first(seq_count))

    lag_width = width // chan_count
    lags = call(
        unpack_lags,
        [struct((lag_width, rows), F32)] * chan_count,
        [sorted_chunks, struct((width, rows), F32)],
    )(*result)
    lags = exchange(lags, "chan", far_first(chan_count))
    (grad_out,) = call(unpack_gradient, [struct((1, rows, width), BF16)], [sorted_chunks])(*result)
    (lag_grad,) = call(add_up, [struct((lag_width, rows), F32)])(*lags)
    return grad_out, lag_grad.T[None]


def solution(mesh):
    placed = (
        P("section", None, "seq", "chan"),
        P("section", None, "seq", "chan"),
        P("section", None, "seq", "chan"),
        P("section", "seq", "chan"),
        P("seq", "chan"),
        P("section", "seq", None),
        P("section", None),
    )

    def program(*args):
        return jax.shard_map(
            functools.partial(body, *transform_tables(args[0].shape[2])),
            mesh=mesh,
            in_specs=placed,
            out_specs=(P("section", "seq", "chan"), P("section", "seq", "chan")),
            check_vma=False,
        )(*args)

    return program
```

time: 34.5 us -> 32.9 us (0.954)
  Pallas kernels: 8.15 us -> 6.47 us
  waiting for transfers between devices: 7.4 us -> 7.05 us
    pallas_call x7 -> x8, Pallas kernels: 8.15 us -> 6.47 us  [run(): pl.pallas_call(kernel, out_shape=out_shape, in_specs=[pl.BlockSpec(memory...]
    ppermute x12, starting transfers between devices: 16.6 us -> 17 us  [exchange(): lax.ppermute(chunks[step], axis, [(i, i ^ step) for i in range(size)])]
  transfers between devices with their start and end apart: 13 -> 13, of which waited for: 6 -> 7; matrix products, arithmetic and copies ran while one was open for 0% -> 0% of each run, Pallas kernels for 12% -> 11%
where the time goes in v5:
time: 32.9 us; the launch traced here: 32.8 us
  starting transfers between devices  18.5 us (56%)
  waiting for transfers between devices  7.05 us (21%)
  Pallas kernels  6.47 us (20%)
  between operations  0.69 us (2%)
    ppermute x12, starting transfers between devices, exchange(): lax.ppermute(chunks[step], axis, [(i, i ^ step) for i in range(size)])  17 us
    pallas_call x8, Pallas kernels, run(): pl.pallas_call(kernel, out_shape=out_shape, in_specs=[pl.BlockSpec(memory...  6.47 us
    ppermute x12, waiting for transfers between devices, exchange(): lax.ppermute(chunks[step], axis, [(i, i ^ step) for i in range(size)])  6.1 us
    ppermute x1, starting transfers between devices, body(): received = lax.ppermute(gradient, 'section', ring)  1.56 us
    ppermute x1, waiting for transfers between devices, body(): received = lax.ppermute(gradient, 'section', ring)  0.96 us
  transfers between devices with their start and end apart: 13, of which 7 were waited for; matrix products, arithmetic and copies ran while one was open for 0% of the time, Pallas kernels for 11%

profile of v5, /device:TPU:0, one launch (start us, length us, event | category | flops | bytes accessed | tf_op | source)
XLA Modules:
  0.0 32.8 jit_solution(10401909577990227935)
XLA Ops:
  0.6 1.2 %shard_map.104 = (bf16[128,256]{1,0:T(8,128)(2,1)S(1)}, bf16[128,256]{1,0:T(8,128)(2,1)S(1)}, bf16[128,256]{1,0:T(8,128)(2,1)S(1)}, bf16[128,256]{1,0:T(8,128)(2,1)S(1)}) custom-call(bf16[1,2,128,256]{3,2,1,0:T(8,128)(2,1)} %post.3, bf16[1,128,256]{2,1,0:T(8,128)(2,1)} %held.1, bf16[128,256]{1,0:T(8,128)(2,1)} %loss.1, bf16[1,2,128,256]{3,2,1,0:T(8,128)(2,1)} %pre.3, ...), custom_call_target="tpu_custom_call" | custom-call | tf_op jit(solution)/shard_map/pallas_call | solution.py:45
  1.9 4.1 %collective-permute-start = (bf16[128,256]{1,0:T(8,128)(2,1)S(1)}, bf16[128,256]{1,0:T(8,128)(2,1)S(1)}, u32[]{:S(2)}, u32[]{:S(2)}) collective-permute-start(bf16[128,256]{1,0:T(8,128)(2,1)S(1)} %get-tuple-element.31), channel_id=1, source_target_pairs={{0,8},{4,12},{8,0},{12,4},{1,9},{5,13},{9,1},{13,5},{2,10},{6,14},... | collective-permute-start | bytes 196616 | tf_op jit(solution)/shard_map/ppermute | solution.py:265
  6.0 1.3 %collective-permute-start.1 = (bf16[128,256]{1,0:T(8,128)(2,1)S(1)}, bf16[128,256]{1,0:T(8,128)(2,1)S(1)}, u32[]{:S(2)}, u32[]{:S(2)}) collective-permute-start(bf16[128,256]{1,0:T(8,128)(2,1)S(1)} %get-tuple-element.32), channel_id=1, source_target_pairs={{0,12},{4,8},{8,4},{12,0},{1,13},{5,9},{9,5},{13,1},{2,14},{6,10},... | collective-permute-start | bytes 196616 | tf_op jit(solution)/shard_map/ppermute | solution.py:265
  7.6 1.5 %shard_map.105 = (bf16[128,256]{1,0:T(8,128)(2,1)S(1)}, bf16[128,256]{1,0:T(8,128)(2,1)S(1)}, bf16[128,256]{1,0:T(8,128)(2,1)S(1)}, bf16[128,256]{1,0:T(8,128)(2...) custom-call(bf16[128,256]{1,0:T(8,128)(2,1)S(1)} %get-tuple-element.27.after.rest_0_, ...), custom_call_target="tpu_custom_call" | custom-call | tf_op jit(solution)/shard_map/pallas_call | solution.py:45
  9.0 1.9 %collective-permute-start.4 = (bf16[128,256]{1,0:T(8,128)(2,1)S(1)}, bf16[128,256]{1,0:T(8,128)(2,1)S(1)}, u32[]{:S(2)}, u32[]{:S(2)}) collective-permute-start(bf16[128,256]{1,0:T(8,128)(2,1)S(1)} %get-tuple-element.37), channel_id=1, source_target_pairs={{0,4},{4,0},{8,12},{12,8},{1,5},{5,1},{9,13},{13,9},{2,6},{6,2},{1... | collective-permute-start | bytes 196616 | tf_op jit(solution)/shard_map/ppermute | solution.py:265
  10.9 1.7 %collective-permute-start.5 = (bf16[128,256]{1,0:T(8,128)(2,1)S(1)}, bf16[128,256]{1,0:T(8,128)(2,1)S(1)}, u32[]{:S(2)}, u32[]{:S(2)}) collective-permute-start(bf16[128,256]{1,0:T(8,128)(2,1)S(1)} %get-tuple-element.38), channel_id=1, source_target_pairs={{0,8},{4,12},{8,0},{12,4},{1,9},{5,13},{9,1},{13,5},{2,10},{6,14},... | collective-permute-start | bytes 196616 | tf_op jit(solution)/shard_map/ppermute | solution.py:265
  12.6 2.3 %collective-permute-start.6 = (bf16[128,256]{1,0:T(8,128)(2,1)S(1)}, bf16[128,256]{1,0:T(8,128)(2,1)S(1)}, u32[]{:S(2)}, u32[]{:S(2)}) collective-permute-start(bf16[128,256]{1,0:T(8,128)(2,1)S(1)} %get-tuple-element.39), channel_id=1, source_target_pairs={{0,12},{4,8},{8,4},{12,0},{1,13},{5,9},{9,5},{13,1},{2,14},{6,10},... | collective-permute-start | bytes 196616 | tf_op jit(solution)/shard_map/ppermute | solution.py:265
  14.9 0.9 %shard_map.106 = (bf16[256,128]{1,0:T(8,128)(2,1)S(1)}, f32[2,512,128]{2,1,0:T(8,128)S(1)}) custom-call(f32[1,128]{1,0:T(1,128)S(1)} %get-tuple-element.28.gain, bf16[1024,256]{1,0:T(8,128)(2,1)S(1)} %get-tuple-element.29.forward, bf16[256,1024]{1,0:T(8,128)(2,1)S(1)} %get-tuple-element.30.backward, bf16[128,256]{1,0:T(8,128)(2,1)S(1)} %get-tuple-element.27.after.rest_0_, ...), custom_call_target="tpu_custom_call" | custom-call | tf_op jit(solution)/shard_map/pallas_call | solution.py:45
  15.8 1.6 %collective-permute-start.3 = (bf16[256,128]{1,0:T(8,128)(2,1)S(1)}, bf16[256,128]{1,0:T(8,128)(2,1)S(1)}, u32[]{:S(2)}, u32[]{:S(2)}) collective-permute-start(bf16[256,128]{1,0:T(8,128)(2,1)S(1)} %get-tuple-element.34), channel_id=1, source_target_pairs={{0,16},{16,0},{1,17},{17,1},{2,18},{18,2},{3,19},{19,3},{4,20},{20... | collective-permute-start | bytes 196616 | tf_op jit(solution)/shard_map/ppermute | solution.py:326
  17.5 1.3 %collective-permute-done.6.rest_3_ = bf16[128,256]{1,0:T(8,128)(2,1)S(1)} collective-permute-done((bf16[128,256]{1,0:T(8,128)(2,1)S(1)}, bf16[128,256]{1,0:T(8,128)(2,1)S(1)}, u32[]{:S(2)}, u32[]{:S(2)}) %collective-permute-start.6) | collective-permute-done | bytes 65568 | tf_op jit(solution)/shard_map/ppermute | solution.py:265
  18.8 0.4 %shard_map.107 = (f32[2,256,128]{2,1,0:T(8,128)S(1)}, f32[2,256,128]{2,1,0:T(8,128)S(1)}, f32[2,512,128]{2,1,0:T(8,128)S(1)}, f32[2,512,128]{2,1,0:T(8,128)S(1)}) custom-call(bf16[1024,256]{1,0:T(8,128)(2,1)S(1)} %get-tuple-element.29.forward, f32[2,512,128]{2,1,0:T(8,128)S(1)} %get-tuple-element.35.spectra, bf16[128,256]{1,0:T(8,128)(2,1)S(1)} %get-tuple-element.36.rest_0_, ...), custom_call_target="tpu_custom_call" | custom-call | tf_op jit(solution)/shard_map/pallas_call | solution.py:45
  19.2 1.0 %collective-permute-done.3.received = bf16[256,128]{1,0:T(8,128)(2,1)S(1)} collective-permute-done((bf16[256,128]{1,0:T(8,128)(2,1)S(1)}, bf16[256,128]{1,0:T(8,128)(2,1)S(1)}, u32[]{:S(2)}, u32[]{:S(2)}) %collective-permute-start.3) | collective-permute-done | bytes 65568 | tf_op jit(solution)/shard_map/ppermute | solution.py:326
  20.1 0.9 %shard_map.108 = (bf16[128,128]{1,0:T(8,128)(2,1)S(1)}, bf16[128,128]{1,0:T(8,128)(2,1)S(1)}, bf16[128,128]{1,0:T(8,128)(2,1)S(1)}, bf16[128,128]{1,0:T(8,128)(2,1)S(1)}) custom-call(f32[1,128]{1,0:T(1,128)S(1)} %get-tuple-element.28.gain, bf16[1024,256]{1,0:T(8,128)(2,1)S(1)} %get-tuple-element.29.forward, ...), custom_call_target="tpu_custom_call" | custom-call | tf_op jit(solution)/shard_map/pallas_call | solution.py:45
  21.0 1.1 %collective-permute-start.7 = (bf16[128,128]{1,0:T(8,128)(2,1)S(1)}, bf16[128,128]{1,0:T(8,128)(2,1)S(1)}, u32[]{:S(2)}, u32[]{:S(2)}) collective-permute-start(bf16[128,128]{1,0:T(8,128)(2,1)S(1)} %get-tuple-element.45), channel_id=1, source_target_pairs={{0,8},{4,12},{8,0},{12,4},{1,9},{5,13},{9,1},{13,5},{2,10},{6,14},... | collective-permute-start | bytes 98312 | tf_op jit(solution)/shard_map/ppermute | solution.py:265
  22.1 1.1 %collective-permute-start.8 = (bf16[128,128]{1,0:T(8,128)(2,1)S(1)}, bf16[128,128]{1,0:T(8,128)(2,1)S(1)}, u32[]{:S(2)}, u32[]{:S(2)}) collective-permute-start(bf16[128,128]{1,0:T(8,128)(2,1)S(1)} %get-tuple-element.46), channel_id=1, source_target_pairs={{0,12},{4,8},{8,4},{12,0},{1,13},{5,9},{9,5},{13,1},{2,14},{6,10},... | collective-permute-start | bytes 98312 | tf_op jit(solution)/shard_map/ppermute | solution.py:265
  23.2 1.4 %collective-permute-start.9 = (bf16[128,128]{1,0:T(8,128)(2,1)S(1)}, bf16[128,128]{1,0:T(8,128)(2,1)S(1)}, u32[]{:S(2)}, u32[]{:S(2)}) collective-permute-start(bf16[128,128]{1,0:T(8,128)(2,1)S(1)} %get-tuple-element.47), channel_id=1, source_target_pairs={{0,4},{4,0},{8,12},{12,8},{1,5},{5,1},{9,13},{13,9},{2,6},{6,2},{1... | collective-permute-start | bytes 98312 | tf_op jit(solution)/shard_map/ppermute | solution.py:265
  24.6 1.3 %collective-permute-done.7.rest_1_ = bf16[128,128]{1,0:T(8,128)(2,1)S(1)} collective-permute-done((bf16[128,128]{1,0:T(8,128)(2,1)S(1)}, bf16[128,128]{1,0:T(8,128)(2,1)S(1)}, u32[]{:S(2)}, u32[]{:S(2)}) %collective-permute-start.7) | collective-permute-done | bytes 32800 | tf_op jit(solution)/shard_map/ppermute | solution.py:265
  25.9 1.9 %collective-permute-done.8.rest_2_ = bf16[128,128]{1,0:T(8,128)(2,1)S(1)} collective-permute-done((bf16[128,128]{1,0:T(8,128)(2,1)S(1)}, bf16[128,128]{1,0:T(8,128)(2,1)S(1)}, u32[]{:S(2)}, u32[]{:S(2)}) %collective-permute-start.8) | collective-permute-done | bytes 32800 | tf_op jit(solution)/shard_map/ppermute | solution.py:265
  28.1 1.6 %collective-permute-start.11 = (f32[64,128]{1,0:T(8,128)S(1)}, f32[64,128]{1,0:T(8,128)S(1)}, u32[]{:S(2)}, u32[]{:S(2)}) collective-permute-start(f32[64,128]{1,0:T(8,128)S(1)} %get-tuple-element.50), channel_id=1, source_target_pairs={{0,2},{1,3},{2,0},{3,1},{4,6},{5,7},{6,4},{7,5},{8,10},{9,11},{10,... | collective-permute-start | bytes 98312 | tf_op jit(solution)/shard_map/ppermute | solution.py:265
  29.7 0.3 collective-permute-start.12
  30.0 0.7 %shard_map.109 = bf16[1,128,256]{2,1,0:T(8,128)(2,1)} custom-call(bf16[128,128]{1,0:T(8,128)(2,1)S(1)} %get-tuple-element.44.rest_0_, bf16[128,128]{1,0:T(8,128)(2,1)S(1)} %collective-permute-done.7.rest_1_, bf16[128,128]{1,0:T(8,128)(2,1)S(1)} %collective-permute-done.8.rest_2_, bf16[128,128]{1,0:T(8,128)(2,1)S(1)} %collective-permute-done.9.rest_3_), custom_call_target="tpu_custom_call" | custom-call | tf_op jit(solution)/shard_map/pallas_call | solution.py:45
  30.7 1.0 %collective-permute-done.10.refs_1_ = f32[64,128]{1,0:T(8,128)S(1)} collective-permute-done((f32[64,128]{1,0:T(8,128)S(1)}, f32[64,128]{1,0:T(8,128)S(1)}, u32[]{:S(2)}, u32[]{:S(2)}) %collective-permute-start.10) | collective-permute-done | bytes 32800 | tf_op jit(solution)/shard_map/ppermute | solution.py:265
  31.7 0.4 %collective-permute-done.11.refs_2_ = f32[64,128]{1,0:T(8,128)S(1)} collective-permute-done((f32[64,128]{1,0:T(8,128)S(1)}, f32[64,128]{1,0:T(8,128)S(1)}, u32[]{:S(2)}, u32[]{:S(2)}) %collective-permute-start.11) | collective-permute-done | bytes 32800 | tf_op jit(solution)/shard_map/ppermute | solution.py:265
  32.1 0.6 %shard_map.111 = f32[64,128]{1,0:T(8,128)} custom-call(f32[64,128]{1,0:T(8,128)S(1)} %get-tuple-element.48.refs_0_, f32[64,128]{1,0:T(8,128)S(1)} %collective-permute-done.10.refs_1_, f32[64,128]{1,0:T(8,128)S(1)} %collective-permute-done.11.refs_2_, f32[64,128]{1,0:T(8,128)S(1)} %collective-permute-done.12.refs_3_), custom_call_target="tpu_custom_call" | custom-call | tf_op jit(solution)/shard_map/pallas_call | solution.py:45
  (10 shorter events, 0.6 us)
Async XLA Ops:
  1.9 10.7 %collective-permute-start = (bf16[128,256]{1,0:T(8,128)(2,1)S(1)}, bf16[128,256]{1,0:T(8,128)(2,1)S(1)}, u32[]{:S(2)}, u32[]{:S(2)}) collective-permute-start(bf16[128,256]{1,0:T(8,128)(2,1)S(1)} %get-tuple-element.31), channel_id=1, source_target_pairs={{0,8},{4,12},{8,0},{12,4},{1,9},{5,13},{9,1},{13,5},{2,10},{6,14},... | collective-permute-start | bytes 196616 | tf_op jit(solution)/shard_map/ppermute | solution.py:265
  6.0 8.9 %collective-permute-start.1 = (bf16[128,256]{1,0:T(8,128)(2,1)S(1)}, bf16[128,256]{1,0:T(8,128)(2,1)S(1)}, u32[]{:S(2)}, u32[]{:S(2)}) collective-permute-start(bf16[128,256]{1,0:T(8,128)(2,1)S(1)} %get-tuple-element.32), channel_id=1, source_target_pairs={{0,12},{4,8},{8,4},{12,0},{1,13},{5,9},{9,5},{13,1},{2,14},{6,10},... | collective-permute-start | bytes 196616 | tf_op jit(solution)/shard_map/ppermute | solution.py:265
  7.3 7.5 %collective-permute-start.2 = (bf16[128,256]{1,0:T(8,128)(2,1)S(1)}, bf16[128,256]{1,0:T(8,128)(2,1)S(1)}, u32[]{:S(2)}, u32[]{:S(2)}) collective-permute-start(bf16[128,256]{1,0:T(8,128)(2,1)S(1)} %get-tuple-element.33), channel_id=1, source_target_pairs={{0,4},{4,0},{8,12},{12,8},{1,5},{5,1},{9,13},{13,9},{2,6},{6,2},{1... | collective-permute-start | bytes 196616 | tf_op jit(solution)/shard_map/ppermute | solution.py:265
  9.0 8.3 %collective-permute-start.4 = (bf16[128,256]{1,0:T(8,128)(2,1)S(1)}, bf16[128,256]{1,0:T(8,128)(2,1)S(1)}, u32[]{:S(2)}, u32[]{:S(2)}) collective-permute-start(bf16[128,256]{1,0:T(8,128)(2,1)S(1)} %get-tuple-element.37), channel_id=1, source_target_pairs={{0,4},{4,0},{8,12},{12,8},{1,5},{5,1},{9,13},{13,9},{2,6},{6,2},{1... | collective-permute-start | bytes 196616 | tf_op jit(solution)/shard_map/ppermute | solution.py:265
  10.9 6.6 %collective-permute-start.5 = (bf16[128,256]{1,0:T(8,128)(2,1)S(1)}, bf16[128,256]{1,0:T(8,128)(2,1)S(1)}, u32[]{:S(2)}, u32[]{:S(2)}) collective-permute-start(bf16[128,256]{1,0:T(8,128)(2,1)S(1)} %get-tuple-element.38), channel_id=1, source_target_pairs={{0,8},{4,12},{8,0},{12,4},{1,9},{5,13},{9,1},{13,5},{2,10},{6,14},... | collective-permute-start | bytes 196616 | tf_op jit(solution)/shard_map/ppermute | solution.py:265
  12.6 6.2 %collective-permute-start.6 = (bf16[128,256]{1,0:T(8,128)(2,1)S(1)}, bf16[128,256]{1,0:T(8,128)(2,1)S(1)}, u32[]{:S(2)}, u32[]{:S(2)}) collective-permute-start(bf16[128,256]{1,0:T(8,128)(2,1)S(1)} %get-tuple-element.39), channel_id=1, source_target_pairs={{0,12},{4,8},{8,4},{12,0},{1,13},{5,9},{9,5},{13,1},{2,14},{6,10},... | collective-permute-start | bytes 196616 | tf_op jit(solution)/shard_map/ppermute | solution.py:265
  15.8 4.3 %collective-permute-start.3 = (bf16[256,128]{1,0:T(8,128)(2,1)S(1)}, bf16[256,128]{1,0:T(8,128)(2,1)S(1)}, u32[]{:S(2)}, u32[]{:S(2)}) collective-permute-start(bf16[256,128]{1,0:T(8,128)(2,1)S(1)} %get-tuple-element.34), channel_id=1, source_target_pairs={{0,16},{16,0},{1,17},{17,1},{2,18},{18,2},{3,19},{19,3},{4,20},{20... | collective-permute-start | bytes 196616 | tf_op jit(solution)/shard_map/ppermute | solution.py:326
  21.0 4.9 %collective-permute-start.7 = (bf16[128,128]{1,0:T(8,128)(2,1)S(1)}, bf16[128,128]{1,0:T(8,128)(2,1)S(1)}, u32[]{:S(2)}, u32[]{:S(2)}) collective-permute-start(bf16[128,128]{1,0:T(8,128)(2,1)S(1)} %get-tuple-element.45), channel_id=1, source_target_pairs={{0,8},{4,12},{8,0},{12,4},{1,9},{5,13},{9,1},{13,5},{2,10},{6,14},... | collective-permute-start | bytes 98312 | tf_op jit(solution)/shard_map/ppermute | solution.py:265
  22.1 5.7 %collective-permute-start.8 = (bf16[128,128]{1,0:T(8,128)(2,1)S(1)}, bf16[128,128]{1,0:T(8,128)(2,1)S(1)}, u32[]{:S(2)}, u32[]{:S(2)}) collective-permute-start(bf16[128,128]{1,0:T(8,128)(2,1)S(1)} %get-tuple-element.46), channel_id=1, source_target_pairs={{0,12},{4,8},{8,4},{12,0},{1,13},{5,9},{9,5},{13,1},{2,14},{6,10},... | collective-permute-start | bytes 98312 | tf_op jit(solution)/shard_map/ppermute | solution.py:265
  23.2 4.6 %collective-permute-start.9 = (bf16[128,128]{1,0:T(8,128)(2,1)S(1)}, bf16[128,128]{1,0:T(8,128)(2,1)S(1)}, u32[]{:S(2)}, u32[]{:S(2)}) collective-permute-start(bf16[128,128]{1,0:T(8,128)(2,1)S(1)} %get-tuple-element.47), channel_id=1, source_target_pairs={{0,4},{4,0},{8,12},{12,8},{1,5},{5,1},{9,13},{13,9},{2,6},{6,2},{1... | collective-permute-start | bytes 98312 | tf_op jit(solution)/shard_map/ppermute | solution.py:265
  28.0 3.7 %collective-permute-start.10 = (f32[64,128]{1,0:T(8,128)S(1)}, f32[64,128]{1,0:T(8,128)S(1)}, u32[]{:S(2)}, u32[]{:S(2)}) collective-permute-start(f32[64,128]{1,0:T(8,128)S(1)} %get-tuple-element.49), channel_id=1, source_target_pairs={{0,3},{1,2},{2,1},{3,0},{4,7},{5,6},{6,5},{7,4},{8,11},{9,10},{10,... | collective-permute-start | bytes 98312 | tf_op jit(solution)/shard_map/ppermute | solution.py:265
  28.1 4.0 %collective-permute-start.11 = (f32[64,128]{1,0:T(8,128)S(1)}, f32[64,128]{1,0:T(8,128)S(1)}, u32[]{:S(2)}, u32[]{:S(2)}) collective-permute-start(f32[64,128]{1,0:T(8,128)S(1)} %get-tuple-element.50), channel_id=1, source_target_pairs={{0,2},{1,3},{2,0},{3,1},{4,6},{5,7},{6,4},{7,5},{8,10},{9,11},{10,... | collective-permute-start | bytes 98312 | tf_op jit(solution)/shard_map/ppermute | solution.py:265
  29.7 2.4 %collective-permute-start.12 = (f32[64,128]{1,0:T(8,128)S(1)}, f32[64,128]{1,0:T(8,128)S(1)}, u32[]{:S(2)}, u32[]{:S(2)}) collective-permute-start(f32[64,128]{1,0:T(8,128)S(1)} %get-tuple-element.51), channel_id=1, source_target_pairs={{0,1},{1,0},{2,3},{3,2},{4,5},{5,4},{6,7},{7,6},{8,9},{9,8},{10,11... | collective-permute-start | bytes 98312 | tf_op jit(solution)/shard_map/ppermute | solution.py:265

commit v6 on v5

--- a/solution.py
+++ b/solution.py
@@ -248,7 +248,7 @@
     for step, chunk in zip([0, *middle_first(count)], chunks):
         stage[seq_index ^ step] = chunk[...]
     lag_grad = jnp.concatenate([stage[block][:, unit:] for block in range(count)], axis=1)
-    lag_stage[...] = lag_grad.astype(F32).T
+    lag_stage[...] = lag_grad.astype(F32).T.astype(BF16)
     for step, lag in enumerate(lags):
         width = lag.shape[0]
         lag[...] = lag_stage[pl.ds(pl.multiple_of((chan_index ^ step) * width, width), width), :]
@@ -256,7 +256,7 @@
 
 def add_up(*refs):
     *lags, out = refs
-    out[...] = functools.reduce(jnp.add, [lag[...] for lag in lags])
+    out[...] = functools.reduce(jnp.add, [lag[...].astype(F32) for lag in lags])
 
 
 def exchange(chunks, axis, steps):
@@ -342,8 +342,8 @@
     lag_width = width // chan_count
     lags = call(
         unpack_lags,
-        [struct((lag_width, rows), F32)] * chan_count,
-        [sorted_chunks, struct((width, rows), F32)],
+        [struct((lag_width, rows), BF16)] * chan_count,
+        [sorted_chunks, struct((width, rows), BF16)],
     )(*result)
     lags = exchange(lags, "chan", far_first(chan_count))
     (grad_out,) = call(unpack_gradient, [struct((1, rows, width), BF16)], [sorted_chunks])(*result)

time: 32.9 us -> 32.7 us (level)
  no operation moved by 1% of the time
where the time goes in v6:
time: 32.7 us; the launch traced here: 32.5 us
  starting transfers between devices  18.5 us (57%)
  waiting for transfers between devices  6.83 us (21%)
  Pallas kernels  6.46 us (20%)
  between operations  0.69 us (2%)
    ppermute x12, starting transfers between devices, exchange(): lax.ppermute(chunks[step], axis, [(i, i ^ step) for i in range(size)])  17 us
    pallas_call x8, Pallas kernels, run(): pl.pallas_call(kernel, out_shape=out_shape, in_specs=[pl.BlockSpec(memory...  6.46 us
    ppermute x12, waiting for transfers between devices, exchange(): lax.ppermute(chunks[step], axis, [(i, i ^ step) for i in range(size)])  5.87 us
    ppermute x1, starting transfers between devices, body(): received = lax.ppermute(gradient, 'section', ring)  1.56 us
    ppermute x1, waiting for transfers between devices, body(): received = lax.ppermute(gradient, 'section', ring)  0.96 us
  transfers between devices with their start and end apart: 13, of which 7 were waited for; matrix products, arithmetic and copies ran while one was open for 0% of the time, Pallas kernels for 11%

profile of v6, /device:TPU:0, one launch (start us, length us, event | category | flops | bytes accessed | tf_op | source)
XLA Modules:
  0.0 32.5 jit_solution(11742491752623202821)
XLA Ops:
  0.6 1.2 %shard_map.104 = (bf16[128,256]{1,0:T(8,128)(2,1)S(1)}, bf16[128,256]{1,0:T(8,128)(2,1)S(1)}, bf16[128,256]{1,0:T(8,128)(2,1)S(1)}, bf16[128,256]{1,0:T(8,128)(2,1)S(1)}) custom-call(bf16[1,2,128,256]{3,2,1,0:T(8,128)(2,1)} %post.3, bf16[1,128,256]{2,1,0:T(8,128)(2,1)} %held.1, bf16[128,256]{1,0:T(8,128)(2,1)} %loss.1, bf16[1,2,128,256]{3,2,1,0:T(8,128)(2,1)} %pre.3, ...), custom_call_target="tpu_custom_call" | custom-call | tf_op jit(solution)/shard_map/pallas_call | solution.py:45
  1.9 4.1 %collective-permute-start = (bf16[128,256]{1,0:T(8,128)(2,1)S(1)}, bf16[128,256]{1,0:T(8,128)(2,1)S(1)}, u32[]{:S(2)}, u32[]{:S(2)}) collective-permute-start(bf16[128,256]{1,0:T(8,128)(2,1)S(1)} %get-tuple-element.31), channel_id=1, source_target_pairs={{0,8},{4,12},{8,0},{12,4},{1,9},{5,13},{9,1},{13,5},{2,10},{6,14},... | collective-permute-start | bytes 196616 | tf_op jit(solution)/shard_map/ppermute | solution.py:265
  6.0 1.3 %collective-permute-start.1 = (bf16[128,256]{1,0:T(8,128)(2,1)S(1)}, bf16[128,256]{1,0:T(8,128)(2,1)S(1)}, u32[]{:S(2)}, u32[]{:S(2)}) collective-permute-start(bf16[128,256]{1,0:T(8,128)(2,1)S(1)} %get-tuple-element.32), channel_id=1, source_target_pairs={{0,12},{4,8},{8,4},{12,0},{1,13},{5,9},{9,5},{13,1},{2,14},{6,10},... | collective-permute-start | bytes 196616 | tf_op jit(solution)/shard_map/ppermute | solution.py:265
  7.6 1.5 %shard_map.105 = (bf16[128,256]{1,0:T(8,128)(2,1)S(1)}, bf16[128,256]{1,0:T(8,128)(2,1)S(1)}, bf16[128,256]{1,0:T(8,128)(2,1)S(1)}, bf16[128,256]{1,0:T(8,128)(2...) custom-call(bf16[128,256]{1,0:T(8,128)(2,1)S(1)} %get-tuple-element.27.after.rest_0_, ...), custom_call_target="tpu_custom_call" | custom-call | tf_op jit(solution)/shard_map/pallas_call | solution.py:45
  9.0 1.9 %collective-permute-start.4 = (bf16[128,256]{1,0:T(8,128)(2,1)S(1)}, bf16[128,256]{1,0:T(8,128)(2,1)S(1)}, u32[]{:S(2)}, u32[]{:S(2)}) collective-permute-start(bf16[128,256]{1,0:T(8,128)(2,1)S(1)} %get-tuple-element.37), channel_id=1, source_target_pairs={{0,4},{4,0},{8,12},{12,8},{1,5},{5,1},{9,13},{13,9},{2,6},{6,2},{1... | collective-permute-start | bytes 196616 | tf_op jit(solution)/shard_map/ppermute | solution.py:265
  10.9 1.7 %collective-permute-start.5 = (bf16[128,256]{1,0:T(8,128)(2,1)S(1)}, bf16[128,256]{1,0:T(8,128)(2,1)S(1)}, u32[]{:S(2)}, u32[]{:S(2)}) collective-permute-start(bf16[128,256]{1,0:T(8,128)(2,1)S(1)} %get-tuple-element.38), channel_id=1, source_target_pairs={{0,8},{4,12},{8,0},{12,4},{1,9},{5,13},{9,1},{13,5},{2,10},{6,14},... | collective-permute-start | bytes 196616 | tf_op jit(solution)/shard_map/ppermute | solution.py:265
  12.6 2.3 %collective-permute-start.6 = (bf16[128,256]{1,0:T(8,128)(2,1)S(1)}, bf16[128,256]{1,0:T(8,128)(2,1)S(1)}, u32[]{:S(2)}, u32[]{:S(2)}) collective-permute-start(bf16[128,256]{1,0:T(8,128)(2,1)S(1)} %get-tuple-element.39), channel_id=1, source_target_pairs={{0,12},{4,8},{8,4},{12,0},{1,13},{5,9},{9,5},{13,1},{2,14},{6,10},... | collective-permute-start | bytes 196616 | tf_op jit(solution)/shard_map/ppermute | solution.py:265
  14.9 0.9 %shard_map.106 = (bf16[256,128]{1,0:T(8,128)(2,1)S(1)}, f32[2,512,128]{2,1,0:T(8,128)S(1)}) custom-call(f32[1,128]{1,0:T(1,128)S(1)} %get-tuple-element.28.gain, bf16[1024,256]{1,0:T(8,128)(2,1)S(1)} %get-tuple-element.29.forward, bf16[256,1024]{1,0:T(8,128)(2,1)S(1)} %get-tuple-element.30.backward, bf16[128,256]{1,0:T(8,128)(2,1)S(1)} %get-tuple-element.27.after.rest_0_, ...), custom_call_target="tpu_custom_call" | custom-call | tf_op jit(solution)/shard_map/pallas_call | solution.py:45
  15.8 1.6 %collective-permute-start.3 = (bf16[256,128]{1,0:T(8,128)(2,1)S(1)}, bf16[256,128]{1,0:T(8,128)(2,1)S(1)}, u32[]{:S(2)}, u32[]{:S(2)}) collective-permute-start(bf16[256,128]{1,0:T(8,128)(2,1)S(1)} %get-tuple-element.34), channel_id=1, source_target_pairs={{0,16},{16,0},{1,17},{17,1},{2,18},{18,2},{3,19},{19,3},{4,20},{20... | collective-permute-start | bytes 196616 | tf_op jit(solution)/shard_map/ppermute | solution.py:326
  17.5 1.3 %collective-permute-done.6.rest_3_ = bf16[128,256]{1,0:T(8,128)(2,1)S(1)} collective-permute-done((bf16[128,256]{1,0:T(8,128)(2,1)S(1)}, bf16[128,256]{1,0:T(8,128)(2,1)S(1)}, u32[]{:S(2)}, u32[]{:S(2)}) %collective-permute-start.6) | collective-permute-done | bytes 65568 | tf_op jit(solution)/shard_map/ppermute | solution.py:265
  18.8 0.4 %shard_map.107 = (f32[2,256,128]{2,1,0:T(8,128)S(1)}, f32[2,256,128]{2,1,0:T(8,128)S(1)}, f32[2,512,128]{2,1,0:T(8,128)S(1)}, f32[2,512,128]{2,1,0:T(8,128)S(1)}) custom-call(bf16[1024,256]{1,0:T(8,128)(2,1)S(1)} %get-tuple-element.29.forward, f32[2,512,128]{2,1,0:T(8,128)S(1)} %get-tuple-element.35.spectra, bf16[128,256]{1,0:T(8,128)(2,1)S(1)} %get-tuple-element.36.rest_0_, ...), custom_call_target="tpu_custom_call" | custom-call | tf_op jit(solution)/shard_map/pallas_call | solution.py:45
  19.2 1.0 %collective-permute-done.3.received = bf16[256,128]{1,0:T(8,128)(2,1)S(1)} collective-permute-done((bf16[256,128]{1,0:T(8,128)(2,1)S(1)}, bf16[256,128]{1,0:T(8,128)(2,1)S(1)}, u32[]{:S(2)}, u32[]{:S(2)}) %collective-permute-start.3) | collective-permute-done | bytes 65568 | tf_op jit(solution)/shard_map/ppermute | solution.py:326
  20.1 0.9 %shard_map.108 = (bf16[128,128]{1,0:T(8,128)(2,1)S(1)}, bf16[128,128]{1,0:T(8,128)(2,1)S(1)}, bf16[128,128]{1,0:T(8,128)(2,1)S(1)}, bf16[128,128]{1,0:T(8,128)(2,1)S(1)}) custom-call(f32[1,128]{1,0:T(1,128)S(1)} %get-tuple-element.28.gain, bf16[1024,256]{1,0:T(8,128)(2,1)S(1)} %get-tuple-element.29.forward, ...), custom_call_target="tpu_custom_call" | custom-call | tf_op jit(solution)/shard_map/pallas_call | solution.py:45
  21.0 1.1 %collective-permute-start.7 = (bf16[128,128]{1,0:T(8,128)(2,1)S(1)}, bf16[128,128]{1,0:T(8,128)(2,1)S(1)}, u32[]{:S(2)}, u32[]{:S(2)}) collective-permute-start(bf16[128,128]{1,0:T(8,128)(2,1)S(1)} %get-tuple-element.45), channel_id=1, source_target_pairs={{0,8},{4,12},{8,0},{12,4},{1,9},{5,13},{9,1},{13,5},{2,10},{6,14},... | collective-permute-start | bytes 98312 | tf_op jit(solution)/shard_map/ppermute | solution.py:265
  22.1 1.1 %collective-permute-start.8 = (bf16[128,128]{1,0:T(8,128)(2,1)S(1)}, bf16[128,128]{1,0:T(8,128)(2,1)S(1)}, u32[]{:S(2)}, u32[]{:S(2)}) collective-permute-start(bf16[128,128]{1,0:T(8,128)(2,1)S(1)} %get-tuple-element.46), channel_id=1, source_target_pairs={{0,12},{4,8},{8,4},{12,0},{1,13},{5,9},{9,5},{13,1},{2,14},{6,10},... | collective-permute-start | bytes 98312 | tf_op jit(solution)/shard_map/ppermute | solution.py:265
  23.2 1.4 %collective-permute-start.9 = (bf16[128,128]{1,0:T(8,128)(2,1)S(1)}, bf16[128,128]{1,0:T(8,128)(2,1)S(1)}, u32[]{:S(2)}, u32[]{:S(2)}) collective-permute-start(bf16[128,128]{1,0:T(8,128)(2,1)S(1)} %get-tuple-element.47), channel_id=1, source_target_pairs={{0,4},{4,0},{8,12},{12,8},{1,5},{5,1},{9,13},{13,9},{2,6},{6,2},{1... | collective-permute-start | bytes 98312 | tf_op jit(solution)/shard_map/ppermute | solution.py:265
  24.6 1.3 %collective-permute-done.7.rest_1_ = bf16[128,128]{1,0:T(8,128)(2,1)S(1)} collective-permute-done((bf16[128,128]{1,0:T(8,128)(2,1)S(1)}, bf16[128,128]{1,0:T(8,128)(2,1)S(1)}, u32[]{:S(2)}, u32[]{:S(2)}) %collective-permute-start.7) | collective-permute-done | bytes 32800 | tf_op jit(solution)/shard_map/ppermute | solution.py:265
  25.9 1.9 %collective-permute-done.8.rest_2_ = bf16[128,128]{1,0:T(8,128)(2,1)S(1)} collective-permute-done((bf16[128,128]{1,0:T(8,128)(2,1)S(1)}, bf16[128,128]{1,0:T(8,128)(2,1)S(1)}, u32[]{:S(2)}, u32[]{:S(2)}) %collective-permute-start.8) | collective-permute-done | bytes 32800 | tf_op jit(solution)/shard_map/ppermute | solution.py:265
  28.1 1.6 %collective-permute-start.11 = (bf16[64,128]{1,0:T(8,128)(2,1)S(1)}, bf16[64,128]{1,0:T(8,128)(2,1)S(1)}, u32[]{:S(2)}, u32[]{:S(2)}) collective-permute-start(bf16[64,128]{1,0:T(8,128)(2,1)S(1)} %get-tuple-element.50), channel_id=1, source_target_pairs={{0,2},{1,3},{2,0},{3,1},{4,6},{5,7},{6,4},{7,5},{8,10},{9,11},{10,... | collective-permute-start | bytes 49160 | tf_op jit(solution)/shard_map/ppermute | solution.py:265
  29.7 0.3 collective-permute-start.12
  29.9 0.7 %shard_map.109 = bf16[1,128,256]{2,1,0:T(8,128)(2,1)} custom-call(bf16[128,128]{1,0:T(8,128)(2,1)S(1)} %get-tuple-element.44.rest_0_, bf16[128,128]{1,0:T(8,128)(2,1)S(1)} %collective-permute-done.7.rest_1_, bf16[128,128]{1,0:T(8,128)(2,1)S(1)} %collective-permute-done.8.rest_2_, bf16[128,128]{1,0:T(8,128)(2,1)S(1)} %collective-permute-done.9.rest_3_), custom_call_target="tpu_custom_call" | custom-call | tf_op jit(solution)/shard_map/pallas_call | solution.py:45
  30.7 0.7 %collective-permute-done.10.refs_1_ = bf16[64,128]{1,0:T(8,128)(2,1)S(1)} collective-permute-done((bf16[64,128]{1,0:T(8,128)(2,1)S(1)}, bf16[64,128]{1,0:T(8,128)(2,1)S(1)}, u32[]{:S(2)}, u32[]{:S(2)}) %collective-permute-start.10) | collective-permute-done | bytes 16416 | tf_op jit(solution)/shard_map/ppermute | solution.py:265
  31.3 0.6 %collective-permute-done.11.refs_2_ = bf16[64,128]{1,0:T(8,128)(2,1)S(1)} collective-permute-done((bf16[64,128]{1,0:T(8,128)(2,1)S(1)}, bf16[64,128]{1,0:T(8,128)(2,1)S(1)}, u32[]{:S(2)}, u32[]{:S(2)}) %collective-permute-start.11) | collective-permute-done | bytes 16416 | tf_op jit(solution)/shard_map/ppermute | solution.py:265
  31.9 0.6 %shard_map.111 = f32[64,128]{1,0:T(8,128)} custom-call(bf16[64,128]{1,0:T(8,128)(2,1)S(1)} %get-tuple-element.48.refs_0_, bf16[64,128]{1,0:T(8,128)(2,1)S(1)} %collective-permute-done.10.refs_1_, bf16[64,128]{1,0:T(8,128)(2,1)S(1)} %collective-permute-done.11.refs_2_, bf16[64,128]{1,0:T(8,128)(2,1)S(1)} %collective-permute-done.12.refs_3_), custom_call_target="tpu_custom_call" | custom-call | tf_op jit(solution)/shard_map/pallas_call | solution.py:45
  (10 shorter events, 0.6 us)
Async XLA Ops:
  1.9 10.7 %collective-permute-start = (bf16[128,256]{1,0:T(8,128)(2,1)S(1)}, bf16[128,256]{1,0:T(8,128)(2,1)S(1)}, u32[]{:S(2)}, u32[]{:S(2)}) collective-permute-start(bf16[128,256]{1,0:T(8,128)(2,1)S(1)} %get-tuple-element.31), channel_id=1, source_target_pairs={{0,8},{4,12},{8,0},{12,4},{1,9},{5,13},{9,1},{13,5},{2,10},{6,14},... | collective-permute-start | bytes 196616 | tf_op jit(solution)/shard_map/ppermute | solution.py:265
  6.0 8.9 %collective-permute-start.1 = (bf16[128,256]{1,0:T(8,128)(2,1)S(1)}, bf16[128,256]{1,0:T(8,128)(2,1)S(1)}, u32[]{:S(2)}, u32[]{:S(2)}) collective-permute-start(bf16[128,256]{1,0:T(8,128)(2,1)S(1)} %get-tuple-element.32), channel_id=1, source_target_pairs={{0,12},{4,8},{8,4},{12,0},{1,13},{5,9},{9,5},{13,1},{2,14},{6,10},... | collective-permute-start | bytes 196616 | tf_op jit(solution)/shard_map/ppermute | solution.py:265
  7.3 7.5 %collective-permute-start.2 = (bf16[128,256]{1,0:T(8,128)(2,1)S(1)}, bf16[128,256]{1,0:T(8,128)(2,1)S(1)}, u32[]{:S(2)}, u32[]{:S(2)}) collective-permute-start(bf16[128,256]{1,0:T(8,128)(2,1)S(1)} %get-tuple-element.33), channel_id=1, source_target_pairs={{0,4},{4,0},{8,12},{12,8},{1,5},{5,1},{9,13},{13,9},{2,6},{6,2},{1... | collective-permute-start | bytes 196616 | tf_op jit(solution)/shard_map/ppermute | solution.py:265
  9.0 8.3 %collective-permute-start.4 = (bf16[128,256]{1,0:T(8,128)(2,1)S(1)}, bf16[128,256]{1,0:T(8,128)(2,1)S(1)}, u32[]{:S(2)}, u32[]{:S(2)}) collective-permute-start(bf16[128,256]{1,0:T(8,128)(2,1)S(1)} %get-tuple-element.37), channel_id=1, source_target_pairs={{0,4},{4,0},{8,12},{12,8},{1,5},{5,1},{9,13},{13,9},{2,6},{6,2},{1... | collective-permute-start | bytes 196616 | tf_op jit(solution)/shard_map/ppermute | solution.py:265
  10.9 6.6 %collective-permute-start.5 = (bf16[128,256]{1,0:T(8,128)(2,1)S(1)}, bf16[128,256]{1,0:T(8,128)(2,1)S(1)}, u32[]{:S(2)}, u32[]{:S(2)}) collective-permute-start(bf16[128,256]{1,0:T(8,128)(2,1)S(1)} %get-tuple-element.38), channel_id=1, source_target_pairs={{0,8},{4,12},{8,0},{12,4},{1,9},{5,13},{9,1},{13,5},{2,10},{6,14},... | collective-permute-start | bytes 196616 | tf_op jit(solution)/shard_map/ppermute | solution.py:265
  12.6 6.2 %collective-permute-start.6 = (bf16[128,256]{1,0:T(8,128)(2,1)S(1)}, bf16[128,256]{1,0:T(8,128)(2,1)S(1)}, u32[]{:S(2)}, u32[]{:S(2)}) collective-permute-start(bf16[128,256]{1,0:T(8,128)(2,1)S(1)} %get-tuple-element.39), channel_id=1, source_target_pairs={{0,12},{4,8},{8,4},{12,0},{1,13},{5,9},{9,5},{13,1},{2,14},{6,10},... | collective-permute-start | bytes 196616 | tf_op jit(solution)/shard_map/ppermute | solution.py:265
  15.8 4.3 %collective-permute-start.3 = (bf16[256,128]{1,0:T(8,128)(2,1)S(1)}, bf16[256,128]{1,0:T(8,128)(2,1)S(1)}, u32[]{:S(2)}, u32[]{:S(2)}) collective-permute-start(bf16[256,128]{1,0:T(8,128)(2,1)S(1)} %get-tuple-element.34), channel_id=1, source_target_pairs={{0,16},{16,0},{1,17},{17,1},{2,18},{18,2},{3,19},{19,3},{4,20},{20... | collective-permute-start | bytes 196616 | tf_op jit(solution)/shard_map/ppermute | solution.py:326
  21.0 4.9 %collective-permute-start.7 = (bf16[128,128]{1,0:T(8,128)(2,1)S(1)}, bf16[128,128]{1,0:T(8,128)(2,1)S(1)}, u32[]{:S(2)}, u32[]{:S(2)}) collective-permute-start(bf16[128,128]{1,0:T(8,128)(2,1)S(1)} %get-tuple-element.45), channel_id=1, source_target_pairs={{0,8},{4,12},{8,0},{12,4},{1,9},{5,13},{9,1},{13,5},{2,10},{6,14},... | collective-permute-start | bytes 98312 | tf_op jit(solution)/shard_map/ppermute | solution.py:265
  22.1 5.7 %collective-permute-start.8 = (bf16[128,128]{1,0:T(8,128)(2,1)S(1)}, bf16[128,128]{1,0:T(8,128)(2,1)S(1)}, u32[]{:S(2)}, u32[]{:S(2)}) collective-permute-start(bf16[128,128]{1,0:T(8,128)(2,1)S(1)} %get-tuple-element.46), channel_id=1, source_target_pairs={{0,12},{4,8},{8,4},{12,0},{1,13},{5,9},{9,5},{13,1},{2,14},{6,10},... | collective-permute-start | bytes 98312 | tf_op jit(solution)/shard_map/ppermute | solution.py:265
  23.2 4.6 %collective-permute-start.9 = (bf16[128,128]{1,0:T(8,128)(2,1)S(1)}, bf16[128,128]{1,0:T(8,128)(2,1)S(1)}, u32[]{:S(2)}, u32[]{:S(2)}) collective-permute-start(bf16[128,128]{1,0:T(8,128)(2,1)S(1)} %get-tuple-element.47), channel_id=1, source_target_pairs={{0,4},{4,0},{8,12},{12,8},{1,5},{5,1},{9,13},{13,9},{2,6},{6,2},{1... | collective-permute-start | bytes 98312 | tf_op jit(solution)/shard_map/ppermute | solution.py:265
  28.0 3.3 %collective-permute-start.10 = (bf16[64,128]{1,0:T(8,128)(2,1)S(1)}, bf16[64,128]{1,0:T(8,128)(2,1)S(1)}, u32[]{:S(2)}, u32[]{:S(2)}) collective-permute-start(bf16[64,128]{1,0:T(8,128)(2,1)S(1)} %get-tuple-element.49), channel_id=1, source_target_pairs={{0,3},{1,2},{2,1},{3,0},{4,7},{5,6},{6,5},{7,4},{8,11},{9,10},{10,... | collective-permute-start | bytes 49160 | tf_op jit(solution)/shard_map/ppermute | solution.py:265
  28.1 3.8 %collective-permute-start.11 = (bf16[64,128]{1,0:T(8,128)(2,1)S(1)}, bf16[64,128]{1,0:T(8,128)(2,1)S(1)}, u32[]{:S(2)}, u32[]{:S(2)}) collective-permute-start(bf16[64,128]{1,0:T(8,128)(2,1)S(1)} %get-tuple-element.50), channel_id=1, source_target_pairs={{0,2},{1,3},{2,0},{3,1},{4,6},{5,7},{6,4},{7,5},{8,10},{9,11},{10,... | collective-permute-start | bytes 49160 | tf_op jit(solution)/shard_map/ppermute | solution.py:265
  29.7 2.2 %collective-permute-start.12 = (bf16[64,128]{1,0:T(8,128)(2,1)S(1)}, bf16[64,128]{1,0:T(8,128)(2,1)S(1)}, u32[]{:S(2)}, u32[]{:S(2)}) collective-permute-start(bf16[64,128]{1,0:T(8,128)(2,1)S(1)} %get-tuple-element.51), channel_id=1, source_target_pairs={{0,1},{1,0},{2,3},{3,2},{4,5},{5,4},{6,7},{7,6},{8,9},{9,8},{10,11... | collective-permute-start | bytes 49160 | tf_op jit(solution)/shard_map/ppermute | solution.py:265

commit v7 on v6

--- a/solution.py
+++ b/solution.py
@@ -234,7 +234,7 @@
     count = stage.shape[0]
     unit = stage.shape[2] // 2
     seq_index = lax.axis_index("seq")
-    for step, chunk in zip([0, *middle_first(count)], chunks):
+    for step, chunk in zip([0, *farthest_first(count)], chunks):
         stage[seq_index ^ step] = chunk[...]
     grad[0] = jnp.concatenate([stage[block][:, :unit] for block in range(count)], axis=1)
 
@@ -245,7 +245,7 @@
     chunks, lags = refs[:count], refs[count:]
     unit = stage.shape[2] // 2
     seq_index, chan_index = lax.axis_index("seq"), lax.axis_index("chan")
-    for step, chunk in zip([0, *middle_first(count)], chunks):
+    for step, chunk in zip([0, *farthest_first(count)], chunks):
         stage[seq_index ^ step] = chunk[...]
     lag_grad = jnp.concatenate([stage[block][:, unit:] for block in range(count)], axis=1)
     lag_stage[...] = lag_grad.astype(F32).T.astype(BF16)
@@ -268,6 +268,10 @@
 
 def middle_first(size):
     return [*range(2, size), 1]
+
+
+def farthest_first(size):
+    return [size - 1, *range(1, size - 1)]
 
 
 def near_first(size):
@@ -337,7 +341,7 @@
         [struct((rows, 2 * unit), BF16)] * seq_count,
         [sorted_chunks],
     )(gain, forward, backward, received, *prepared)
-    result = exchange(result, "seq", middle_first(seq_count))
+    result = exchange(result, "seq", farthest_first(seq_count))
 
     lag_width = width // chan_count
     lags = call(

time: 32.7 us -> 32.4 us (level)
  waiting for transfers between devices: 6.83 us -> 5.6 us
  starting transfers between devices: 18.5 us -> 19.4 us
    ppermute x12, waiting for transfers between devices: 5.87 us -> 4.64 us  [exchange(): lax.ppermute(chunks[step], axis, [(i, i ^ step) for i in range(size)])]
    ppermute x12, starting transfers between devices: 17 us -> 17.9 us  [exchange(): lax.ppermute(chunks[step], axis, [(i, i ^ step) for i in range(size)])]
where the time goes in v7:
time: 32.4 us; the launch traced here: 32.2 us
  starting transfers between devices  19.4 us (60%)
  Pallas kernels  6.46 us (20%)
  waiting for transfers between devices  5.6 us (17%)
  between operations  0.69 us (2%)
    ppermute x12, starting transfers between devices, exchange(): lax.ppermute(chunks[step], axis, [(i, i ^ step) for i in range(size)])  17.9 us
    pallas_call x8, Pallas kernels, run(): pl.pallas_call(kernel, out_shape=out_shape, in_specs=[pl.BlockSpec(memory...  6.46 us
    ppermute x12, waiting for transfers between devices, exchange(): lax.ppermute(chunks[step], axis, [(i, i ^ step) for i in range(size)])  4.64 us
    ppermute x1, starting transfers between devices, body(): received = lax.ppermute(gradient, 'section', ring)  1.56 us
    ppermute x1, waiting for transfers between devices, body(): received = lax.ppermute(gradient, 'section', ring)  0.96 us
  transfers between devices with their start and end apart: 13, of which 7 were waited for; matrix products, arithmetic and copies ran while one was open for 0% of the time, Pallas kernels for 11%

profile of v7, /device:TPU:0, one launch (start us, length us, event | category | flops | bytes accessed | tf_op | source)
XLA Modules:
  0.0 32.2 jit_solution(11662893724121488994)
XLA Ops:
  0.6 1.2 %shard_map.104 = (bf16[128,256]{1,0:T(8,128)(2,1)S(1)}, bf16[128,256]{1,0:T(8,128)(2,1)S(1)}, bf16[128,256]{1,0:T(8,128)(2,1)S(1)}, bf16[128,256]{1,0:T(8,128)(2,1)S(1)}) custom-call(bf16[1,2,128,256]{3,2,1,0:T(8,128)(2,1)} %post.3, bf16[1,128,256]{2,1,0:T(8,128)(2,1)} %held.1, bf16[128,256]{1,0:T(8,128)(2,1)} %loss.1, bf16[1,2,128,256]{3,2,1,0:T(8,128)(2,1)} %pre.3, ...), custom_call_target="tpu_custom_call" | custom-call | tf_op jit(solution)/shard_map/pallas_call | solution.py:45
  1.9 4.1 %collective-permute-start = (bf16[128,256]{1,0:T(8,128)(2,1)S(1)}, bf16[128,256]{1,0:T(8,128)(2,1)S(1)}, u32[]{:S(2)}, u32[]{:S(2)}) collective-permute-start(bf16[128,256]{1,0:T(8,128)(2,1)S(1)} %get-tuple-element.31), channel_id=1, source_target_pairs={{0,8},{4,12},{8,0},{12,4},{1,9},{5,13},{9,1},{13,5},{2,10},{6,14},... | collective-permute-start | bytes 196616 | tf_op jit(solution)/shard_map/ppermute | solution.py:265
  6.0 1.3 %collective-permute-start.1 = (bf16[128,256]{1,0:T(8,128)(2,1)S(1)}, bf16[128,256]{1,0:T(8,128)(2,1)S(1)}, u32[]{:S(2)}, u32[]{:S(2)}) collective-permute-start(bf16[128,256]{1,0:T(8,128)(2,1)S(1)} %get-tuple-element.32), channel_id=1, source_target_pairs={{0,12},{4,8},{8,4},{12,0},{1,13},{5,9},{9,5},{13,1},{2,14},{6,10},... | collective-permute-start | bytes 196616 | tf_op jit(solution)/shard_map/ppermute | solution.py:265
  7.3 0.2 collective-permute-start.2
  7.6 1.5 %shard_map.105 = (bf16[128,256]{1,0:T(8,128)(2,1)S(1)}, bf16[128,256]{1,0:T(8,128)(2,1)S(1)}, bf16[128,256]{1,0:T(8,128)(2,1)S(1)}, bf16[128,256]{1,0:T(8,128)(2...) custom-call(bf16[128,256]{1,0:T(8,128)(2,1)S(1)} %get-tuple-element.27.after.rest_0_, ...), custom_call_target="tpu_custom_call" | custom-call | tf_op jit(solution)/shard_map/pallas_call | solution.py:45
  9.0 1.9 %collective-permute-start.4 = (bf16[128,256]{1,0:T(8,128)(2,1)S(1)}, bf16[128,256]{1,0:T(8,128)(2,1)S(1)}, u32[]{:S(2)}, u32[]{:S(2)}) collective-permute-start(bf16[128,256]{1,0:T(8,128)(2,1)S(1)} %get-tuple-element.37), channel_id=1, source_target_pairs={{0,4},{4,0},{8,12},{12,8},{1,5},{5,1},{9,13},{13,9},{2,6},{6,2},{1... | collective-permute-start | bytes 196616 | tf_op jit(solution)/shard_map/ppermute | solution.py:265
  10.9 1.7 %collective-permute-start.5 = (bf16[128,256]{1,0:T(8,128)(2,1)S(1)}, bf16[128,256]{1,0:T(8,128)(2,1)S(1)}, u32[]{:S(2)}, u32[]{:S(2)}) collective-permute-start(bf16[128,256]{1,0:T(8,128)(2,1)S(1)} %get-tuple-element.38), channel_id=1, source_target_pairs={{0,8},{4,12},{8,0},{12,4},{1,9},{5,13},{9,1},{13,5},{2,10},{6,14},... | collective-permute-start | bytes 196616 | tf_op jit(solution)/shard_map/ppermute | solution.py:265
  12.6 2.3 %collective-permute-start.6 = (bf16[128,256]{1,0:T(8,128)(2,1)S(1)}, bf16[128,256]{1,0:T(8,128)(2,1)S(1)}, u32[]{:S(2)}, u32[]{:S(2)}) collective-permute-start(bf16[128,256]{1,0:T(8,128)(2,1)S(1)} %get-tuple-element.39), channel_id=1, source_target_pairs={{0,12},{4,8},{8,4},{12,0},{1,13},{5,9},{9,5},{13,1},{2,14},{6,10},... | collective-permute-start | bytes 196616 | tf_op jit(solution)/shard_map/ppermute | solution.py:265
  14.9 0.9 %shard_map.106 = (bf16[256,128]{1,0:T(8,128)(2,1)S(1)}, f32[2,512,128]{2,1,0:T(8,128)S(1)}) custom-call(f32[1,128]{1,0:T(1,128)S(1)} %get-tuple-element.28.gain, bf16[1024,256]{1,0:T(8,128)(2,1)S(1)} %get-tuple-element.29.forward, bf16[256,1024]{1,0:T(8,128)(2,1)S(1)} %get-tuple-element.30.backward, bf16[128,256]{1,0:T(8,128)(2,1)S(1)} %get-tuple-element.27.after.rest_0_, ...), custom_call_target="tpu_custom_call" | custom-call | tf_op jit(solution)/shard_map/pallas_call | solution.py:45
  15.8 1.6 %collective-permute-start.3 = (bf16[256,128]{1,0:T(8,128)(2,1)S(1)}, bf16[256,128]{1,0:T(8,128)(2,1)S(1)}, u32[]{:S(2)}, u32[]{:S(2)}) collective-permute-start(bf16[256,128]{1,0:T(8,128)(2,1)S(1)} %get-tuple-element.34), channel_id=1, source_target_pairs={{0,16},{16,0},{1,17},{17,1},{2,18},{18,2},{3,19},{19,3},{4,20},{20... | collective-permute-start | bytes 196616 | tf_op jit(solution)/shard_map/ppermute | solution.py:330
  17.5 1.3 %collective-permute-done.6.rest_3_ = bf16[128,256]{1,0:T(8,128)(2,1)S(1)} collective-permute-done((bf16[128,256]{1,0:T(8,128)(2,1)S(1)}, bf16[128,256]{1,0:T(8,128)(2,1)S(1)}, u32[]{:S(2)}, u32[]{:S(2)}) %collective-permute-start.6) | collective-permute-done | bytes 65568 | tf_op jit(solution)/shard_map/ppermute | solution.py:265
  18.8 0.4 %shard_map.107 = (f32[2,256,128]{2,1,0:T(8,128)S(1)}, f32[2,256,128]{2,1,0:T(8,128)S(1)}, f32[2,512,128]{2,1,0:T(8,128)S(1)}, f32[2,512,128]{2,1,0:T(8,128)S(1)}) custom-call(bf16[1024,256]{1,0:T(8,128)(2,1)S(1)} %get-tuple-element.29.forward, f32[2,512,128]{2,1,0:T(8,128)S(1)} %get-tuple-element.35.spectra, bf16[128,256]{1,0:T(8,128)(2,1)S(1)} %get-tuple-element.36.rest_0_, ...), custom_call_target="tpu_custom_call" | custom-call | tf_op jit(solution)/shard_map/pallas_call | solution.py:45
  19.2 1.0 %collective-permute-done.3.received = bf16[256,128]{1,0:T(8,128)(2,1)S(1)} collective-permute-done((bf16[256,128]{1,0:T(8,128)(2,1)S(1)}, bf16[256,128]{1,0:T(8,128)(2,1)S(1)}, u32[]{:S(2)}, u32[]{:S(2)}) %collective-permute-start.3) | collective-permute-done | bytes 65568 | tf_op jit(solution)/shard_map/ppermute | solution.py:330
  20.1 0.9 %shard_map.108 = (bf16[128,128]{1,0:T(8,128)(2,1)S(1)}, bf16[128,128]{1,0:T(8,128)(2,1)S(1)}, bf16[128,128]{1,0:T(8,128)(2,1)S(1)}, bf16[128,128]{1,0:T(8,128)(2,1)S(1)}) custom-call(f32[1,128]{1,0:T(1,128)S(1)} %get-tuple-element.28.gain, bf16[1024,256]{1,0:T(8,128)(2,1)S(1)} %get-tuple-element.29.forward, ...), custom_call_target="tpu_custom_call" | custom-call | tf_op jit(solution)/shard_map/pallas_call | solution.py:45
  21.0 1.6 %collective-permute-start.7 = (bf16[128,128]{1,0:T(8,128)(2,1)S(1)}, bf16[128,128]{1,0:T(8,128)(2,1)S(1)}, u32[]{:S(2)}, u32[]{:S(2)}) collective-permute-start(bf16[128,128]{1,0:T(8,128)(2,1)S(1)} %get-tuple-element.45), channel_id=1, source_target_pairs={{0,12},{4,8},{8,4},{12,0},{1,13},{5,9},{9,5},{13,1},{2,14},{6,10},... | collective-permute-start | bytes 98312 | tf_op jit(solution)/shard_map/ppermute | solution.py:265
  22.7 2.8 %collective-permute-start.9 = (bf16[128,128]{1,0:T(8,128)(2,1)S(1)}, bf16[128,128]{1,0:T(8,128)(2,1)S(1)}, u32[]{:S(2)}, u32[]{:S(2)}) collective-permute-start(bf16[128,128]{1,0:T(8,128)(2,1)S(1)} %get-tuple-element.47), channel_id=1, source_target_pairs={{0,8},{4,12},{8,0},{12,4},{1,9},{5,13},{9,1},{13,5},{2,10},{6,14},... | collective-permute-start | bytes 98312 | tf_op jit(solution)/shard_map/ppermute | solution.py:265
  25.5 1.4 %collective-permute-done.7.rest_1_ = bf16[128,128]{1,0:T(8,128)(2,1)S(1)} collective-permute-done((bf16[128,128]{1,0:T(8,128)(2,1)S(1)}, bf16[128,128]{1,0:T(8,128)(2,1)S(1)}, u32[]{:S(2)}, u32[]{:S(2)}) %collective-permute-start.7) | collective-permute-done | bytes 32800 | tf_op jit(solution)/shard_map/ppermute | solution.py:265
  26.9 0.6 %collective-permute-done.9.rest_3_ = bf16[128,128]{1,0:T(8,128)(2,1)S(1)} collective-permute-done((bf16[128,128]{1,0:T(8,128)(2,1)S(1)}, bf16[128,128]{1,0:T(8,128)(2,1)S(1)}, u32[]{:S(2)}, u32[]{:S(2)}) %collective-permute-start.9) | collective-permute-done | bytes 32800 | tf_op jit(solution)/shard_map/ppermute | solution.py:265
  27.8 1.6 %collective-permute-start.11 = (bf16[64,128]{1,0:T(8,128)(2,1)S(1)}, bf16[64,128]{1,0:T(8,128)(2,1)S(1)}, u32[]{:S(2)}, u32[]{:S(2)}) collective-permute-start(bf16[64,128]{1,0:T(8,128)(2,1)S(1)} %get-tuple-element.50), channel_id=1, source_target_pairs={{0,2},{1,3},{2,0},{3,1},{4,6},{5,7},{6,4},{7,5},{8,10},{9,11},{10,... | collective-permute-start | bytes 49160 | tf_op jit(solution)/shard_map/ppermute | solution.py:265
  29.3 0.3 collective-permute-start.12
  29.6 0.7 %shard_map.109 = bf16[1,128,256]{2,1,0:T(8,128)(2,1)} custom-call(bf16[128,128]{1,0:T(8,128)(2,1)S(1)} %get-tuple-element.44.rest_0_, bf16[128,128]{1,0:T(8,128)(2,1)S(1)} %collective-permute-done.7.rest_1_, bf16[128,128]{1,0:T(8,128)(2,1)S(1)} %collective-permute-done.8.rest_2_, bf16[128,128]{1,0:T(8,128)(2,1)S(1)} %collective-permute-done.9.rest_3_), custom_call_target="tpu_custom_call" | custom-call | tf_op jit(solution)/shard_map/pallas_call | solution.py:45
  30.3 0.7 %collective-permute-done.10.refs_1_ = bf16[64,128]{1,0:T(8,128)(2,1)S(1)} collective-permute-done((bf16[64,128]{1,0:T(8,128)(2,1)S(1)}, bf16[64,128]{1,0:T(8,128)(2,1)S(1)}, u32[]{:S(2)}, u32[]{:S(2)}) %collective-permute-start.10) | collective-permute-done | bytes 16416 | tf_op jit(solution)/shard_map/ppermute | solution.py:265
  31.0 0.6 %collective-permute-done.11.refs_2_ = bf16[64,128]{1,0:T(8,128)(2,1)S(1)} collective-permute-done((bf16[64,128]{1,0:T(8,128)(2,1)S(1)}, bf16[64,128]{1,0:T(8,128)(2,1)S(1)}, u32[]{:S(2)}, u32[]{:S(2)}) %collective-permute-start.11) | collective-permute-done | bytes 16416 | tf_op jit(solution)/shard_map/ppermute | solution.py:265
  31.6 0.6 %shard_map.111 = f32[64,128]{1,0:T(8,128)} custom-call(bf16[64,128]{1,0:T(8,128)(2,1)S(1)} %get-tuple-element.48.refs_0_, bf16[64,128]{1,0:T(8,128)(2,1)S(1)} %collective-permute-done.10.refs_1_, bf16[64,128]{1,0:T(8,128)(2,1)S(1)} %collective-permute-done.11.refs_2_, bf16[64,128]{1,0:T(8,128)(2,1)S(1)} %collective-permute-done.12.refs_3_), custom_call_target="tpu_custom_call" | custom-call | tf_op jit(solution)/shard_map/pallas_call | solution.py:45
  (10 shorter events, 0.4 us)
Async XLA Ops:
  1.9 10.7 %collective-permute-start = (bf16[128,256]{1,0:T(8,128)(2,1)S(1)}, bf16[128,256]{1,0:T(8,128)(2,1)S(1)}, u32[]{:S(2)}, u32[]{:S(2)}) collective-permute-start(bf16[128,256]{1,0:T(8,128)(2,1)S(1)} %get-tuple-element.31), channel_id=1, source_target_pairs={{0,8},{4,12},{8,0},{12,4},{1,9},{5,13},{9,1},{13,5},{2,10},{6,14},... | collective-permute-start | bytes 196616 | tf_op jit(solution)/shard_map/ppermute | solution.py:265
  6.0 8.9 %collective-permute-start.1 = (bf16[128,256]{1,0:T(8,128)(2,1)S(1)}, bf16[128,256]{1,0:T(8,128)(2,1)S(1)}, u32[]{:S(2)}, u32[]{:S(2)}) collective-permute-start(bf16[128,256]{1,0:T(8,128)(2,1)S(1)} %get-tuple-element.32), channel_id=1, source_target_pairs={{0,12},{4,8},{8,4},{12,0},{1,13},{5,9},{9,5},{13,1},{2,14},{6,10},... | collective-permute-start | bytes 196616 | tf_op jit(solution)/shard_map/ppermute | solution.py:265
  7.3 7.5 %collective-permute-start.2 = (bf16[128,256]{1,0:T(8,128)(2,1)S(1)}, bf16[128,256]{1,0:T(8,128)(2,1)S(1)}, u32[]{:S(2)}, u32[]{:S(2)}) collective-permute-start(bf16[128,256]{1,0:T(8,128)(2,1)S(1)} %get-tuple-element.33), channel_id=1, source_target_pairs={{0,4},{4,0},{8,12},{12,8},{1,5},{5,1},{9,13},{13,9},{2,6},{6,2},{1... | collective-permute-start | bytes 196616 | tf_op jit(solution)/shard_map/ppermute | solution.py:265
  9.0 8.3 %collective-permute-start.4 = (bf16[128,256]{1,0:T(8,128)(2,1)S(1)}, bf16[128,256]{1,0:T(8,128)(2,1)S(1)}, u32[]{:S(2)}, u32[]{:S(2)}) collective-permute-start(bf16[128,256]{1,0:T(8,128)(2,1)S(1)} %get-tuple-element.37), channel_id=1, source_target_pairs={{0,4},{4,0},{8,12},{12,8},{1,5},{5,1},{9,13},{13,9},{2,6},{6,2},{1... | collective-permute-start | bytes 196616 | tf_op jit(solution)/shard_map/ppermute | solution.py:265
  10.9 6.6 %collective-permute-start.5 = (bf16[128,256]{1,0:T(8,128)(2,1)S(1)}, bf16[128,256]{1,0:T(8,128)(2,1)S(1)}, u32[]{:S(2)}, u32[]{:S(2)}) collective-permute-start(bf16[128,256]{1,0:T(8,128)(2,1)S(1)} %get-tuple-element.38), channel_id=1, source_target_pairs={{0,8},{4,12},{8,0},{12,4},{1,9},{5,13},{9,1},{13,5},{2,10},{6,14},... | collective-permute-start | bytes 196616 | tf_op jit(solution)/shard_map/ppermute | solution.py:265
  12.6 6.2 %collective-permute-start.6 = (bf16[128,256]{1,0:T(8,128)(2,1)S(1)}, bf16[128,256]{1,0:T(8,128)(2,1)S(1)}, u32[]{:S(2)}, u32[]{:S(2)}) collective-permute-start(bf16[128,256]{1,0:T(8,128)(2,1)S(1)} %get-tuple-element.39), channel_id=1, source_target_pairs={{0,12},{4,8},{8,4},{12,0},{1,13},{5,9},{9,5},{13,1},{2,14},{6,10},... | collective-permute-start | bytes 196616 | tf_op jit(solution)/shard_map/ppermute | solution.py:265
  15.8 4.3 %collective-permute-start.3 = (bf16[256,128]{1,0:T(8,128)(2,1)S(1)}, bf16[256,128]{1,0:T(8,128)(2,1)S(1)}, u32[]{:S(2)}, u32[]{:S(2)}) collective-permute-start(bf16[256,128]{1,0:T(8,128)(2,1)S(1)} %get-tuple-element.34), channel_id=1, source_target_pairs={{0,16},{16,0},{1,17},{17,1},{2,18},{18,2},{3,19},{19,3},{4,20},{20... | collective-permute-start | bytes 196616 | tf_op jit(solution)/shard_map/ppermute | solution.py:330
  21.0 5.9 %collective-permute-start.7 = (bf16[128,128]{1,0:T(8,128)(2,1)S(1)}, bf16[128,128]{1,0:T(8,128)(2,1)S(1)}, u32[]{:S(2)}, u32[]{:S(2)}) collective-permute-start(bf16[128,128]{1,0:T(8,128)(2,1)S(1)} %get-tuple-element.45), channel_id=1, source_target_pairs={{0,12},{4,8},{8,4},{12,0},{1,13},{5,9},{9,5},{13,1},{2,14},{6,10},... | collective-permute-start | bytes 98312 | tf_op jit(solution)/shard_map/ppermute | solution.py:265
  22.6 4.3 %collective-permute-start.8 = (bf16[128,128]{1,0:T(8,128)(2,1)S(1)}, bf16[128,128]{1,0:T(8,128)(2,1)S(1)}, u32[]{:S(2)}, u32[]{:S(2)}) collective-permute-start(bf16[128,128]{1,0:T(8,128)(2,1)S(1)} %get-tuple-element.46), channel_id=1, source_target_pairs={{0,4},{4,0},{8,12},{12,8},{1,5},{5,1},{9,13},{13,9},{2,6},{6,2},{1... | collective-permute-start | bytes 98312 | tf_op jit(solution)/shard_map/ppermute | solution.py:265
  22.7 4.8 %collective-permute-start.9 = (bf16[128,128]{1,0:T(8,128)(2,1)S(1)}, bf16[128,128]{1,0:T(8,128)(2,1)S(1)}, u32[]{:S(2)}, u32[]{:S(2)}) collective-permute-start(bf16[128,128]{1,0:T(8,128)(2,1)S(1)} %get-tuple-element.47), channel_id=1, source_target_pairs={{0,8},{4,12},{8,0},{12,4},{1,9},{5,13},{9,1},{13,5},{2,10},{6,14},... | collective-permute-start | bytes 98312 | tf_op jit(solution)/shard_map/ppermute | solution.py:265
  27.7 3.3 %collective-permute-start.10 = (bf16[64,128]{1,0:T(8,128)(2,1)S(1)}, bf16[64,128]{1,0:T(8,128)(2,1)S(1)}, u32[]{:S(2)}, u32[]{:S(2)}) collective-permute-start(bf16[64,128]{1,0:T(8,128)(2,1)S(1)} %get-tuple-element.49), channel_id=1, source_target_pairs={{0,3},{1,2},{2,1},{3,0},{4,7},{5,6},{6,5},{7,4},{8,11},{9,10},{10,... | collective-permute-start | bytes 49160 | tf_op jit(solution)/shard_map/ppermute | solution.py:265
  27.8 3.8 %collective-permute-start.11 = (bf16[64,128]{1,0:T(8,128)(2,1)S(1)}, bf16[64,128]{1,0:T(8,128)(2,1)S(1)}, u32[]{:S(2)}, u32[]{:S(2)}) collective-permute-start(bf16[64,128]{1,0:T(8,128)(2,1)S(1)} %get-tuple-element.50), channel_id=1, source_target_pairs={{0,2},{1,3},{2,0},{3,1},{4,6},{5,7},{6,4},{7,5},{8,10},{9,11},{10,... | collective-permute-start | bytes 49160 | tf_op jit(solution)/shard_map/ppermute | solution.py:265
  29.3 2.2 %collective-permute-start.12 = (bf16[64,128]{1,0:T(8,128)(2,1)S(1)}, bf16[64,128]{1,0:T(8,128)(2,1)S(1)}, u32[]{:S(2)}, u32[]{:S(2)}) collective-permute-start(bf16[64,128]{1,0:T(8,128)(2,1)S(1)} %get-tuple-element.51), channel_id=1, source_target_pairs={{0,1},{1,0},{2,3},{3,2},{4,5},{5,4},{6,7},{7,6},{8,9},{9,8},{10,11... | collective-permute-start | bytes 49160 | tf_op jit(solution)/shard_map/ppermute | solution.py:265

commit v8 on v6

--- a/solution.py
+++ b/solution.py
@@ -13,6 +13,24 @@
 BF16 = jnp.bfloat16
 F32 = jnp.float32
 HALF_TURN = math.sqrt(0.5)
+OWN = (0, 0)
+
+
+def both(steps):
+    return [(step, step) for step in steps]
+
+
+def first_steps(size):
+    return both([*range(2, size), 1])
+
+
+def second_steps(size):
+    near = list(range(1, size))
+    return list(zip(near, [*near[1::-1], *near[2:]]))
+
+
+def last_steps(size):
+    return both([size - 1, *range(1, size - 1)])
 
 
 def transform_tables(length):
@@ -75,15 +93,19 @@
     return jnp.dot(left, right, preferred_element_type=F32)
 
 
-def pack(arrays, stage, outs):
-    seq_index = lax.axis_index("seq")
+def place(step):
+    even, odd = step
+    return lax.axis_index("seq") ^ jnp.where(lax.axis_index("section") % 2 == 0, even, odd)
+
+
+def pack(arrays, stage, outs, steps):
     count = len(outs)
     unit = arrays[0].shape[1] // count
     for block in range(count):
         lanes = slice(block * unit, (block + 1) * unit)
         stage[block] = jnp.concatenate([array[:, lanes] for array in arrays], axis=1)
-    for step, out in enumerate(outs):
-        out[...] = stage[seq_index ^ step]
+    for step, out in zip([OWN, *steps], outs):
+        out[...] = stage[place(step)]
 
 
 def pack_first(post, held, loss, pre, filters, *rest):
@@ -92,7 +114,7 @@
     wait(fetch(sources, [gates.at[at] for at in range(4)] + [lags], semaphores))
     gated = (gates[0].astype(F32) * gates[1].astype(F32)).astype(BF16)
     kept = jnp.where(lax.axis_index("section") == 0, gates[2], gates[1])
-    pack([lags[...].astype(BF16), gated, gates[3], kept], stage, outs)
+    pack([lags[...].astype(BF16), gated, gates[3], kept], stage, outs, first_steps(len(outs)))
 
 
 def pack_second(after, saved, pre, post, gains, forward, backward, *rest):
@@ -107,7 +129,7 @@
     )
     wait(copies[:6])
     mixed = (gates[0:2].astype(F32) * gates[2:4].astype(F32)).astype(BF16)
-    pack([mixed[0], mixed[1], gates[4], gates[3]], stage, outs)
+    pack([mixed[0], mixed[1], gates[4], gates[3]], stage, outs, second_steps(len(outs)))
     unit = gain.shape[1] // 2
     for block in range(len(outs)):
 
@@ -120,10 +142,9 @@
 
 
 def gather_positions(chunks, steps, held):
-    seq_index = lax.axis_index("seq")
     rows = chunks[0].shape[0]
-    for step, chunk in zip([0, *steps], chunks):
-        at = pl.multiple_of((seq_index ^ step) * rows, rows)
+    for step, chunk in zip([OWN, *steps], chunks):
+        at = pl.multiple_of(place(step) * rows, rows)
         held[pl.ds(at, rows), :] = chunk[...]
 
 
@@ -175,7 +196,7 @@
 
 def first_tick(gain, forward, backward, *rest):
     *chunks, out, spectra, held = rest
-    gather_positions(chunks, middle_first(len(chunks)), held)
+    gather_positions(chunks, first_steps(len(chunks)), held)
     length, lanes = held.shape[0], gain.shape[1]
     parts = halves(held)
     real, imag = spectrum(forward, parts[0][0], parts[1][0])
@@ -193,7 +214,7 @@
 
 def mixed_spectra(scale, forward, spectra, *rest):
     *chunks, post, weight, other, lag_spec, held = rest
-    gather_positions(chunks, near_first(len(chunks)), held)
+    gather_positions(chunks, second_steps(len(chunks)), held)
     parts = halves(held)
     real, imag = spectrum(forward, parts[0][0], parts[1][0])
     low = first_unit(real)
@@ -225,17 +246,16 @@
         result = jnp.where(low, carried[part] + result, result).astype(BF16)
         for block in range(count // 2):
             stage[part * (count // 2) + block] = result[block * rows : (block + 1) * rows]
-    for step, out in enumerate(outs):
-        out[...] = stage[lax.axis_index("seq") ^ step]
+    for step, out in zip([OWN, *last_steps(count)], outs):
+        out[...] = stage[place(step)]
 
 
 def unpack_gradient(*rest):
     *chunks, grad, stage = rest
     count = stage.shape[0]
     unit = stage.shape[2] // 2
-    seq_index = lax.axis_index("seq")
-    for step, chunk in zip([0, *middle_first(count)], chunks):
-        stage[seq_index ^ step] = chunk[...]
+    for step, chunk in zip([OWN, *last_steps(count)], chunks):
+        stage[place(step)] = chunk[...]
     grad[0] = jnp.concatenate([stage[block][:, :unit] for block in range(count)], axis=1)
 
 
@@ -244,9 +264,9 @@
     count = stage.shape[0]
     chunks, lags = refs[:count], refs[count:]
     unit = stage.shape[2] // 2
-    seq_index, chan_index = lax.axis_index("seq"), lax.axis_index("chan")
-    for step, chunk in zip([0, *middle_first(count)], chunks):
-        stage[seq_index ^ step] = chunk[...]
+    chan_index = lax.axis_index("chan")
+    for step, chunk in zip([OWN, *last_steps(count)], chunks):
+        stage[place(step)] = chunk[...]
     lag_grad = jnp.concatenate([stage[block][:, unit:] for block in range(count)], axis=1)
     lag_stage[...] = lag_grad.astype(F32).T.astype(BF16)
     for step, lag in enumerate(lags):
@@ -259,23 +279,28 @@
     out[...] = functools.reduce(jnp.add, [lag[...].astype(F32) for lag in lags])
 
 
-def exchange(chunks, axis, steps):
-    size = lax.axis_size(axis)
+def exchange_chan(chunks):
+    size = lax.axis_size("chan")
     return [chunks[0]] + [
-        lax.ppermute(chunks[step], axis, [(i, i ^ step) for i in range(size)]) for step in steps
+        lax.ppermute(chunks[step], "chan", [(i, i ^ step) for i in range(size)])
+        for step in reversed(range(1, size))
     ]
 
 
-def middle_first(size):
-    return [*range(2, size), 1]
-
-
-def near_first(size):
-    return list(range(1, size))
-
-
-def far_first(size):
-    return list(reversed(range(1, size)))
+def exchange_seq(chunks, steps):
+    size = lax.axis_size("seq")
+    places = [(section, seq) for section in range(lax.axis_size("section")) for seq in range(size)]
+    return [chunks[0]] + [
+        lax.ppermute(
+            chunk,
+            ("section", "seq"),
+            [
+                (section * size + seq, section * size + (seq ^ step[section % 2]))
+                for section, seq in places
+            ],
+        )
+        for chunk, step in zip(chunks[1:], steps)
+    ]
 
 
 def body(forward, backward, *args):
@@ -314,8 +339,8 @@
         [pl.ANY] + [pltpu.HBM] * 6,
         8,
     )(first[0], saved_input, pre_gate, post_gate, skip_gain, forward, backward)
-    first = exchange(first, "seq", middle_first(seq_count))
-    second = exchange(second, "seq", near_first(seq_count))
+    first = exchange_seq(first, first_steps(seq_count))
+    second = exchange_seq(second, second_steps(seq_count))
 
     gradient, spectra = call(
         first_tick,
@@ -337,7 +362,7 @@
         [struct((rows, 2 * unit), BF16)] * seq_count,
         [sorted_chunks],
     )(gain, forward, backward, received, *prepared)
-    result = exchange(result, "seq", middle_first(seq_count))
+    result = exchange_seq(result, last_steps(seq_count))
 
     lag_width = width // chan_count
     lags = call(
@@ -345,7 +370,7 @@
         [struct((lag_width, rows), BF16)] * chan_count,
         [sorted_chunks, struct((width, rows), BF16)],
     )(*result)
-    lags = exchange(lags, "chan", far_first(chan_count))
+    lags = exchange_chan(lags)
     (grad_out,) = call(unpack_gradient, [struct((1, rows, width), BF16)], [sorted_chunks])(*result)
     (lag_grad,) = call(add_up, [struct((lag_width, rows), F32)])(*lags)
     return grad_out, lag_grad.T[None]

time: 32.7 us -> 32.4 us (level)
  waiting for transfers between devices: 6.83 us -> 5.6 us
  starting transfers between devices: 18.5 us -> 19.4 us
    ppermute x12, waiting for transfers between devices: 5.87 us -> 4.64 us  [the longest x9 3.41 us: exchange_seq(): lax.ppermute(chunk, ('section', 'seq'), [(section * size + seq, section *...]
    ppermute x12, starting transfers between devices: 17 us -> 17.9 us  [the longest x9 16 us: exchange_seq(): lax.ppermute(chunk, ('section', 'seq'), [(section * size + seq, section *...]
where the time goes in v8:
time: 32.4 us; the launch traced here: 32.2 us
  starting transfers between devices  19.4 us (60%)
  Pallas kernels  6.46 us (20%)
  waiting for transfers between devices  5.6 us (17%)
  between operations  0.69 us (2%)
    ppermute x9, starting transfers between devices, exchange_seq(): lax.ppermute(chunk, ('section', 'seq'), [(section * size + seq, section *...  16 us
    pallas_call x8, Pallas kernels, run(): pl.pallas_call(kernel, out_shape=out_shape, in_specs=[pl.BlockSpec(memory...  6.46 us
    ppermute x9, waiting for transfers between devices, exchange_seq(): lax.ppermute(chunk, ('section', 'seq'), [(section * size + seq, section *...  3.41 us
    ppermute x3, starting transfers between devices, exchange_chan(): lax.ppermute(chunks[step], 'chan', [(i, i ^ step) for i in range(size)])  1.92 us
    ppermute x1, starting transfers between devices, body(): received = lax.ppermute(gradient, 'section', ring)  1.56 us
    ppermute x3, waiting for transfers between devices, exchange_chan(): lax.ppermute(chunks[step], 'chan', [(i, i ^ step) for i in range(size)])  1.23 us
    ppermute x1, waiting for transfers between devices, body(): received = lax.ppermute(gradient, 'section', ring)  0.96 us
  transfers between devices with their start and end apart: 13, of which 7 were waited for; matrix products, arithmetic and copies ran while one was open for 0% of the time, Pallas kernels for 11%

profile of v8, /device:TPU:0, one launch (start us, length us, event | category | flops | bytes accessed | tf_op | source)
XLA Modules:
  0.0 32.2 jit_solution(4454226107657511953)
XLA Ops:
  0.6 1.2 %shard_map.104 = (bf16[128,256]{1,0:T(8,128)(2,1)S(1)}, bf16[128,256]{1,0:T(8,128)(2,1)S(1)}, bf16[128,256]{1,0:T(8,128)(2,1)S(1)}, bf16[128,256]{1,0:T(8,128)(2,1)S(1)}) custom-call(bf16[1,2,128,256]{3,2,1,0:T(8,128)(2,1)} %post.3, bf16[1,128,256]{2,1,0:T(8,128)(2,1)} %held.1, bf16[128,256]{1,0:T(8,128)(2,1)} %loss.1, bf16[1,2,128,256]{3,2,1,0:T(8,128)(2,1)} %pre.3, ...), custom_call_target="tpu_custom_call" | custom-call | tf_op jit(solution)/shard_map/pallas_call | solution.py:63
  1.9 4.1 %collective-permute-start = (bf16[128,256]{1,0:T(8,128)(2,1)S(1)}, bf16[128,256]{1,0:T(8,128)(2,1)S(1)}, u32[]{:S(2)}, u32[]{:S(2)}) collective-permute-start(bf16[128,256]{1,0:T(8,128)(2,1)S(1)} %get-tuple-element.31), channel_id=1, source_target_pairs={{0,8},{4,12},{8,0},{12,4},{16,24},{20,28},{24,16},{28,20},{1,9},{5... | collective-permute-start | bytes 196616 | tf_op jit(solution)/shard_map/ppermute | solution.py:294
  6.0 1.3 %collective-permute-start.1 = (bf16[128,256]{1,0:T(8,128)(2,1)S(1)}, bf16[128,256]{1,0:T(8,128)(2,1)S(1)}, u32[]{:S(2)}, u32[]{:S(2)}) collective-permute-start(bf16[128,256]{1,0:T(8,128)(2,1)S(1)} %get-tuple-element.32), channel_id=1, source_target_pairs={{0,12},{4,8},{8,4},{12,0},{16,28},{20,24},{24,20},{28,16},{1,13},{... | collective-permute-start | bytes 196616 | tf_op jit(solution)/shard_map/ppermute | solution.py:294
  7.3 0.2 collective-permute-start.2
  7.6 1.5 %shard_map.105 = (bf16[128,256]{1,0:T(8,128)(2,1)S(1)}, bf16[128,256]{1,0:T(8,128)(2,1)S(1)}, bf16[128,256]{1,0:T(8,128)(2,1)S(1)}, bf16[128,256]{1,0:T(8,128)(2...) custom-call(bf16[128,256]{1,0:T(8,128)(2,1)S(1)} %get-tuple-element.27.after.rest_0_, ...), custom_call_target="tpu_custom_call" | custom-call | tf_op jit(solution)/shard_map/pallas_call | solution.py:63
  9.0 1.9 %collective-permute-start.4 = (bf16[128,256]{1,0:T(8,128)(2,1)S(1)}, bf16[128,256]{1,0:T(8,128)(2,1)S(1)}, u32[]{:S(2)}, u32[]{:S(2)}) collective-permute-start(bf16[128,256]{1,0:T(8,128)(2,1)S(1)} %get-tuple-element.37), channel_id=1, source_target_pairs={{0,4},{4,0},{8,12},{12,8},{16,24},{20,28},{24,16},{28,20},{1,5},{5... | collective-permute-start | bytes 196616 | tf_op jit(solution)/shard_map/ppermute | solution.py:294
  10.9 1.7 %collective-permute-start.5 = (bf16[128,256]{1,0:T(8,128)(2,1)S(1)}, bf16[128,256]{1,0:T(8,128)(2,1)S(1)}, u32[]{:S(2)}, u32[]{:S(2)}) collective-permute-start(bf16[128,256]{1,0:T(8,128)(2,1)S(1)} %get-tuple-element.38), channel_id=1, source_target_pairs={{0,8},{4,12},{8,0},{12,4},{16,20},{20,16},{24,28},{28,24},{1,9},{5... | collective-permute-start | bytes 196616 | tf_op jit(solution)/shard_map/ppermute | solution.py:294
  12.6 2.3 %collective-permute-start.6 = (bf16[128,256]{1,0:T(8,128)(2,1)S(1)}, bf16[128,256]{1,0:T(8,128)(2,1)S(1)}, u32[]{:S(2)}, u32[]{:S(2)}) collective-permute-start(bf16[128,256]{1,0:T(8,128)(2,1)S(1)} %get-tuple-element.39), channel_id=1, source_target_pairs={{0,12},{4,8},{8,4},{12,0},{16,28},{20,24},{24,20},{28,16},{1,13},{... | collective-permute-start | bytes 196616 | tf_op jit(solution)/shard_map/ppermute | solution.py:294
  14.9 0.9 %shard_map.106 = (bf16[256,128]{1,0:T(8,128)(2,1)S(1)}, f32[2,512,128]{2,1,0:T(8,128)S(1)}) custom-call(f32[1,128]{1,0:T(1,128)S(1)} %get-tuple-element.28.gain, bf16[1024,256]{1,0:T(8,128)(2,1)S(1)} %get-tuple-element.29.forward, bf16[256,1024]{1,0:T(8,128)(2,1)S(1)} %get-tuple-element.30.backward, bf16[128,256]{1,0:T(8,128)(2,1)S(1)} %get-tuple-element.27.after.rest_0_, ...), custom_call_target="tpu_custom_call" | custom-call | tf_op jit(solution)/shard_map/pallas_call | solution.py:63
  15.8 1.6 %collective-permute-start.3 = (bf16[256,128]{1,0:T(8,128)(2,1)S(1)}, bf16[256,128]{1,0:T(8,128)(2,1)S(1)}, u32[]{:S(2)}, u32[]{:S(2)}) collective-permute-start(bf16[256,128]{1,0:T(8,128)(2,1)S(1)} %get-tuple-element.34), channel_id=1, source_target_pairs={{0,16},{16,0},{1,17},{17,1},{2,18},{18,2},{3,19},{19,3},{4,20},{20... | collective-permute-start | bytes 196616 | tf_op jit(solution)/shard_map/ppermute | solution.py:351
  17.5 1.3 %collective-permute-done.6.rest_3_ = bf16[128,256]{1,0:T(8,128)(2,1)S(1)} collective-permute-done((bf16[128,256]{1,0:T(8,128)(2,1)S(1)}, bf16[128,256]{1,0:T(8,128)(2,1)S(1)}, u32[]{:S(2)}, u32[]{:S(2)}) %collective-permute-start.6) | collective-permute-done | bytes 65568 | tf_op jit(solution)/shard_map/ppermute | solution.py:294
  18.8 0.4 %shard_map.107 = (f32[2,256,128]{2,1,0:T(8,128)S(1)}, f32[2,256,128]{2,1,0:T(8,128)S(1)}, f32[2,512,128]{2,1,0:T(8,128)S(1)}, f32[2,512,128]{2,1,0:T(8,128)S(1)}) custom-call(bf16[1024,256]{1,0:T(8,128)(2,1)S(1)} %get-tuple-element.29.forward, f32[2,512,128]{2,1,0:T(8,128)S(1)} %get-tuple-element.35.spectra, bf16[128,256]{1,0:T(8,128)(2,1)S(1)} %get-tuple-element.36.rest_0_, ...), custom_call_target="tpu_custom_call" | custom-call | tf_op jit(solution)/shard_map/pallas_call | solution.py:63
  19.2 1.0 %collective-permute-done.3.received = bf16[256,128]{1,0:T(8,128)(2,1)S(1)} collective-permute-done((bf16[256,128]{1,0:T(8,128)(2,1)S(1)}, bf16[256,128]{1,0:T(8,128)(2,1)S(1)}, u32[]{:S(2)}, u32[]{:S(2)}) %collective-permute-start.3) | collective-permute-done | bytes 65568 | tf_op jit(solution)/shard_map/ppermute | solution.py:351
  20.1 0.9 %shard_map.108 = (bf16[128,128]{1,0:T(8,128)(2,1)S(1)}, bf16[128,128]{1,0:T(8,128)(2,1)S(1)}, bf16[128,128]{1,0:T(8,128)(2,1)S(1)}, bf16[128,128]{1,0:T(8,128)(2,1)S(1)}) custom-call(f32[1,128]{1,0:T(1,128)S(1)} %get-tuple-element.28.gain, bf16[1024,256]{1,0:T(8,128)(2,1)S(1)} %get-tuple-element.29.forward, ...), custom_call_target="tpu_custom_call" | custom-call | tf_op jit(solution)/shard_map/pallas_call | solution.py:63
  21.0 1.6 %collective-permute-start.7 = (bf16[128,128]{1,0:T(8,128)(2,1)S(1)}, bf16[128,128]{1,0:T(8,128)(2,1)S(1)}, u32[]{:S(2)}, u32[]{:S(2)}) collective-permute-start(bf16[128,128]{1,0:T(8,128)(2,1)S(1)} %get-tuple-element.45), channel_id=1, source_target_pairs={{0,12},{4,8},{8,4},{12,0},{16,28},{20,24},{24,20},{28,16},{1,13},{... | collective-permute-start | bytes 98312 | tf_op jit(solution)/shard_map/ppermute | solution.py:294
  22.7 2.8 %collective-permute-start.9 = (bf16[128,128]{1,0:T(8,128)(2,1)S(1)}, bf16[128,128]{1,0:T(8,128)(2,1)S(1)}, u32[]{:S(2)}, u32[]{:S(2)}) collective-permute-start(bf16[128,128]{1,0:T(8,128)(2,1)S(1)} %get-tuple-element.47), channel_id=1, source_target_pairs={{0,8},{4,12},{8,0},{12,4},{16,24},{20,28},{24,16},{28,20},{1,9},{5... | collective-permute-start | bytes 98312 | tf_op jit(solution)/shard_map/ppermute | solution.py:294
  25.5 1.4 %collective-permute-done.7.rest_1_ = bf16[128,128]{1,0:T(8,128)(2,1)S(1)} collective-permute-done((bf16[128,128]{1,0:T(8,128)(2,1)S(1)}, bf16[128,128]{1,0:T(8,128)(2,1)S(1)}, u32[]{:S(2)}, u32[]{:S(2)}) %collective-permute-start.7) | collective-permute-done | bytes 32800 | tf_op jit(solution)/shard_map/ppermute | solution.py:294
  26.9 0.6 %collective-permute-done.9.rest_3_ = bf16[128,128]{1,0:T(8,128)(2,1)S(1)} collective-permute-done((bf16[128,128]{1,0:T(8,128)(2,1)S(1)}, bf16[128,128]{1,0:T(8,128)(2,1)S(1)}, u32[]{:S(2)}, u32[]{:S(2)}) %collective-permute-start.9) | collective-permute-done | bytes 32800 | tf_op jit(solution)/shard_map/ppermute | solution.py:294
  27.8 1.6 %collective-permute-start.11 = (bf16[64,128]{1,0:T(8,128)(2,1)S(1)}, bf16[64,128]{1,0:T(8,128)(2,1)S(1)}, u32[]{:S(2)}, u32[]{:S(2)}) collective-permute-start(bf16[64,128]{1,0:T(8,128)(2,1)S(1)} %get-tuple-element.50), channel_id=1, source_target_pairs={{0,2},{1,3},{2,0},{3,1},{4,6},{5,7},{6,4},{7,5},{8,10},{9,11},{10,... | collective-permute-start | bytes 49160 | tf_op jit(solution)/shard_map/ppermute | solution.py:285
  29.3 0.3 collective-permute-start.12
  29.6 0.7 %shard_map.109 = bf16[1,128,256]{2,1,0:T(8,128)(2,1)} custom-call(bf16[128,128]{1,0:T(8,128)(2,1)S(1)} %get-tuple-element.44.rest_0_, bf16[128,128]{1,0:T(8,128)(2,1)S(1)} %collective-permute-done.7.rest_1_, bf16[128,128]{1,0:T(8,128)(2,1)S(1)} %collective-permute-done.8.rest_2_, bf16[128,128]{1,0:T(8,128)(2,1)S(1)} %collective-permute-done.9.rest_3_), custom_call_target="tpu_custom_call" | custom-call | tf_op jit(solution)/shard_map/pallas_call | solution.py:63
  30.3 0.7 %collective-permute-done.10.refs_1_ = bf16[64,128]{1,0:T(8,128)(2,1)S(1)} collective-permute-done((bf16[64,128]{1,0:T(8,128)(2,1)S(1)}, bf16[64,128]{1,0:T(8,128)(2,1)S(1)}, u32[]{:S(2)}, u32[]{:S(2)}) %collective-permute-start.10) | collective-permute-done | bytes 16416 | tf_op jit(solution)/shard_map/ppermute | solution.py:285
  31.0 0.6 %collective-permute-done.11.refs_2_ = bf16[64,128]{1,0:T(8,128)(2,1)S(1)} collective-permute-done((bf16[64,128]{1,0:T(8,128)(2,1)S(1)}, bf16[64,128]{1,0:T(8,128)(2,1)S(1)}, u32[]{:S(2)}, u32[]{:S(2)}) %collective-permute-start.11) | collective-permute-done | bytes 16416 | tf_op jit(solution)/shard_map/ppermute | solution.py:285
  31.6 0.6 %shard_map.111 = f32[64,128]{1,0:T(8,128)} custom-call(bf16[64,128]{1,0:T(8,128)(2,1)S(1)} %get-tuple-element.48.refs_0_, bf16[64,128]{1,0:T(8,128)(2,1)S(1)} %collective-permute-done.10.refs_1_, bf16[64,128]{1,0:T(8,128)(2,1)S(1)} %collective-permute-done.11.refs_2_, bf16[64,128]{1,0:T(8,128)(2,1)S(1)} %collective-permute-done.12.refs_3_), custom_call_target="tpu_custom_call" | custom-call | tf_op jit(solution)/shard_map/pallas_call | solution.py:63
  (10 shorter events, 0.4 us)
Async XLA Ops:
  1.9 10.7 %collective-permute-start = (bf16[128,256]{1,0:T(8,128)(2,1)S(1)}, bf16[128,256]{1,0:T(8,128)(2,1)S(1)}, u32[]{:S(2)}, u32[]{:S(2)}) collective-permute-start(bf16[128,256]{1,0:T(8,128)(2,1)S(1)} %get-tuple-element.31), channel_id=1, source_target_pairs={{0,8},{4,12},{8,0},{12,4},{16,24},{20,28},{24,16},{28,20},{1,9},{5... | collective-permute-start | bytes 196616 | tf_op jit(solution)/shard_map/ppermute | solution.py:294
  6.0 8.9 %collective-permute-start.1 = (bf16[128,256]{1,0:T(8,128)(2,1)S(1)}, bf16[128,256]{1,0:T(8,128)(2,1)S(1)}, u32[]{:S(2)}, u32[]{:S(2)}) collective-permute-start(bf16[128,256]{1,0:T(8,128)(2,1)S(1)} %get-tuple-element.32), channel_id=1, source_target_pairs={{0,12},{4,8},{8,4},{12,0},{16,28},{20,24},{24,20},{28,16},{1,13},{... | collective-permute-start | bytes 196616 | tf_op jit(solution)/shard_map/ppermute | solution.py:294
  7.3 7.5 %collective-permute-start.2 = (bf16[128,256]{1,0:T(8,128)(2,1)S(1)}, bf16[128,256]{1,0:T(8,128)(2,1)S(1)}, u32[]{:S(2)}, u32[]{:S(2)}) collective-permute-start(bf16[128,256]{1,0:T(8,128)(2,1)S(1)} %get-tuple-element.33), channel_id=1, source_target_pairs={{0,4},{4,0},{8,12},{12,8},{16,20},{20,16},{24,28},{28,24},{1,5},{5... | collective-permute-start | bytes 196616 | tf_op jit(solution)/shard_map/ppermute | solution.py:294
  9.0 8.3 %collective-permute-start.4 = (bf16[128,256]{1,0:T(8,128)(2,1)S(1)}, bf16[128,256]{1,0:T(8,128)(2,1)S(1)}, u32[]{:S(2)}, u32[]{:S(2)}) collective-permute-start(bf16[128,256]{1,0:T(8,128)(2,1)S(1)} %get-tuple-element.37), channel_id=1, source_target_pairs={{0,4},{4,0},{8,12},{12,8},{16,24},{20,28},{24,16},{28,20},{1,5},{5... | collective-permute-start | bytes 196616 | tf_op jit(solution)/shard_map/ppermute | solution.py:294
  10.9 6.6 %collective-permute-start.5 = (bf16[128,256]{1,0:T(8,128)(2,1)S(1)}, bf16[128,256]{1,0:T(8,128)(2,1)S(1)}, u32[]{:S(2)}, u32[]{:S(2)}) collective-permute-start(bf16[128,256]{1,0:T(8,128)(2,1)S(1)} %get-tuple-element.38), channel_id=1, source_target_pairs={{0,8},{4,12},{8,0},{12,4},{16,20},{20,16},{24,28},{28,24},{1,9},{5... | collective-permute-start | bytes 196616 | tf_op jit(solution)/shard_map/ppermute | solution.py:294
  12.6 6.2 %collective-permute-start.6 = (bf16[128,256]{1,0:T(8,128)(2,1)S(1)}, bf16[128,256]{1,0:T(8,128)(2,1)S(1)}, u32[]{:S(2)}, u32[]{:S(2)}) collective-permute-start(bf16[128,256]{1,0:T(8,128)(2,1)S(1)} %get-tuple-element.39), channel_id=1, source_target_pairs={{0,12},{4,8},{8,4},{12,0},{16,28},{20,24},{24,20},{28,16},{1,13},{... | collective-permute-start | bytes 196616 | tf_op jit(solution)/shard_map/ppermute | solution.py:294
  15.8 4.3 %collective-permute-start.3 = (bf16[256,128]{1,0:T(8,128)(2,1)S(1)}, bf16[256,128]{1,0:T(8,128)(2,1)S(1)}, u32[]{:S(2)}, u32[]{:S(2)}) collective-permute-start(bf16[256,128]{1,0:T(8,128)(2,1)S(1)} %get-tuple-element.34), channel_id=1, source_target_pairs={{0,16},{16,0},{1,17},{17,1},{2,18},{18,2},{3,19},{19,3},{4,20},{20... | collective-permute-start | bytes 196616 | tf_op jit(solution)/shard_map/ppermute | solution.py:351
  21.0 5.9 %collective-permute-start.7 = (bf16[128,128]{1,0:T(8,128)(2,1)S(1)}, bf16[128,128]{1,0:T(8,128)(2,1)S(1)}, u32[]{:S(2)}, u32[]{:S(2)}) collective-permute-start(bf16[128,128]{1,0:T(8,128)(2,1)S(1)} %get-tuple-element.45), channel_id=1, source_target_pairs={{0,12},{4,8},{8,4},{12,0},{16,28},{20,24},{24,20},{28,16},{1,13},{... | collective-permute-start | bytes 98312 | tf_op jit(solution)/shard_map/ppermute | solution.py:294
  22.6 4.3 %collective-permute-start.8 = (bf16[128,128]{1,0:T(8,128)(2,1)S(1)}, bf16[128,128]{1,0:T(8,128)(2,1)S(1)}, u32[]{:S(2)}, u32[]{:S(2)}) collective-permute-start(bf16[128,128]{1,0:T(8,128)(2,1)S(1)} %get-tuple-element.46), channel_id=1, source_target_pairs={{0,4},{4,0},{8,12},{12,8},{16,20},{20,16},{24,28},{28,24},{1,5},{5... | collective-permute-start | bytes 98312 | tf_op jit(solution)/shard_map/ppermute | solution.py:294
  22.7 4.8 %collective-permute-start.9 = (bf16[128,128]{1,0:T(8,128)(2,1)S(1)}, bf16[128,128]{1,0:T(8,128)(2,1)S(1)}, u32[]{:S(2)}, u32[]{:S(2)}) collective-permute-start(bf16[128,128]{1,0:T(8,128)(2,1)S(1)} %get-tuple-element.47), channel_id=1, source_target_pairs={{0,8},{4,12},{8,0},{12,4},{16,24},{20,28},{24,16},{28,20},{1,9},{5... | collective-permute-start | bytes 98312 | tf_op jit(solution)/shard_map/ppermute | solution.py:294
  27.7 3.3 %collective-permute-start.10 = (bf16[64,128]{1,0:T(8,128)(2,1)S(1)}, bf16[64,128]{1,0:T(8,128)(2,1)S(1)}, u32[]{:S(2)}, u32[]{:S(2)}) collective-permute-start(bf16[64,128]{1,0:T(8,128)(2,1)S(1)} %get-tuple-element.49), channel_id=1, source_target_pairs={{0,3},{1,2},{2,1},{3,0},{4,7},{5,6},{6,5},{7,4},{8,11},{9,10},{10,... | collective-permute-start | bytes 49160 | tf_op jit(solution)/shard_map/ppermute | solution.py:285
  27.8 3.8 %collective-permute-start.11 = (bf16[64,128]{1,0:T(8,128)(2,1)S(1)}, bf16[64,128]{1,0:T(8,128)(2,1)S(1)}, u32[]{:S(2)}, u32[]{:S(2)}) collective-permute-start(bf16[64,128]{1,0:T(8,128)(2,1)S(1)} %get-tuple-element.50), channel_id=1, source_target_pairs={{0,2},{1,3},{2,0},{3,1},{4,6},{5,7},{6,4},{7,5},{8,10},{9,11},{10,... | collective-permute-start | bytes 49160 | tf_op jit(solution)/shard_map/ppermute | solution.py:285
  29.3 2.2 %collective-permute-start.12 = (bf16[64,128]{1,0:T(8,128)(2,1)S(1)}, bf16[64,128]{1,0:T(8,128)(2,1)S(1)}, u32[]{:S(2)}, u32[]{:S(2)}) collective-permute-start(bf16[64,128]{1,0:T(8,128)(2,1)S(1)} %get-tuple-element.51), channel_id=1, source_target_pairs={{0,1},{1,0},{2,3},{3,2},{4,5},{5,4},{6,7},{7,6},{8,9},{9,8},{10,11... | collective-permute-start | bytes 49160 | tf_op jit(solution)/shard_map/ppermute | solution.py:285

commit v9 on v8

--- a/solution.py
+++ b/solution.py
@@ -176,10 +176,12 @@
 
 
 def inverse(backward, real, imag):
-    plus, minus = (real + imag) * HALF_TURN, (real - imag) * HALF_TURN
+    length, lanes = real.shape
+    plus, minus = real + imag, real - imag
     real = jnp.concatenate([real, quarters(plus, -minus, -plus, minus)], axis=1)
     imag = jnp.concatenate([imag, quarters(-minus, -plus, minus, plus)], axis=1)
-    return dot(backward[...], jnp.concatenate([real, imag], axis=0).astype(BF16))
+    sums = dot(backward[...], jnp.concatenate([real, imag], axis=0).astype(BF16))
+    return sums[:, :lanes] * (1.0 / length), sums[:, lanes:] * (HALF_TURN / length)
 
 
 def times_conj(real, imag, other_real, other_imag):
@@ -197,16 +199,14 @@
 def first_tick(gain, forward, backward, *rest):
     *chunks, out, spectra, held = rest
     gather_positions(chunks, first_steps(len(chunks)), held)
-    length, lanes = held.shape[0], gain.shape[1]
     parts = halves(held)
     real, imag = spectrum(forward, parts[0][0], parts[1][0])
     spectra[0], spectra[1] = real, imag
-    both = inverse(backward, *times_conj(real, imag, swap(real), swap(imag))) * (1.0 / length)
+    convolved = inverse(backward, *times_conj(real, imag, swap(real), swap(imag)))
     gradients = []
     for part, (first, second) in enumerate(parts):
-        correlated = both[:, part * lanes : (part + 1) * lanes]
         kept = second.astype(F32)
-        gradient = kept + swap(kept) * (correlated + gain[...] * first.astype(F32))
+        gradient = kept + swap(kept) * (convolved[part] + gain[...] * first.astype(F32))
         gradients.append(jnp.where(lax.axis_index("section") == 0, kept, gradient))
     top, bottom = gradients
     out[...] = jnp.where(first_unit(top), swap(top), bottom).astype(BF16)
@@ -232,17 +232,16 @@
 
 def second_tick(gain, forward, backward, received, post, weight, other, lag_spec, *rest):
     *outs, stage = rest
-    count, rows, lanes = stage.shape
-    length = count * rows
+    count, rows, _ = stage.shape
     carried = received[...].astype(F32)
     low = first_unit(carried)
     carried = [jnp.where(low, carried, swap(carried)), jnp.where(low, swap(carried), carried)]
     gated = [(post[part] * carried[part]).astype(BF16) for part in range(2)]
     real, imag = times_conj(*spectrum(forward, *gated), other[0], other[1])
-    both = inverse(backward, real + lag_spec[0], imag + lag_spec[1]) * (1.0 / length)
+    convolved = inverse(backward, real + lag_spec[0], imag + lag_spec[1])
     for part in range(2):
         skipped = jnp.where(low, gain[...] * gated[part].astype(F32), 0.0)
-        result = weight[part] * (both[:, part * lanes : (part + 1) * lanes] + skipped)
+        result = weight[part] * (convolved[part] + skipped)
         result = jnp.where(low, carried[part] + result, result).astype(BF16)
         for block in range(count // 2):
             stage[part * (count // 2) + block] = result[block * rows : (block + 1) * rows]

time: 32.4 us -> 32.3 us (level)
  no operation moved by 1% of the time
where the time goes in v9:
time: 32.3 us; the launch traced here: 32.2 us
  starting transfers between devices  19.4 us (60%)
  Pallas kernels  6.45 us (20%)
  waiting for transfers between devices  5.6 us (17%)
  between operations  0.69 us (2%)
    ppermute x9, starting transfers between devices, exchange_seq(): lax.ppermute(chunk, ('section', 'seq'), [(section * size + seq, section *...  16 us
    pallas_call x8, Pallas kernels, run(): pl.pallas_call(kernel, out_shape=out_shape, in_specs=[pl.BlockSpec(memory...  6.45 us
    ppermute x9, waiting for transfers between devices, exchange_seq(): lax.ppermute(chunk, ('section', 'seq'), [(section * size + seq, section *...  3.42 us
    ppermute x3, starting transfers between devices, exchange_chan(): lax.ppermute(chunks[step], 'chan', [(i, i ^ step) for i in range(size)])  1.92 us
    ppermute x1, starting transfers between devices, body(): received = lax.ppermute(gradient, 'section', ring)  1.56 us
    ppermute x3, waiting for transfers between devices, exchange_chan(): lax.ppermute(chunks[step], 'chan', [(i, i ^ step) for i in range(size)])  1.23 us
    ppermute x1, waiting for transfers between devices, body(): received = lax.ppermute(gradient, 'section', ring)  0.95 us
  transfers between devices with their start and end apart: 13, of which 7 were waited for; matrix products, arithmetic and copies ran while one was open for 0% of the time, Pallas kernels for 11%

profile of v9, /device:TPU:0, one launch (start us, length us, event | category | flops | bytes accessed | tf_op | source)
XLA Modules:
  0.0 32.2 jit_solution(14899336091028752148)
XLA Ops:
  0.6 1.2 %shard_map.104 = (bf16[128,256]{1,0:T(8,128)(2,1)S(1)}, bf16[128,256]{1,0:T(8,128)(2,1)S(1)}, bf16[128,256]{1,0:T(8,128)(2,1)S(1)}, bf16[128,256]{1,0:T(8,128)(2,1)S(1)}) custom-call(bf16[1,2,128,256]{3,2,1,0:T(8,128)(2,1)} %post.3, bf16[1,128,256]{2,1,0:T(8,128)(2,1)} %held.1, bf16[128,256]{1,0:T(8,128)(2,1)} %loss.1, bf16[1,2,128,256]{3,2,1,0:T(8,128)(2,1)} %pre.3, ...), custom_call_target="tpu_custom_call" | custom-call | tf_op jit(solution)/shard_map/pallas_call | solution.py:63
  1.9 4.1 %collective-permute-start = (bf16[128,256]{1,0:T(8,128)(2,1)S(1)}, bf16[128,256]{1,0:T(8,128)(2,1)S(1)}, u32[]{:S(2)}, u32[]{:S(2)}) collective-permute-start(bf16[128,256]{1,0:T(8,128)(2,1)S(1)} %get-tuple-element.31), channel_id=1, source_target_pairs={{0,8},{4,12},{8,0},{12,4},{16,24},{20,28},{24,16},{28,20},{1,9},{5... | collective-permute-start | bytes 196616 | tf_op jit(solution)/shard_map/ppermute | solution.py:293
  6.0 1.3 %collective-permute-start.1 = (bf16[128,256]{1,0:T(8,128)(2,1)S(1)}, bf16[128,256]{1,0:T(8,128)(2,1)S(1)}, u32[]{:S(2)}, u32[]{:S(2)}) collective-permute-start(bf16[128,256]{1,0:T(8,128)(2,1)S(1)} %get-tuple-element.32), channel_id=1, source_target_pairs={{0,12},{4,8},{8,4},{12,0},{16,28},{20,24},{24,20},{28,16},{1,13},{... | collective-permute-start | bytes 196616 | tf_op jit(solution)/shard_map/ppermute | solution.py:293
  7.3 0.2 collective-permute-start.2
  7.6 1.5 %shard_map.105 = (bf16[128,256]{1,0:T(8,128)(2,1)S(1)}, bf16[128,256]{1,0:T(8,128)(2,1)S(1)}, bf16[128,256]{1,0:T(8,128)(2,1)S(1)}, bf16[128,256]{1,0:T(8,128)(2...) custom-call(bf16[128,256]{1,0:T(8,128)(2,1)S(1)} %get-tuple-element.27.after.rest_0_, ...), custom_call_target="tpu_custom_call" | custom-call | tf_op jit(solution)/shard_map/pallas_call | solution.py:63
  9.0 1.9 %collective-permute-start.4 = (bf16[128,256]{1,0:T(8,128)(2,1)S(1)}, bf16[128,256]{1,0:T(8,128)(2,1)S(1)}, u32[]{:S(2)}, u32[]{:S(2)}) collective-permute-start(bf16[128,256]{1,0:T(8,128)(2,1)S(1)} %get-tuple-element.37), channel_id=1, source_target_pairs={{0,4},{4,0},{8,12},{12,8},{16,24},{20,28},{24,16},{28,20},{1,5},{5... | collective-permute-start | bytes 196616 | tf_op jit(solution)/shard_map/ppermute | solution.py:293
  10.9 1.7 %collective-permute-start.5 = (bf16[128,256]{1,0:T(8,128)(2,1)S(1)}, bf16[128,256]{1,0:T(8,128)(2,1)S(1)}, u32[]{:S(2)}, u32[]{:S(2)}) collective-permute-start(bf16[128,256]{1,0:T(8,128)(2,1)S(1)} %get-tuple-element.38), channel_id=1, source_target_pairs={{0,8},{4,12},{8,0},{12,4},{16,20},{20,16},{24,28},{28,24},{1,9},{5... | collective-permute-start | bytes 196616 | tf_op jit(solution)/shard_map/ppermute | solution.py:293
  12.6 2.3 %collective-permute-start.6 = (bf16[128,256]{1,0:T(8,128)(2,1)S(1)}, bf16[128,256]{1,0:T(8,128)(2,1)S(1)}, u32[]{:S(2)}, u32[]{:S(2)}) collective-permute-start(bf16[128,256]{1,0:T(8,128)(2,1)S(1)} %get-tuple-element.39), channel_id=1, source_target_pairs={{0,12},{4,8},{8,4},{12,0},{16,28},{20,24},{24,20},{28,16},{1,13},{... | collective-permute-start | bytes 196616 | tf_op jit(solution)/shard_map/ppermute | solution.py:293
  14.9 0.9 %shard_map.106 = (bf16[256,128]{1,0:T(8,128)(2,1)S(1)}, f32[2,512,128]{2,1,0:T(8,128)S(1)}) custom-call(f32[1,128]{1,0:T(1,128)S(1)} %get-tuple-element.28.gain, bf16[1024,256]{1,0:T(8,128)(2,1)S(1)} %get-tuple-element.29.forward, bf16[256,1024]{1,0:T(8,128)(2,1)S(1)} %get-tuple-element.30.backward, bf16[128,256]{1,0:T(8,128)(2,1)S(1)} %get-tuple-element.27.after.rest_0_, ...), custom_call_target="tpu_custom_call" | custom-call | tf_op jit(solution)/shard_map/pallas_call | solution.py:63
  15.8 1.6 %collective-permute-start.3 = (bf16[256,128]{1,0:T(8,128)(2,1)S(1)}, bf16[256,128]{1,0:T(8,128)(2,1)S(1)}, u32[]{:S(2)}, u32[]{:S(2)}) collective-permute-start(bf16[256,128]{1,0:T(8,128)(2,1)S(1)} %get-tuple-element.34), channel_id=1, source_target_pairs={{0,16},{16,0},{1,17},{17,1},{2,18},{18,2},{3,19},{19,3},{4,20},{20... | collective-permute-start | bytes 196616 | tf_op jit(solution)/shard_map/ppermute | solution.py:350
  17.5 1.3 %collective-permute-done.6.rest_3_ = bf16[128,256]{1,0:T(8,128)(2,1)S(1)} collective-permute-done((bf16[128,256]{1,0:T(8,128)(2,1)S(1)}, bf16[128,256]{1,0:T(8,128)(2,1)S(1)}, u32[]{:S(2)}, u32[]{:S(2)}) %collective-permute-start.6) | collective-permute-done | bytes 65568 | tf_op jit(solution)/shard_map/ppermute | solution.py:293
  18.8 0.4 %shard_map.107 = (f32[2,256,128]{2,1,0:T(8,128)S(1)}, f32[2,256,128]{2,1,0:T(8,128)S(1)}, f32[2,512,128]{2,1,0:T(8,128)S(1)}, f32[2,512,128]{2,1,0:T(8,128)S(1)}) custom-call(bf16[1024,256]{1,0:T(8,128)(2,1)S(1)} %get-tuple-element.29.forward, f32[2,512,128]{2,1,0:T(8,128)S(1)} %get-tuple-element.35.spectra, bf16[128,256]{1,0:T(8,128)(2,1)S(1)} %get-tuple-element.36.rest_0_, ...), custom_call_target="tpu_custom_call" | custom-call | tf_op jit(solution)/shard_map/pallas_call | solution.py:63
  19.2 1.0 %collective-permute-done.3.received = bf16[256,128]{1,0:T(8,128)(2,1)S(1)} collective-permute-done((bf16[256,128]{1,0:T(8,128)(2,1)S(1)}, bf16[256,128]{1,0:T(8,128)(2,1)S(1)}, u32[]{:S(2)}, u32[]{:S(2)}) %collective-permute-start.3) | collective-permute-done | bytes 65568 | tf_op jit(solution)/shard_map/ppermute | solution.py:350
  20.1 0.9 %shard_map.108 = (bf16[128,128]{1,0:T(8,128)(2,1)S(1)}, bf16[128,128]{1,0:T(8,128)(2,1)S(1)}, bf16[128,128]{1,0:T(8,128)(2,1)S(1)}, bf16[128,128]{1,0:T(8,128)(2,1)S(1)}) custom-call(f32[1,128]{1,0:T(1,128)S(1)} %get-tuple-element.28.gain, bf16[1024,256]{1,0:T(8,128)(2,1)S(1)} %get-tuple-element.29.forward, ...), custom_call_target="tpu_custom_call" | custom-call | tf_op jit(solution)/shard_map/pallas_call | solution.py:63
  21.0 1.6 %collective-permute-start.7 = (bf16[128,128]{1,0:T(8,128)(2,1)S(1)}, bf16[128,128]{1,0:T(8,128)(2,1)S(1)}, u32[]{:S(2)}, u32[]{:S(2)}) collective-permute-start(bf16[128,128]{1,0:T(8,128)(2,1)S(1)} %get-tuple-element.45), channel_id=1, source_target_pairs={{0,12},{4,8},{8,4},{12,0},{16,28},{20,24},{24,20},{28,16},{1,13},{... | collective-permute-start | bytes 98312 | tf_op jit(solution)/shard_map/ppermute | solution.py:293
  22.7 2.8 %collective-permute-start.9 = (bf16[128,128]{1,0:T(8,128)(2,1)S(1)}, bf16[128,128]{1,0:T(8,128)(2,1)S(1)}, u32[]{:S(2)}, u32[]{:S(2)}) collective-permute-start(bf16[128,128]{1,0:T(8,128)(2,1)S(1)} %get-tuple-element.47), channel_id=1, source_target_pairs={{0,8},{4,12},{8,0},{12,4},{16,24},{20,28},{24,16},{28,20},{1,9},{5... | collective-permute-start | bytes 98312 | tf_op jit(solution)/shard_map/ppermute | solution.py:293
  25.5 1.4 %collective-permute-done.7.rest_1_ = bf16[128,128]{1,0:T(8,128)(2,1)S(1)} collective-permute-done((bf16[128,128]{1,0:T(8,128)(2,1)S(1)}, bf16[128,128]{1,0:T(8,128)(2,1)S(1)}, u32[]{:S(2)}, u32[]{:S(2)}) %collective-permute-start.7) | collective-permute-done | bytes 32800 | tf_op jit(solution)/shard_map/ppermute | solution.py:293
  26.9 0.6 %collective-permute-done.9.rest_3_ = bf16[128,128]{1,0:T(8,128)(2,1)S(1)} collective-permute-done((bf16[128,128]{1,0:T(8,128)(2,1)S(1)}, bf16[128,128]{1,0:T(8,128)(2,1)S(1)}, u32[]{:S(2)}, u32[]{:S(2)}) %collective-permute-start.9) | collective-permute-done | bytes 32800 | tf_op jit(solution)/shard_map/ppermute | solution.py:293
  27.7 1.6 %collective-permute-start.11 = (bf16[64,128]{1,0:T(8,128)(2,1)S(1)}, bf16[64,128]{1,0:T(8,128)(2,1)S(1)}, u32[]{:S(2)}, u32[]{:S(2)}) collective-permute-start(bf16[64,128]{1,0:T(8,128)(2,1)S(1)} %get-tuple-element.50), channel_id=1, source_target_pairs={{0,2},{1,3},{2,0},{3,1},{4,6},{5,7},{6,4},{7,5},{8,10},{9,11},{10,... | collective-permute-start | bytes 49160 | tf_op jit(solution)/shard_map/ppermute | solution.py:284
  29.3 0.3 collective-permute-start.12
  29.6 0.7 %shard_map.109 = bf16[1,128,256]{2,1,0:T(8,128)(2,1)} custom-call(bf16[128,128]{1,0:T(8,128)(2,1)S(1)} %get-tuple-element.44.rest_0_, bf16[128,128]{1,0:T(8,128)(2,1)S(1)} %collective-permute-done.7.rest_1_, bf16[128,128]{1,0:T(8,128)(2,1)S(1)} %collective-permute-done.8.rest_2_, bf16[128,128]{1,0:T(8,128)(2,1)S(1)} %collective-permute-done.9.rest_3_), custom_call_target="tpu_custom_call" | custom-call | tf_op jit(solution)/shard_map/pallas_call | solution.py:63
  30.3 0.7 %collective-permute-done.10.refs_1_ = bf16[64,128]{1,0:T(8,128)(2,1)S(1)} collective-permute-done((bf16[64,128]{1,0:T(8,128)(2,1)S(1)}, bf16[64,128]{1,0:T(8,128)(2,1)S(1)}, u32[]{:S(2)}, u32[]{:S(2)}) %collective-permute-start.10) | collective-permute-done | bytes 16416 | tf_op jit(solution)/shard_map/ppermute | solution.py:284
  31.0 0.6 %collective-permute-done.11.refs_2_ = bf16[64,128]{1,0:T(8,128)(2,1)S(1)} collective-permute-done((bf16[64,128]{1,0:T(8,128)(2,1)S(1)}, bf16[64,128]{1,0:T(8,128)(2,1)S(1)}, u32[]{:S(2)}, u32[]{:S(2)}) %collective-permute-start.11) | collective-permute-done | bytes 16416 | tf_op jit(solution)/shard_map/ppermute | solution.py:284
  31.6 0.6 %shard_map.111 = f32[64,128]{1,0:T(8,128)} custom-call(bf16[64,128]{1,0:T(8,128)(2,1)S(1)} %get-tuple-element.48.refs_0_, bf16[64,128]{1,0:T(8,128)(2,1)S(1)} %collective-permute-done.10.refs_1_, bf16[64,128]{1,0:T(8,128)(2,1)S(1)} %collective-permute-done.11.refs_2_, bf16[64,128]{1,0:T(8,128)(2,1)S(1)} %collective-permute-done.12.refs_3_), custom_call_target="tpu_custom_call" | custom-call | tf_op jit(solution)/shard_map/pallas_call | solution.py:63
  (10 shorter events, 0.4 us)
Async XLA Ops:
  1.9 10.7 %collective-permute-start = (bf16[128,256]{1,0:T(8,128)(2,1)S(1)}, bf16[128,256]{1,0:T(8,128)(2,1)S(1)}, u32[]{:S(2)}, u32[]{:S(2)}) collective-permute-start(bf16[128,256]{1,0:T(8,128)(2,1)S(1)} %get-tuple-element.31), channel_id=1, source_target_pairs={{0,8},{4,12},{8,0},{12,4},{16,24},{20,28},{24,16},{28,20},{1,9},{5... | collective-permute-start | bytes 196616 | tf_op jit(solution)/shard_map/ppermute | solution.py:293
  6.0 8.9 %collective-permute-start.1 = (bf16[128,256]{1,0:T(8,128)(2,1)S(1)}, bf16[128,256]{1,0:T(8,128)(2,1)S(1)}, u32[]{:S(2)}, u32[]{:S(2)}) collective-permute-start(bf16[128,256]{1,0:T(8,128)(2,1)S(1)} %get-tuple-element.32), channel_id=1, source_target_pairs={{0,12},{4,8},{8,4},{12,0},{16,28},{20,24},{24,20},{28,16},{1,13},{... | collective-permute-start | bytes 196616 | tf_op jit(solution)/shard_map/ppermute | solution.py:293
  7.3 7.5 %collective-permute-start.2 = (bf16[128,256]{1,0:T(8,128)(2,1)S(1)}, bf16[128,256]{1,0:T(8,128)(2,1)S(1)}, u32[]{:S(2)}, u32[]{:S(2)}) collective-permute-start(bf16[128,256]{1,0:T(8,128)(2,1)S(1)} %get-tuple-element.33), channel_id=1, source_target_pairs={{0,4},{4,0},{8,12},{12,8},{16,20},{20,16},{24,28},{28,24},{1,5},{5... | collective-permute-start | bytes 196616 | tf_op jit(solution)/shard_map/ppermute | solution.py:293
  9.0 8.3 %collective-permute-start.4 = (bf16[128,256]{1,0:T(8,128)(2,1)S(1)}, bf16[128,256]{1,0:T(8,128)(2,1)S(1)}, u32[]{:S(2)}, u32[]{:S(2)}) collective-permute-start(bf16[128,256]{1,0:T(8,128)(2,1)S(1)} %get-tuple-element.37), channel_id=1, source_target_pairs={{0,4},{4,0},{8,12},{12,8},{16,24},{20,28},{24,16},{28,20},{1,5},{5... | collective-permute-start | bytes 196616 | tf_op jit(solution)/shard_map/ppermute | solution.py:293
  10.9 6.6 %collective-permute-start.5 = (bf16[128,256]{1,0:T(8,128)(2,1)S(1)}, bf16[128,256]{1,0:T(8,128)(2,1)S(1)}, u32[]{:S(2)}, u32[]{:S(2)}) collective-permute-start(bf16[128,256]{1,0:T(8,128)(2,1)S(1)} %get-tuple-element.38), channel_id=1, source_target_pairs={{0,8},{4,12},{8,0},{12,4},{16,20},{20,16},{24,28},{28,24},{1,9},{5... | collective-permute-start | bytes 196616 | tf_op jit(solution)/shard_map/ppermute | solution.py:293
  12.6 6.2 %collective-permute-start.6 = (bf16[128,256]{1,0:T(8,128)(2,1)S(1)}, bf16[128,256]{1,0:T(8,128)(2,1)S(1)}, u32[]{:S(2)}, u32[]{:S(2)}) collective-permute-start(bf16[128,256]{1,0:T(8,128)(2,1)S(1)} %get-tuple-element.39), channel_id=1, source_target_pairs={{0,12},{4,8},{8,4},{12,0},{16,28},{20,24},{24,20},{28,16},{1,13},{... | collective-permute-start | bytes 196616 | tf_op jit(solution)/shard_map/ppermute | solution.py:293
  15.8 4.3 %collective-permute-start.3 = (bf16[256,128]{1,0:T(8,128)(2,1)S(1)}, bf16[256,128]{1,0:T(8,128)(2,1)S(1)}, u32[]{:S(2)}, u32[]{:S(2)}) collective-permute-start(bf16[256,128]{1,0:T(8,128)(2,1)S(1)} %get-tuple-element.34), channel_id=1, source_target_pairs={{0,16},{16,0},{1,17},{17,1},{2,18},{18,2},{3,19},{19,3},{4,20},{20... | collective-permute-start | bytes 196616 | tf_op jit(solution)/shard_map/ppermute | solution.py:350
  21.0 5.9 %collective-permute-start.7 = (bf16[128,128]{1,0:T(8,128)(2,1)S(1)}, bf16[128,128]{1,0:T(8,128)(2,1)S(1)}, u32[]{:S(2)}, u32[]{:S(2)}) collective-permute-start(bf16[128,128]{1,0:T(8,128)(2,1)S(1)} %get-tuple-element.45), channel_id=1, source_target_pairs={{0,12},{4,8},{8,4},{12,0},{16,28},{20,24},{24,20},{28,16},{1,13},{... | collective-permute-start | bytes 98312 | tf_op jit(solution)/shard_map/ppermute | solution.py:293
  22.6 4.3 %collective-permute-start.8 = (bf16[128,128]{1,0:T(8,128)(2,1)S(1)}, bf16[128,128]{1,0:T(8,128)(2,1)S(1)}, u32[]{:S(2)}, u32[]{:S(2)}) collective-permute-start(bf16[128,128]{1,0:T(8,128)(2,1)S(1)} %get-tuple-element.46), channel_id=1, source_target_pairs={{0,4},{4,0},{8,12},{12,8},{16,20},{20,16},{24,28},{28,24},{1,5},{5... | collective-permute-start | bytes 98312 | tf_op jit(solution)/shard_map/ppermute | solution.py:293
  22.7 4.8 %collective-permute-start.9 = (bf16[128,128]{1,0:T(8,128)(2,1)S(1)}, bf16[128,128]{1,0:T(8,128)(2,1)S(1)}, u32[]{:S(2)}, u32[]{:S(2)}) collective-permute-start(bf16[128,128]{1,0:T(8,128)(2,1)S(1)} %get-tuple-element.47), channel_id=1, source_target_pairs={{0,8},{4,12},{8,0},{12,4},{16,24},{20,28},{24,16},{28,20},{1,9},{5... | collective-permute-start | bytes 98312 | tf_op jit(solution)/shard_map/ppermute | solution.py:293
  27.7 3.3 %collective-permute-start.10 = (bf16[64,128]{1,0:T(8,128)(2,1)S(1)}, bf16[64,128]{1,0:T(8,128)(2,1)S(1)}, u32[]{:S(2)}, u32[]{:S(2)}) collective-permute-start(bf16[64,128]{1,0:T(8,128)(2,1)S(1)} %get-tuple-element.49), channel_id=1, source_target_pairs={{0,3},{1,2},{2,1},{3,0},{4,7},{5,6},{6,5},{7,4},{8,11},{9,10},{10,... | collective-permute-start | bytes 49160 | tf_op jit(solution)/shard_map/ppermute | solution.py:284
  27.7 3.8 %collective-permute-start.11 = (bf16[64,128]{1,0:T(8,128)(2,1)S(1)}, bf16[64,128]{1,0:T(8,128)(2,1)S(1)}, u32[]{:S(2)}, u32[]{:S(2)}) collective-permute-start(bf16[64,128]{1,0:T(8,128)(2,1)S(1)} %get-tuple-element.50), channel_id=1, source_target_pairs={{0,2},{1,3},{2,0},{3,1},{4,6},{5,7},{6,4},{7,5},{8,10},{9,11},{10,... | collective-permute-start | bytes 49160 | tf_op jit(solution)/shard_map/ppermute | solution.py:284
  29.3 2.2 %collective-permute-start.12 = (bf16[64,128]{1,0:T(8,128)(2,1)S(1)}, bf16[64,128]{1,0:T(8,128)(2,1)S(1)}, u32[]{:S(2)}, u32[]{:S(2)}) collective-permute-start(bf16[64,128]{1,0:T(8,128)(2,1)S(1)} %get-tuple-element.51), channel_id=1, source_target_pairs={{0,1},{1,0},{2,3},{3,2},{4,5},{5,4},{6,7},{7,6},{8,9},{9,8},{10,11... | collective-permute-start | bytes 49160 | tf_op jit(solution)/shard_map/ppermute | solution.py:284

commit v10 on v9

--- a/solution.py
+++ b/solution.py
@@ -267,7 +267,7 @@
     for step, chunk in zip([OWN, *last_steps(count)], chunks):
         stage[place(step)] = chunk[...]
     lag_grad = jnp.concatenate([stage[block][:, unit:] for block in range(count)], axis=1)
-    lag_stage[...] = lag_grad.astype(F32).T.astype(BF16)
+    lag_stage[...] = lag_grad.T
     for step, lag in enumerate(lags):
         width = lag.shape[0]
         lag[...] = lag_stage[pl.ds(pl.multiple_of((chan_index ^ step) * width, width), width), :]

time: 32.3 us -> 32.3 us (level)
  no operation moved by 1% of the time
where the time goes in v10:
time: 32.3 us; the launch traced here: 32.2 us
  starting transfers between devices  19.4 us (60%)
  Pallas kernels  6.42 us (20%)
  waiting for transfers between devices  5.6 us (17%)
  between operations  0.69 us (2%)
    ppermute x9, starting transfers between devices, exchange_seq(): lax.ppermute(chunk, ('section', 'seq'), [(section * size + seq, section *...  16 us
    pallas_call x8, Pallas kernels, run(): pl.pallas_call(kernel, out_shape=out_shape, in_specs=[pl.BlockSpec(memory...  6.42 us
    ppermute x9, waiting for transfers between devices, exchange_seq(): lax.ppermute(chunk, ('section', 'seq'), [(section * size + seq, section *...  3.42 us
    ppermute x3, starting transfers between devices, exchange_chan(): lax.ppermute(chunks[step], 'chan', [(i, i ^ step) for i in range(size)])  1.92 us
    ppermute x1, starting transfers between devices, body(): received = lax.ppermute(gradient, 'section', ring)  1.56 us
    ppermute x3, waiting for transfers between devices, exchange_chan(): lax.ppermute(chunks[step], 'chan', [(i, i ^ step) for i in range(size)])  1.23 us
    ppermute x1, waiting for transfers between devices, body(): received = lax.ppermute(gradient, 'section', ring)  0.95 us
  transfers between devices with their start and end apart: 13, of which 7 were waited for; matrix products, arithmetic and copies ran while one was open for 0% of the time, Pallas kernels for 11%

profile of v10, /device:TPU:0, one launch (start us, length us, event | category | flops | bytes accessed | tf_op | source)
XLA Modules:
  0.0 32.2 jit_solution(1432777033157564255)
XLA Ops:
  0.6 1.2 %shard_map.104 = (bf16[128,256]{1,0:T(8,128)(2,1)S(1)}, bf16[128,256]{1,0:T(8,128)(2,1)S(1)}, bf16[128,256]{1,0:T(8,128)(2,1)S(1)}, bf16[128,256]{1,0:T(8,128)(2,1)S(1)}) custom-call(bf16[1,2,128,256]{3,2,1,0:T(8,128)(2,1)} %post.3, bf16[1,128,256]{2,1,0:T(8,128)(2,1)} %held.1, bf16[128,256]{1,0:T(8,128)(2,1)} %loss.1, bf16[1,2,128,256]{3,2,1,0:T(8,128)(2,1)} %pre.3, ...), custom_call_target="tpu_custom_call" | custom-call | tf_op jit(solution)/shard_map/pallas_call | solution.py:63
  1.9 4.1 %collective-permute-start = (bf16[128,256]{1,0:T(8,128)(2,1)S(1)}, bf16[128,256]{1,0:T(8,128)(2,1)S(1)}, u32[]{:S(2)}, u32[]{:S(2)}) collective-permute-start(bf16[128,256]{1,0:T(8,128)(2,1)S(1)} %get-tuple-element.31), channel_id=1, source_target_pairs={{0,8},{4,12},{8,0},{12,4},{16,24},{20,28},{24,16},{28,20},{1,9},{5... | collective-permute-start | bytes 196616 | tf_op jit(solution)/shard_map/ppermute | solution.py:293
  6.0 1.3 %collective-permute-start.1 = (bf16[128,256]{1,0:T(8,128)(2,1)S(1)}, bf16[128,256]{1,0:T(8,128)(2,1)S(1)}, u32[]{:S(2)}, u32[]{:S(2)}) collective-permute-start(bf16[128,256]{1,0:T(8,128)(2,1)S(1)} %get-tuple-element.32), channel_id=1, source_target_pairs={{0,12},{4,8},{8,4},{12,0},{16,28},{20,24},{24,20},{28,16},{1,13},{... | collective-permute-start | bytes 196616 | tf_op jit(solution)/shard_map/ppermute | solution.py:293
  7.3 0.2 collective-permute-start.2
  7.6 1.5 %shard_map.105 = (bf16[128,256]{1,0:T(8,128)(2,1)S(1)}, bf16[128,256]{1,0:T(8,128)(2,1)S(1)}, bf16[128,256]{1,0:T(8,128)(2,1)S(1)}, bf16[128,256]{1,0:T(8,128)(2...) custom-call(bf16[128,256]{1,0:T(8,128)(2,1)S(1)} %get-tuple-element.27.after.rest_0_, ...), custom_call_target="tpu_custom_call" | custom-call | tf_op jit(solution)/shard_map/pallas_call | solution.py:63
  9.0 1.9 %collective-permute-start.4 = (bf16[128,256]{1,0:T(8,128)(2,1)S(1)}, bf16[128,256]{1,0:T(8,128)(2,1)S(1)}, u32[]{:S(2)}, u32[]{:S(2)}) collective-permute-start(bf16[128,256]{1,0:T(8,128)(2,1)S(1)} %get-tuple-element.37), channel_id=1, source_target_pairs={{0,4},{4,0},{8,12},{12,8},{16,24},{20,28},{24,16},{28,20},{1,5},{5... | collective-permute-start | bytes 196616 | tf_op jit(solution)/shard_map/ppermute | solution.py:293
  10.9 1.7 %collective-permute-start.5 = (bf16[128,256]{1,0:T(8,128)(2,1)S(1)}, bf16[128,256]{1,0:T(8,128)(2,1)S(1)}, u32[]{:S(2)}, u32[]{:S(2)}) collective-permute-start(bf16[128,256]{1,0:T(8,128)(2,1)S(1)} %get-tuple-element.38), channel_id=1, source_target_pairs={{0,8},{4,12},{8,0},{12,4},{16,20},{20,16},{24,28},{28,24},{1,9},{5... | collective-permute-start | bytes 196616 | tf_op jit(solution)/shard_map/ppermute | solution.py:293
  12.6 2.3 %collective-permute-start.6 = (bf16[128,256]{1,0:T(8,128)(2,1)S(1)}, bf16[128,256]{1,0:T(8,128)(2,1)S(1)}, u32[]{:S(2)}, u32[]{:S(2)}) collective-permute-start(bf16[128,256]{1,0:T(8,128)(2,1)S(1)} %get-tuple-element.39), channel_id=1, source_target_pairs={{0,12},{4,8},{8,4},{12,0},{16,28},{20,24},{24,20},{28,16},{1,13},{... | collective-permute-start | bytes 196616 | tf_op jit(solution)/shard_map/ppermute | solution.py:293
  14.9 0.9 %shard_map.106 = (bf16[256,128]{1,0:T(8,128)(2,1)S(1)}, f32[2,512,128]{2,1,0:T(8,128)S(1)}) custom-call(f32[1,128]{1,0:T(1,128)S(1)} %get-tuple-element.28.gain, bf16[1024,256]{1,0:T(8,128)(2,1)S(1)} %get-tuple-element.29.forward, bf16[256,1024]{1,0:T(8,128)(2,1)S(1)} %get-tuple-element.30.backward, bf16[128,256]{1,0:T(8,128)(2,1)S(1)} %get-tuple-element.27.after.rest_0_, ...), custom_call_target="tpu_custom_call" | custom-call | tf_op jit(solution)/shard_map/pallas_call | solution.py:63
  15.8 1.6 %collective-permute-start.3 = (bf16[256,128]{1,0:T(8,128)(2,1)S(1)}, bf16[256,128]{1,0:T(8,128)(2,1)S(1)}, u32[]{:S(2)}, u32[]{:S(2)}) collective-permute-start(bf16[256,128]{1,0:T(8,128)(2,1)S(1)} %get-tuple-element.34), channel_id=1, source_target_pairs={{0,16},{16,0},{1,17},{17,1},{2,18},{18,2},{3,19},{19,3},{4,20},{20... | collective-permute-start | bytes 196616 | tf_op jit(solution)/shard_map/ppermute | solution.py:350
  17.5 1.3 %collective-permute-done.6.rest_3_ = bf16[128,256]{1,0:T(8,128)(2,1)S(1)} collective-permute-done((bf16[128,256]{1,0:T(8,128)(2,1)S(1)}, bf16[128,256]{1,0:T(8,128)(2,1)S(1)}, u32[]{:S(2)}, u32[]{:S(2)}) %collective-permute-start.6) | collective-permute-done | bytes 65568 | tf_op jit(solution)/shard_map/ppermute | solution.py:293
  18.8 0.4 %shard_map.107 = (f32[2,256,128]{2,1,0:T(8,128)S(1)}, f32[2,256,128]{2,1,0:T(8,128)S(1)}, f32[2,512,128]{2,1,0:T(8,128)S(1)}, f32[2,512,128]{2,1,0:T(8,128)S(1)}) custom-call(bf16[1024,256]{1,0:T(8,128)(2,1)S(1)} %get-tuple-element.29.forward, f32[2,512,128]{2,1,0:T(8,128)S(1)} %get-tuple-element.35.spectra, bf16[128,256]{1,0:T(8,128)(2,1)S(1)} %get-tuple-element.36.rest_0_, ...), custom_call_target="tpu_custom_call" | custom-call | tf_op jit(solution)/shard_map/pallas_call | solution.py:63
  19.2 1.0 %collective-permute-done.3.received = bf16[256,128]{1,0:T(8,128)(2,1)S(1)} collective-permute-done((bf16[256,128]{1,0:T(8,128)(2,1)S(1)}, bf16[256,128]{1,0:T(8,128)(2,1)S(1)}, u32[]{:S(2)}, u32[]{:S(2)}) %collective-permute-start.3) | collective-permute-done | bytes 65568 | tf_op jit(solution)/shard_map/ppermute | solution.py:350
  20.1 0.9 %shard_map.108 = (bf16[128,128]{1,0:T(8,128)(2,1)S(1)}, bf16[128,128]{1,0:T(8,128)(2,1)S(1)}, bf16[128,128]{1,0:T(8,128)(2,1)S(1)}, bf16[128,128]{1,0:T(8,128)(2,1)S(1)}) custom-call(f32[1,128]{1,0:T(1,128)S(1)} %get-tuple-element.28.gain, bf16[1024,256]{1,0:T(8,128)(2,1)S(1)} %get-tuple-element.29.forward, ...), custom_call_target="tpu_custom_call" | custom-call | tf_op jit(solution)/shard_map/pallas_call | solution.py:63
  21.0 1.6 %collective-permute-start.7 = (bf16[128,128]{1,0:T(8,128)(2,1)S(1)}, bf16[128,128]{1,0:T(8,128)(2,1)S(1)}, u32[]{:S(2)}, u32[]{:S(2)}) collective-permute-start(bf16[128,128]{1,0:T(8,128)(2,1)S(1)} %get-tuple-element.45), channel_id=1, source_target_pairs={{0,12},{4,8},{8,4},{12,0},{16,28},{20,24},{24,20},{28,16},{1,13},{... | collective-permute-start | bytes 98312 | tf_op jit(solution)/shard_map/ppermute | solution.py:293
  22.7 2.8 %collective-permute-start.9 = (bf16[128,128]{1,0:T(8,128)(2,1)S(1)}, bf16[128,128]{1,0:T(8,128)(2,1)S(1)}, u32[]{:S(2)}, u32[]{:S(2)}) collective-permute-start(bf16[128,128]{1,0:T(8,128)(2,1)S(1)} %get-tuple-element.47), channel_id=1, source_target_pairs={{0,8},{4,12},{8,0},{12,4},{16,24},{20,28},{24,16},{28,20},{1,9},{5... | collective-permute-start | bytes 98312 | tf_op jit(solution)/shard_map/ppermute | solution.py:293
  25.5 1.4 %collective-permute-done.7.rest_1_ = bf16[128,128]{1,0:T(8,128)(2,1)S(1)} collective-permute-done((bf16[128,128]{1,0:T(8,128)(2,1)S(1)}, bf16[128,128]{1,0:T(8,128)(2,1)S(1)}, u32[]{:S(2)}, u32[]{:S(2)}) %collective-permute-start.7) | collective-permute-done | bytes 32800 | tf_op jit(solution)/shard_map/ppermute | solution.py:293
  26.9 0.6 %collective-permute-done.9.rest_3_ = bf16[128,128]{1,0:T(8,128)(2,1)S(1)} collective-permute-done((bf16[128,128]{1,0:T(8,128)(2,1)S(1)}, bf16[128,128]{1,0:T(8,128)(2,1)S(1)}, u32[]{:S(2)}, u32[]{:S(2)}) %collective-permute-start.9) | collective-permute-done | bytes 32800 | tf_op jit(solution)/shard_map/ppermute | solution.py:293
  27.7 1.6 %collective-permute-start.11 = (bf16[64,128]{1,0:T(8,128)(2,1)S(1)}, bf16[64,128]{1,0:T(8,128)(2,1)S(1)}, u32[]{:S(2)}, u32[]{:S(2)}) collective-permute-start(bf16[64,128]{1,0:T(8,128)(2,1)S(1)} %get-tuple-element.50), channel_id=1, source_target_pairs={{0,2},{1,3},{2,0},{3,1},{4,6},{5,7},{6,4},{7,5},{8,10},{9,11},{10,... | collective-permute-start | bytes 49160 | tf_op jit(solution)/shard_map/ppermute | solution.py:284
  29.3 0.3 collective-permute-start.12
  29.6 0.7 %shard_map.109 = bf16[1,128,256]{2,1,0:T(8,128)(2,1)} custom-call(bf16[128,128]{1,0:T(8,128)(2,1)S(1)} %get-tuple-element.44.rest_0_, bf16[128,128]{1,0:T(8,128)(2,1)S(1)} %collective-permute-done.7.rest_1_, bf16[128,128]{1,0:T(8,128)(2,1)S(1)} %collective-permute-done.8.rest_2_, bf16[128,128]{1,0:T(8,128)(2,1)S(1)} %collective-permute-done.9.rest_3_), custom_call_target="tpu_custom_call" | custom-call | tf_op jit(solution)/shard_map/pallas_call | solution.py:63
  30.3 0.7 %collective-permute-done.10.refs_1_ = bf16[64,128]{1,0:T(8,128)(2,1)S(1)} collective-permute-done((bf16[64,128]{1,0:T(8,128)(2,1)S(1)}, bf16[64,128]{1,0:T(8,128)(2,1)S(1)}, u32[]{:S(2)}, u32[]{:S(2)}) %collective-permute-start.10) | collective-permute-done | bytes 16416 | tf_op jit(solution)/shard_map/ppermute | solution.py:284
  31.0 0.6 %collective-permute-done.11.refs_2_ = bf16[64,128]{1,0:T(8,128)(2,1)S(1)} collective-permute-done((bf16[64,128]{1,0:T(8,128)(2,1)S(1)}, bf16[64,128]{1,0:T(8,128)(2,1)S(1)}, u32[]{:S(2)}, u32[]{:S(2)}) %collective-permute-start.11) | collective-permute-done | bytes 16416 | tf_op jit(solution)/shard_map/ppermute | solution.py:284
  31.5 0.6 %shard_map.111 = f32[64,128]{1,0:T(8,128)} custom-call(bf16[64,128]{1,0:T(8,128)(2,1)S(1)} %get-tuple-element.48.refs_0_, bf16[64,128]{1,0:T(8,128)(2,1)S(1)} %collective-permute-done.10.refs_1_, bf16[64,128]{1,0:T(8,128)(2,1)S(1)} %collective-permute-done.11.refs_2_, bf16[64,128]{1,0:T(8,128)(2,1)S(1)} %collective-permute-done.12.refs_3_), custom_call_target="tpu_custom_call" | custom-call | tf_op jit(solution)/shard_map/pallas_call | solution.py:63
  (10 shorter events, 0.4 us)
Async XLA Ops:
  1.9 10.7 %collective-permute-start = (bf16[128,256]{1,0:T(8,128)(2,1)S(1)}, bf16[128,256]{1,0:T(8,128)(2,1)S(1)}, u32[]{:S(2)}, u32[]{:S(2)}) collective-permute-start(bf16[128,256]{1,0:T(8,128)(2,1)S(1)} %get-tuple-element.31), channel_id=1, source_target_pairs={{0,8},{4,12},{8,0},{12,4},{16,24},{20,28},{24,16},{28,20},{1,9},{5... | collective-permute-start | bytes 196616 | tf_op jit(solution)/shard_map/ppermute | solution.py:293
  6.0 8.9 %collective-permute-start.1 = (bf16[128,256]{1,0:T(8,128)(2,1)S(1)}, bf16[128,256]{1,0:T(8,128)(2,1)S(1)}, u32[]{:S(2)}, u32[]{:S(2)}) collective-permute-start(bf16[128,256]{1,0:T(8,128)(2,1)S(1)} %get-tuple-element.32), channel_id=1, source_target_pairs={{0,12},{4,8},{8,4},{12,0},{16,28},{20,24},{24,20},{28,16},{1,13},{... | collective-permute-start | bytes 196616 | tf_op jit(solution)/shard_map/ppermute | solution.py:293
  7.3 7.5 %collective-permute-start.2 = (bf16[128,256]{1,0:T(8,128)(2,1)S(1)}, bf16[128,256]{1,0:T(8,128)(2,1)S(1)}, u32[]{:S(2)}, u32[]{:S(2)}) collective-permute-start(bf16[128,256]{1,0:T(8,128)(2,1)S(1)} %get-tuple-element.33), channel_id=1, source_target_pairs={{0,4},{4,0},{8,12},{12,8},{16,20},{20,16},{24,28},{28,24},{1,5},{5... | collective-permute-start | bytes 196616 | tf_op jit(solution)/shard_map/ppermute | solution.py:293
  9.0 8.3 %collective-permute-start.4 = (bf16[128,256]{1,0:T(8,128)(2,1)S(1)}, bf16[128,256]{1,0:T(8,128)(2,1)S(1)}, u32[]{:S(2)}, u32[]{:S(2)}) collective-permute-start(bf16[128,256]{1,0:T(8,128)(2,1)S(1)} %get-tuple-element.37), channel_id=1, source_target_pairs={{0,4},{4,0},{8,12},{12,8},{16,24},{20,28},{24,16},{28,20},{1,5},{5... | collective-permute-start | bytes 196616 | tf_op jit(solution)/shard_map/ppermute | solution.py:293
  10.9 6.6 %collective-permute-start.5 = (bf16[128,256]{1,0:T(8,128)(2,1)S(1)}, bf16[128,256]{1,0:T(8,128)(2,1)S(1)}, u32[]{:S(2)}, u32[]{:S(2)}) collective-permute-start(bf16[128,256]{1,0:T(8,128)(2,1)S(1)} %get-tuple-element.38), channel_id=1, source_target_pairs={{0,8},{4,12},{8,0},{12,4},{16,20},{20,16},{24,28},{28,24},{1,9},{5... | collective-permute-start | bytes 196616 | tf_op jit(solution)/shard_map/ppermute | solution.py:293
  12.6 6.2 %collective-permute-start.6 = (bf16[128,256]{1,0:T(8,128)(2,1)S(1)}, bf16[128,256]{1,0:T(8,128)(2,1)S(1)}, u32[]{:S(2)}, u32[]{:S(2)}) collective-permute-start(bf16[128,256]{1,0:T(8,128)(2,1)S(1)} %get-tuple-element.39), channel_id=1, source_target_pairs={{0,12},{4,8},{8,4},{12,0},{16,28},{20,24},{24,20},{28,16},{1,13},{... | collective-permute-start | bytes 196616 | tf_op jit(solution)/shard_map/ppermute | solution.py:293
  15.8 4.3 %collective-permute-start.3 = (bf16[256,128]{1,0:T(8,128)(2,1)S(1)}, bf16[256,128]{1,0:T(8,128)(2,1)S(1)}, u32[]{:S(2)}, u32[]{:S(2)}) collective-permute-start(bf16[256,128]{1,0:T(8,128)(2,1)S(1)} %get-tuple-element.34), channel_id=1, source_target_pairs={{0,16},{16,0},{1,17},{17,1},{2,18},{18,2},{3,19},{19,3},{4,20},{20... | collective-permute-start | bytes 196616 | tf_op jit(solution)/shard_map/ppermute | solution.py:350
  21.0 5.9 %collective-permute-start.7 = (bf16[128,128]{1,0:T(8,128)(2,1)S(1)}, bf16[128,128]{1,0:T(8,128)(2,1)S(1)}, u32[]{:S(2)}, u32[]{:S(2)}) collective-permute-start(bf16[128,128]{1,0:T(8,128)(2,1)S(1)} %get-tuple-element.45), channel_id=1, source_target_pairs={{0,12},{4,8},{8,4},{12,0},{16,28},{20,24},{24,20},{28,16},{1,13},{... | collective-permute-start | bytes 98312 | tf_op jit(solution)/shard_map/ppermute | solution.py:293
  22.6 4.3 %collective-permute-start.8 = (bf16[128,128]{1,0:T(8,128)(2,1)S(1)}, bf16[128,128]{1,0:T(8,128)(2,1)S(1)}, u32[]{:S(2)}, u32[]{:S(2)}) collective-permute-start(bf16[128,128]{1,0:T(8,128)(2,1)S(1)} %get-tuple-element.46), channel_id=1, source_target_pairs={{0,4},{4,0},{8,12},{12,8},{16,20},{20,16},{24,28},{28,24},{1,5},{5... | collective-permute-start | bytes 98312 | tf_op jit(solution)/shard_map/ppermute | solution.py:293
  22.7 4.8 %collective-permute-start.9 = (bf16[128,128]{1,0:T(8,128)(2,1)S(1)}, bf16[128,128]{1,0:T(8,128)(2,1)S(1)}, u32[]{:S(2)}, u32[]{:S(2)}) collective-permute-start(bf16[128,128]{1,0:T(8,128)(2,1)S(1)} %get-tuple-element.47), channel_id=1, source_target_pairs={{0,8},{4,12},{8,0},{12,4},{16,24},{20,28},{24,16},{28,20},{1,9},{5... | collective-permute-start | bytes 98312 | tf_op jit(solution)/shard_map/ppermute | solution.py:293
  27.6 3.3 %collective-permute-start.10 = (bf16[64,128]{1,0:T(8,128)(2,1)S(1)}, bf16[64,128]{1,0:T(8,128)(2,1)S(1)}, u32[]{:S(2)}, u32[]{:S(2)}) collective-permute-start(bf16[64,128]{1,0:T(8,128)(2,1)S(1)} %get-tuple-element.49), channel_id=1, source_target_pairs={{0,3},{1,2},{2,1},{3,0},{4,7},{5,6},{6,5},{7,4},{8,11},{9,10},{10,... | collective-permute-start | bytes 49160 | tf_op jit(solution)/shard_map/ppermute | solution.py:284
  27.7 3.8 %collective-permute-start.11 = (bf16[64,128]{1,0:T(8,128)(2,1)S(1)}, bf16[64,128]{1,0:T(8,128)(2,1)S(1)}, u32[]{:S(2)}, u32[]{:S(2)}) collective-permute-start(bf16[64,128]{1,0:T(8,128)(2,1)S(1)} %get-tuple-element.50), channel_id=1, source_target_pairs={{0,2},{1,3},{2,0},{3,1},{4,6},{5,7},{6,4},{7,5},{8,10},{9,11},{10,... | collective-permute-start | bytes 49160 | tf_op jit(solution)/shard_map/ppermute | solution.py:284
  29.3 2.2 %collective-permute-start.12 = (bf16[64,128]{1,0:T(8,128)(2,1)S(1)}, bf16[64,128]{1,0:T(8,128)(2,1)S(1)}, u32[]{:S(2)}, u32[]{:S(2)}) collective-permute-start(bf16[64,128]{1,0:T(8,128)(2,1)S(1)} %get-tuple-element.51), channel_id=1, source_target_pairs={{0,1},{1,0},{2,3},{3,2},{4,5},{5,4},{6,7},{7,6},{8,9},{9,8},{10,11... | collective-permute-start | bytes 49160 | tf_op jit(solution)/shard_map/ppermute | solution.py:284

commit v11 on v10

--- a/solution.py
+++ b/solution.py
@@ -112,7 +112,7 @@
     *outs, stage, gates, lags, semaphores = rest
     sources = [post.at[0, 0], held.at[0], loss, pre.at[0, 0], filters.at[0]]
     wait(fetch(sources, [gates.at[at] for at in range(4)] + [lags], semaphores))
-    gated = (gates[0].astype(F32) * gates[1].astype(F32)).astype(BF16)
+    gated = gates[0] * gates[1]
     kept = jnp.where(lax.axis_index("section") == 0, gates[2], gates[1])
     pack([lags[...].astype(BF16), gated, gates[3], kept], stage, outs, first_steps(len(outs)))
 
@@ -128,7 +128,7 @@
         semaphores,
     )
     wait(copies[:6])
-    mixed = (gates[0:2].astype(F32) * gates[2:4].astype(F32)).astype(BF16)
+    mixed = gates[0:2] * gates[2:4]
     pack([mixed[0], mixed[1], gates[4], gates[3]], stage, outs, second_steps(len(outs)))
     unit = gain.shape[1] // 2
     for block in range(len(outs)):

time: 32.3 us -> 32.3 us (level)
  no operation moved by 1% of the time
where the time goes in v11:
time: 32.3 us; the launch traced here: 32.2 us
  starting transfers between devices  19.4 us (60%)
  Pallas kernels  6.42 us (20%)
  waiting for transfers between devices  5.6 us (17%)
  between operations  0.69 us (2%)
    ppermute x9, starting transfers between devices, exchange_seq(): lax.ppermute(chunk, ('section', 'seq'), [(section * size + seq, section *...  16 us
    pallas_call x8, Pallas kernels, run(): pl.pallas_call(kernel, out_shape=out_shape, in_specs=[pl.BlockSpec(memory...  6.42 us
    ppermute x9, waiting for transfers between devices, exchange_seq(): lax.ppermute(chunk, ('section', 'seq'), [(section * size + seq, section *...  3.42 us
    ppermute x3, starting transfers between devices, exchange_chan(): lax.ppermute(chunks[step], 'chan', [(i, i ^ step) for i in range(size)])  1.92 us
    ppermute x1, starting transfers between devices, body(): received = lax.ppermute(gradient, 'section', ring)  1.56 us
    ppermute x3, waiting for transfers between devices, exchange_chan(): lax.ppermute(chunks[step], 'chan', [(i, i ^ step) for i in range(size)])  1.23 us
    ppermute x1, waiting for transfers between devices, body(): received = lax.ppermute(gradient, 'section', ring)  0.95 us
  transfers between devices with their start and end apart: 13, of which 7 were waited for; matrix products, arithmetic and copies ran while one was open for 0% of the time, Pallas kernels for 11%

profile of v11, /device:TPU:0, one launch (start us, length us, event | category | flops | bytes accessed | tf_op | source)
XLA Modules:
  0.0 32.2 jit_solution(4212470367969498921)
XLA Ops:
  0.6 1.2 %shard_map.104 = (bf16[128,256]{1,0:T(8,128)(2,1)S(1)}, bf16[128,256]{1,0:T(8,128)(2,1)S(1)}, bf16[128,256]{1,0:T(8,128)(2,1)S(1)}, bf16[128,256]{1,0:T(8,128)(2,1)S(1)}) custom-call(bf16[1,2,128,256]{3,2,1,0:T(8,128)(2,1)} %post.3, bf16[1,128,256]{2,1,0:T(8,128)(2,1)} %held.1, bf16[128,256]{1,0:T(8,128)(2,1)} %loss.1, bf16[1,2,128,256]{3,2,1,0:T(8,128)(2,1)} %pre.3, ...), custom_call_target="tpu_custom_call" | custom-call | tf_op jit(solution)/shard_map/pallas_call | solution.py:63
  1.9 4.1 %collective-permute-start = (bf16[128,256]{1,0:T(8,128)(2,1)S(1)}, bf16[128,256]{1,0:T(8,128)(2,1)S(1)}, u32[]{:S(2)}, u32[]{:S(2)}) collective-permute-start(bf16[128,256]{1,0:T(8,128)(2,1)S(1)} %get-tuple-element.31), channel_id=1, source_target_pairs={{0,8},{4,12},{8,0},{12,4},{16,24},{20,28},{24,16},{28,20},{1,9},{5... | collective-permute-start | bytes 196616 | tf_op jit(solution)/shard_map/ppermute | solution.py:293
  6.0 1.3 %collective-permute-start.1 = (bf16[128,256]{1,0:T(8,128)(2,1)S(1)}, bf16[128,256]{1,0:T(8,128)(2,1)S(1)}, u32[]{:S(2)}, u32[]{:S(2)}) collective-permute-start(bf16[128,256]{1,0:T(8,128)(2,1)S(1)} %get-tuple-element.32), channel_id=1, source_target_pairs={{0,12},{4,8},{8,4},{12,0},{16,28},{20,24},{24,20},{28,16},{1,13},{... | collective-permute-start | bytes 196616 | tf_op jit(solution)/shard_map/ppermute | solution.py:293
  7.3 0.2 collective-permute-start.2
  7.6 1.5 %shard_map.105 = (bf16[128,256]{1,0:T(8,128)(2,1)S(1)}, bf16[128,256]{1,0:T(8,128)(2,1)S(1)}, bf16[128,256]{1,0:T(8,128)(2,1)S(1)}, bf16[128,256]{1,0:T(8,128)(2...) custom-call(bf16[128,256]{1,0:T(8,128)(2,1)S(1)} %get-tuple-element.27.after.rest_0_, ...), custom_call_target="tpu_custom_call" | custom-call | tf_op jit(solution)/shard_map/pallas_call | solution.py:63
  9.0 1.9 %collective-permute-start.4 = (bf16[128,256]{1,0:T(8,128)(2,1)S(1)}, bf16[128,256]{1,0:T(8,128)(2,1)S(1)}, u32[]{:S(2)}, u32[]{:S(2)}) collective-permute-start(bf16[128,256]{1,0:T(8,128)(2,1)S(1)} %get-tuple-element.37), channel_id=1, source_target_pairs={{0,4},{4,0},{8,12},{12,8},{16,24},{20,28},{24,16},{28,20},{1,5},{5... | collective-permute-start | bytes 196616 | tf_op jit(solution)/shard_map/ppermute | solution.py:293
  10.9 1.7 %collective-permute-start.5 = (bf16[128,256]{1,0:T(8,128)(2,1)S(1)}, bf16[128,256]{1,0:T(8,128)(2,1)S(1)}, u32[]{:S(2)}, u32[]{:S(2)}) collective-permute-start(bf16[128,256]{1,0:T(8,128)(2,1)S(1)} %get-tuple-element.38), channel_id=1, source_target_pairs={{0,8},{4,12},{8,0},{12,4},{16,20},{20,16},{24,28},{28,24},{1,9},{5... | collective-permute-start | bytes 196616 | tf_op jit(solution)/shard_map/ppermute | solution.py:293
  12.6 2.3 %collective-permute-start.6 = (bf16[128,256]{1,0:T(8,128)(2,1)S(1)}, bf16[128,256]{1,0:T(8,128)(2,1)S(1)}, u32[]{:S(2)}, u32[]{:S(2)}) collective-permute-start(bf16[128,256]{1,0:T(8,128)(2,1)S(1)} %get-tuple-element.39), channel_id=1, source_target_pairs={{0,12},{4,8},{8,4},{12,0},{16,28},{20,24},{24,20},{28,16},{1,13},{... | collective-permute-start | bytes 196616 | tf_op jit(solution)/shard_map/ppermute | solution.py:293
  14.9 0.9 %shard_map.106 = (bf16[256,128]{1,0:T(8,128)(2,1)S(1)}, f32[2,512,128]{2,1,0:T(8,128)S(1)}) custom-call(f32[1,128]{1,0:T(1,128)S(1)} %get-tuple-element.28.gain, bf16[1024,256]{1,0:T(8,128)(2,1)S(1)} %get-tuple-element.29.forward, bf16[256,1024]{1,0:T(8,128)(2,1)S(1)} %get-tuple-element.30.backward, bf16[128,256]{1,0:T(8,128)(2,1)S(1)} %get-tuple-element.27.after.rest_0_, ...), custom_call_target="tpu_custom_call" | custom-call | tf_op jit(solution)/shard_map/pallas_call | solution.py:63
  15.8 1.6 %collective-permute-start.3 = (bf16[256,128]{1,0:T(8,128)(2,1)S(1)}, bf16[256,128]{1,0:T(8,128)(2,1)S(1)}, u32[]{:S(2)}, u32[]{:S(2)}) collective-permute-start(bf16[256,128]{1,0:T(8,128)(2,1)S(1)} %get-tuple-element.34), channel_id=1, source_target_pairs={{0,16},{16,0},{1,17},{17,1},{2,18},{18,2},{3,19},{19,3},{4,20},{20... | collective-permute-start | bytes 196616 | tf_op jit(solution)/shard_map/ppermute | solution.py:350
  17.5 1.3 %collective-permute-done.6.rest_3_ = bf16[128,256]{1,0:T(8,128)(2,1)S(1)} collective-permute-done((bf16[128,256]{1,0:T(8,128)(2,1)S(1)}, bf16[128,256]{1,0:T(8,128)(2,1)S(1)}, u32[]{:S(2)}, u32[]{:S(2)}) %collective-permute-start.6) | collective-permute-done | bytes 65568 | tf_op jit(solution)/shard_map/ppermute | solution.py:293
  18.8 0.4 %shard_map.107 = (f32[2,256,128]{2,1,0:T(8,128)S(1)}, f32[2,256,128]{2,1,0:T(8,128)S(1)}, f32[2,512,128]{2,1,0:T(8,128)S(1)}, f32[2,512,128]{2,1,0:T(8,128)S(1)}) custom-call(bf16[1024,256]{1,0:T(8,128)(2,1)S(1)} %get-tuple-element.29.forward, f32[2,512,128]{2,1,0:T(8,128)S(1)} %get-tuple-element.35.spectra, bf16[128,256]{1,0:T(8,128)(2,1)S(1)} %get-tuple-element.36.rest_0_, ...), custom_call_target="tpu_custom_call" | custom-call | tf_op jit(solution)/shard_map/pallas_call | solution.py:63
  19.2 1.0 %collective-permute-done.3.received = bf16[256,128]{1,0:T(8,128)(2,1)S(1)} collective-permute-done((bf16[256,128]{1,0:T(8,128)(2,1)S(1)}, bf16[256,128]{1,0:T(8,128)(2,1)S(1)}, u32[]{:S(2)}, u32[]{:S(2)}) %collective-permute-start.3) | collective-permute-done | bytes 65568 | tf_op jit(solution)/shard_map/ppermute | solution.py:350
  20.1 0.9 %shard_map.108 = (bf16[128,128]{1,0:T(8,128)(2,1)S(1)}, bf16[128,128]{1,0:T(8,128)(2,1)S(1)}, bf16[128,128]{1,0:T(8,128)(2,1)S(1)}, bf16[128,128]{1,0:T(8,128)(2,1)S(1)}) custom-call(f32[1,128]{1,0:T(1,128)S(1)} %get-tuple-element.28.gain, bf16[1024,256]{1,0:T(8,128)(2,1)S(1)} %get-tuple-element.29.forward, ...), custom_call_target="tpu_custom_call" | custom-call | tf_op jit(solution)/shard_map/pallas_call | solution.py:63
  21.0 1.6 %collective-permute-start.7 = (bf16[128,128]{1,0:T(8,128)(2,1)S(1)}, bf16[128,128]{1,0:T(8,128)(2,1)S(1)}, u32[]{:S(2)}, u32[]{:S(2)}) collective-permute-start(bf16[128,128]{1,0:T(8,128)(2,1)S(1)} %get-tuple-element.45), channel_id=1, source_target_pairs={{0,12},{4,8},{8,4},{12,0},{16,28},{20,24},{24,20},{28,16},{1,13},{... | collective-permute-start | bytes 98312 | tf_op jit(solution)/shard_map/ppermute | solution.py:293
  22.7 2.8 %collective-permute-start.9 = (bf16[128,128]{1,0:T(8,128)(2,1)S(1)}, bf16[128,128]{1,0:T(8,128)(2,1)S(1)}, u32[]{:S(2)}, u32[]{:S(2)}) collective-permute-start(bf16[128,128]{1,0:T(8,128)(2,1)S(1)} %get-tuple-element.47), channel_id=1, source_target_pairs={{0,8},{4,12},{8,0},{12,4},{16,24},{20,28},{24,16},{28,20},{1,9},{5... | collective-permute-start | bytes 98312 | tf_op jit(solution)/shard_map/ppermute | solution.py:293
  25.5 1.4 %collective-permute-done.7.rest_1_ = bf16[128,128]{1,0:T(8,128)(2,1)S(1)} collective-permute-done((bf16[128,128]{1,0:T(8,128)(2,1)S(1)}, bf16[128,128]{1,0:T(8,128)(2,1)S(1)}, u32[]{:S(2)}, u32[]{:S(2)}) %collective-permute-start.7) | collective-permute-done | bytes 32800 | tf_op jit(solution)/shard_map/ppermute | solution.py:293
  26.9 0.6 %collective-permute-done.9.rest_3_ = bf16[128,128]{1,0:T(8,128)(2,1)S(1)} collective-permute-done((bf16[128,128]{1,0:T(8,128)(2,1)S(1)}, bf16[128,128]{1,0:T(8,128)(2,1)S(1)}, u32[]{:S(2)}, u32[]{:S(2)}) %collective-permute-start.9) | collective-permute-done | bytes 32800 | tf_op jit(solution)/shard_map/ppermute | solution.py:293
  27.7 1.6 %collective-permute-start.11 = (bf16[64,128]{1,0:T(8,128)(2,1)S(1)}, bf16[64,128]{1,0:T(8,128)(2,1)S(1)}, u32[]{:S(2)}, u32[]{:S(2)}) collective-permute-start(bf16[64,128]{1,0:T(8,128)(2,1)S(1)} %get-tuple-element.50), channel_id=1, source_target_pairs={{0,2},{1,3},{2,0},{3,1},{4,6},{5,7},{6,4},{7,5},{8,10},{9,11},{10,... | collective-permute-start | bytes 49160 | tf_op jit(solution)/shard_map/ppermute | solution.py:284
  29.3 0.3 collective-permute-start.12
  29.6 0.7 %shard_map.109 = bf16[1,128,256]{2,1,0:T(8,128)(2,1)} custom-call(bf16[128,128]{1,0:T(8,128)(2,1)S(1)} %get-tuple-element.44.rest_0_, bf16[128,128]{1,0:T(8,128)(2,1)S(1)} %collective-permute-done.7.rest_1_, bf16[128,128]{1,0:T(8,128)(2,1)S(1)} %collective-permute-done.8.rest_2_, bf16[128,128]{1,0:T(8,128)(2,1)S(1)} %collective-permute-done.9.rest_3_), custom_call_target="tpu_custom_call" | custom-call | tf_op jit(solution)/shard_map/pallas_call | solution.py:63
  30.3 0.7 %collective-permute-done.10.refs_1_ = bf16[64,128]{1,0:T(8,128)(2,1)S(1)} collective-permute-done((bf16[64,128]{1,0:T(8,128)(2,1)S(1)}, bf16[64,128]{1,0:T(8,128)(2,1)S(1)}, u32[]{:S(2)}, u32[]{:S(2)}) %collective-permute-start.10) | collective-permute-done | bytes 16416 | tf_op jit(solution)/shard_map/ppermute | solution.py:284
  31.0 0.6 %collective-permute-done.11.refs_2_ = bf16[64,128]{1,0:T(8,128)(2,1)S(1)} collective-permute-done((bf16[64,128]{1,0:T(8,128)(2,1)S(1)}, bf16[64,128]{1,0:T(8,128)(2,1)S(1)}, u32[]{:S(2)}, u32[]{:S(2)}) %collective-permute-start.11) | collective-permute-done | bytes 16416 | tf_op jit(solution)/shard_map/ppermute | solution.py:284
  31.5 0.6 %shard_map.111 = f32[64,128]{1,0:T(8,128)} custom-call(bf16[64,128]{1,0:T(8,128)(2,1)S(1)} %get-tuple-element.48.refs_0_, bf16[64,128]{1,0:T(8,128)(2,1)S(1)} %collective-permute-done.10.refs_1_, bf16[64,128]{1,0:T(8,128)(2,1)S(1)} %collective-permute-done.11.refs_2_, bf16[64,128]{1,0:T(8,128)(2,1)S(1)} %collective-permute-done.12.refs_3_), custom_call_target="tpu_custom_call" | custom-call | tf_op jit(solution)/shard_map/pallas_call | solution.py:63
  (10 shorter events, 0.4 us)
Async XLA Ops:
  1.9 10.7 %collective-permute-start = (bf16[128,256]{1,0:T(8,128)(2,1)S(1)}, bf16[128,256]{1,0:T(8,128)(2,1)S(1)}, u32[]{:S(2)}, u32[]{:S(2)}) collective-permute-start(bf16[128,256]{1,0:T(8,128)(2,1)S(1)} %get-tuple-element.31), channel_id=1, source_target_pairs={{0,8},{4,12},{8,0},{12,4},{16,24},{20,28},{24,16},{28,20},{1,9},{5... | collective-permute-start | bytes 196616 | tf_op jit(solution)/shard_map/ppermute | solution.py:293
  6.0 8.9 %collective-permute-start.1 = (bf16[128,256]{1,0:T(8,128)(2,1)S(1)}, bf16[128,256]{1,0:T(8,128)(2,1)S(1)}, u32[]{:S(2)}, u32[]{:S(2)}) collective-permute-start(bf16[128,256]{1,0:T(8,128)(2,1)S(1)} %get-tuple-element.32), channel_id=1, source_target_pairs={{0,12},{4,8},{8,4},{12,0},{16,28},{20,24},{24,20},{28,16},{1,13},{... | collective-permute-start | bytes 196616 | tf_op jit(solution)/shard_map/ppermute | solution.py:293
  7.3 7.5 %collective-permute-start.2 = (bf16[128,256]{1,0:T(8,128)(2,1)S(1)}, bf16[128,256]{1,0:T(8,128)(2,1)S(1)}, u32[]{:S(2)}, u32[]{:S(2)}) collective-permute-start(bf16[128,256]{1,0:T(8,128)(2,1)S(1)} %get-tuple-element.33), channel_id=1, source_target_pairs={{0,4},{4,0},{8,12},{12,8},{16,20},{20,16},{24,28},{28,24},{1,5},{5... | collective-permute-start | bytes 196616 | tf_op jit(solution)/shard_map/ppermute | solution.py:293
  9.0 8.3 %collective-permute-start.4 = (bf16[128,256]{1,0:T(8,128)(2,1)S(1)}, bf16[128,256]{1,0:T(8,128)(2,1)S(1)}, u32[]{:S(2)}, u32[]{:S(2)}) collective-permute-start(bf16[128,256]{1,0:T(8,128)(2,1)S(1)} %get-tuple-element.37), channel_id=1, source_target_pairs={{0,4},{4,0},{8,12},{12,8},{16,24},{20,28},{24,16},{28,20},{1,5},{5... | collective-permute-start | bytes 196616 | tf_op jit(solution)/shard_map/ppermute | solution.py:293
  10.9 6.6 %collective-permute-start.5 = (bf16[128,256]{1,0:T(8,128)(2,1)S(1)}, bf16[128,256]{1,0:T(8,128)(2,1)S(1)}, u32[]{:S(2)}, u32[]{:S(2)}) collective-permute-start(bf16[128,256]{1,0:T(8,128)(2,1)S(1)} %get-tuple-element.38), channel_id=1, source_target_pairs={{0,8},{4,12},{8,0},{12,4},{16,20},{20,16},{24,28},{28,24},{1,9},{5... | collective-permute-start | bytes 196616 | tf_op jit(solution)/shard_map/ppermute | solution.py:293
  12.6 6.2 %collective-permute-start.6 = (bf16[128,256]{1,0:T(8,128)(2,1)S(1)}, bf16[128,256]{1,0:T(8,128)(2,1)S(1)}, u32[]{:S(2)}, u32[]{:S(2)}) collective-permute-start(bf16[128,256]{1,0:T(8,128)(2,1)S(1)} %get-tuple-element.39), channel_id=1, source_target_pairs={{0,12},{4,8},{8,4},{12,0},{16,28},{20,24},{24,20},{28,16},{1,13},{... | collective-permute-start | bytes 196616 | tf_op jit(solution)/shard_map/ppermute | solution.py:293
  15.8 4.3 %collective-permute-start.3 = (bf16[256,128]{1,0:T(8,128)(2,1)S(1)}, bf16[256,128]{1,0:T(8,128)(2,1)S(1)}, u32[]{:S(2)}, u32[]{:S(2)}) collective-permute-start(bf16[256,128]{1,0:T(8,128)(2,1)S(1)} %get-tuple-element.34), channel_id=1, source_target_pairs={{0,16},{16,0},{1,17},{17,1},{2,18},{18,2},{3,19},{19,3},{4,20},{20... | collective-permute-start | bytes 196616 | tf_op jit(solution)/shard_map/ppermute | solution.py:350
  21.0 5.9 %collective-permute-start.7 = (bf16[128,128]{1,0:T(8,128)(2,1)S(1)}, bf16[128,128]{1,0:T(8,128)(2,1)S(1)}, u32[]{:S(2)}, u32[]{:S(2)}) collective-permute-start(bf16[128,128]{1,0:T(8,128)(2,1)S(1)} %get-tuple-element.45), channel_id=1, source_target_pairs={{0,12},{4,8},{8,4},{12,0},{16,28},{20,24},{24,20},{28,16},{1,13},{... | collective-permute-start | bytes 98312 | tf_op jit(solution)/shard_map/ppermute | solution.py:293
  22.6 4.3 %collective-permute-start.8 = (bf16[128,128]{1,0:T(8,128)(2,1)S(1)}, bf16[128,128]{1,0:T(8,128)(2,1)S(1)}, u32[]{:S(2)}, u32[]{:S(2)}) collective-permute-start(bf16[128,128]{1,0:T(8,128)(2,1)S(1)} %get-tuple-element.46), channel_id=1, source_target_pairs={{0,4},{4,0},{8,12},{12,8},{16,20},{20,16},{24,28},{28,24},{1,5},{5... | collective-permute-start | bytes 98312 | tf_op jit(solution)/shard_map/ppermute | solution.py:293
  22.7 4.8 %collective-permute-start.9 = (bf16[128,128]{1,0:T(8,128)(2,1)S(1)}, bf16[128,128]{1,0:T(8,128)(2,1)S(1)}, u32[]{:S(2)}, u32[]{:S(2)}) collective-permute-start(bf16[128,128]{1,0:T(8,128)(2,1)S(1)} %get-tuple-element.47), channel_id=1, source_target_pairs={{0,8},{4,12},{8,0},{12,4},{16,24},{20,28},{24,16},{28,20},{1,9},{5... | collective-permute-start | bytes 98312 | tf_op jit(solution)/shard_map/ppermute | solution.py:293
  27.6 3.3 %collective-permute-start.10 = (bf16[64,128]{1,0:T(8,128)(2,1)S(1)}, bf16[64,128]{1,0:T(8,128)(2,1)S(1)}, u32[]{:S(2)}, u32[]{:S(2)}) collective-permute-start(bf16[64,128]{1,0:T(8,128)(2,1)S(1)} %get-tuple-element.49), channel_id=1, source_target_pairs={{0,3},{1,2},{2,1},{3,0},{4,7},{5,6},{6,5},{7,4},{8,11},{9,10},{10,... | collective-permute-start | bytes 49160 | tf_op jit(solution)/shard_map/ppermute | solution.py:284
  27.7 3.8 %collective-permute-start.11 = (bf16[64,128]{1,0:T(8,128)(2,1)S(1)}, bf16[64,128]{1,0:T(8,128)(2,1)S(1)}, u32[]{:S(2)}, u32[]{:S(2)}) collective-permute-start(bf16[64,128]{1,0:T(8,128)(2,1)S(1)} %get-tuple-element.50), channel_id=1, source_target_pairs={{0,2},{1,3},{2,0},{3,1},{4,6},{5,7},{6,4},{7,5},{8,10},{9,11},{10,... | collective-permute-start | bytes 49160 | tf_op jit(solution)/shard_map/ppermute | solution.py:284
  29.3 2.2 %collective-permute-start.12 = (bf16[64,128]{1,0:T(8,128)(2,1)S(1)}, bf16[64,128]{1,0:T(8,128)(2,1)S(1)}, u32[]{:S(2)}, u32[]{:S(2)}) collective-permute-start(bf16[64,128]{1,0:T(8,128)(2,1)S(1)} %get-tuple-element.51), channel_id=1, source_target_pairs={{0,1},{1,0},{2,3},{3,2},{4,5},{5,4},{6,7},{7,6},{8,9},{9,8},{10,11... | collective-permute-start | bytes 49160 | tf_op jit(solution)/shard_map/ppermute | solution.py:284
